TPU v7x, 32 devices: a whole 2x2x4 slice. The times are simulated.
32 devices in a mesh: seq: 8 (over y, x, core), batch: 4 (over z).
Axes of the slice: x: 2, y: 2, z: 4, core: 2. Of those that a mesh axis runs over, the one named last changes fastest.
Arguments:
- inputs: bfloat16 [8, 1024, 512], P('batch', 'seq'), may hold values from -6 to 6
- doc_lengths: int32 [8, 8], P('batch'), may hold values from 1 to 960, as said below
- norm_gain: float32 [2, 512], replicated, may hold values from 0.1 to 1.9
- decay_log: float32 [2, 384], replicated
- frequency: float32 [2, 384], replicated, may hold values from 0.5 to 30
- step_log: float32 [2, 384], replicated
- in_weight: bfloat16 [2, 512, 768], replicated, may hold values from -0.25 to 0.25
- skip_weight: float32 [2, 512], replicated, may hold values from -4 to 4
- out_weight: bfloat16 [2, 1536, 512], replicated, may hold values from -0.15625 to 0.15625
- glu_weight: bfloat16 [2, 512, 512], replicated, may hold values from -0.25 to 0.25
- cotangent: bfloat16 [8, 1024, 512], P('batch', 'seq'), may hold values from -6 to 6
Outputs:
- output: bfloat16 [8, 1024, 512], P('batch', 'seq')
- input_grad: bfloat16 [8, 1024, 512], P('batch', 'seq')
- gain_grad: float32 [2, 512], replicated
- decay_log_grad: float32 [2, 384], replicated
- frequency_grad: float32 [2, 384], replicated
- step_log_grad: float32 [2, 384], replicated
- in_weight_grad: float32 [2, 512, 768], replicated
- skip_grad: float32 [2, 512], replicated
- out_weight_grad: float32 [2, 1536, 512], replicated
- glu_grad: float32 [2, 512, 512], replicated
Inputs may be any that keep to these rules, and one draw needn't show every extreme that they name: `doc_lengths`: each row's lengths sum to at most 1024; of the 2 rows of each batch index, one holds a document of exactly 960 positions.
All inputs are finite; a program needn't handle non-finite values.
Results may differ from a plain program's by a relative error of at most 0.015.
Values sent between devices are 32-bit elements; how exact they have to be, the bound alone decides.
No kernel may reach another device: no remote copies, remote signals or barrier semaphores. Data moves between devices by JAX's collectives and lax.ppermute only.
A program may use at most 192 MiB of HBM per device.

v0:
```python
import functools
import math

import jax
import jax.numpy as jnp
from jax import lax
from jax.experimental import pallas as pl
from jax.experimental.pallas import tpu as pltpu
from jax.sharding import PartitionSpec as P

epsilon = 1e-05
chunk_count = 8
lane_count = 128
block_rows = 32
vmem_bytes = 56 * 1024 * 1024
gelu_scale = math.sqrt(2.0 / math.pi)
gelu_cubic = 0.044715
f32 = jnp.float32
bf16 = jnp.bfloat16


def complex_mul(left_real, left_imag, right_real, right_imag):
    return (
        left_real * right_real - left_imag * right_imag,
        left_real * right_imag + left_imag * right_real,
    )


def complex_power(real, imag, exponent):
    result = None
    while exponent:
        if exponent & 1:
            result = (real, imag) if result is None else complex_mul(*result, real, imag)
        exponent >>= 1
        if exponent:
            real, imag = complex_mul(real, imag, real, imag)
    return result


def rates(decay_log, frequency, step_log):
    step_size = jnp.exp(step_log)
    pole_real = -jnp.exp(decay_log)
    shrink = step_size * pole_real
    rotation = step_size * frequency
    radius = jnp.exp(shrink)
    decay_real = radius * jnp.cos(rotation)
    decay_imag = radius * jnp.sin(rotation)
    minus_real = jnp.expm1(shrink) * jnp.cos(rotation) - 2.0 * jnp.sin(0.5 * rotation) ** 2
    modulus = pole_real * pole_real + frequency * frequency
    factor_real = (minus_real * pole_real + decay_imag * frequency) / modulus
    factor_imag = (decay_imag * pole_real - minus_real * frequency) / modulus
    return (decay_real, decay_imag, factor_real, factor_imag)


def dot(left, right):
    return lax.dot_general(left, right, (((1,), (0,)), ((), ())), preferred_element_type=f32)


def dot_right(left, right):
    return lax.dot_general(left, right, (((1,), (1,)), ((), ())), preferred_element_type=f32)


def dot_left(left, right):
    return lax.dot_general(left, right, (((0,), (0,)), ((), ())), preferred_element_type=f32)


def spread(narrow, width):
    return jnp.concatenate([narrow] * (width // lane_count), axis=1)


def order_matrix(count, inverse):
    rows = lax.broadcasted_iota(jnp.int32, (count, count), 0)
    cols = lax.broadcasted_iota(jnp.int32, (count, count), 1)
    if inverse:
        rows, cols = cols, rows
    source = lax.rem(rows, chunk_count) * (count // chunk_count) + lax.div(rows, chunk_count)
    return jnp.where(cols == source, 1.0, 0.0).astype(bf16)


def over_blocks(count, body):
    def one(index, carry):
        body(pl.ds(pl.multiple_of(index * block_rows, block_rows), block_rows))
        return carry

    lax.fori_loop(0, count // block_rows, one, 0)


def normalize(values):
    average = jnp.mean(values, axis=-1, keepdims=True)
    centered = values - average
    inverse = lax.rsqrt(jnp.mean(centered * centered, axis=-1, keepdims=True) + epsilon)
    return centered * inverse, inverse


def gelu_parts(mixed):
    square = mixed * mixed
    bend = jnp.tanh(gelu_scale * mixed * (1.0 + gelu_cubic * square))
    half = 0.5 + 0.5 * bend
    slope = half + 0.5 * mixed * (1.0 - bend * bend) * gelu_scale * (
        1.0 + 3.0 * gelu_cubic * square
    )
    return mixed * half, slope


def write_flags(place, docs_ref, flags_ref, blocks_ref, length):
    row_count, doc_count = docs_ref.shape
    span = row_count * length // chunk_count
    per_row = chunk_count // row_count
    offsets = []
    for row in range(row_count):
        running = [jnp.int32(0)]
        for doc in range(doc_count):
            running.append(running[-1] + docs_ref[row, doc])
        offsets.append(running)

    def by_row(row_of, member):
        chosen = jnp.full(row_of.shape, offsets[0][member], jnp.int32)
        for row in range(1, row_count):
            chosen = jnp.where(row_of == row, offsets[row][member], chosen)
        return chosen

    chunk = lax.broadcasted_iota(jnp.int32, (chunk_count, lane_count), 0)
    row_of = lax.div(chunk, per_row)
    bounds = [by_row(row_of, member) for member in range(doc_count + 1)]
    base = place * length + lax.rem(chunk, per_row) * span
    for step in range(span):
        position = base + step
        starts = position == bounds[0]
        endings = position + 1 == bounds[0]
        for bound in bounds[1:]:
            starts = starts | (position == bound)
            endings = endings | (position + 1 == bound)
        window = pl.ds(chunk_count * step, chunk_count)
        flags_ref[0, window, :] = jnp.where(starts, 0.0, 1.0)
        flags_ref[1, window, :] = jnp.where(endings, 0.0, 1.0)
        flags_ref[2, window, :] = jnp.where(position < bounds[-1], 1.0, 0.0)
    entry = lax.broadcasted_iota(jnp.int32, blocks_ref.shape[1:], 0)
    row_of = lax.rem(entry, row_count)
    first = lax.div(entry, row_count) * length
    starts = jnp.zeros(entry.shape, jnp.bool_)
    endings = starts
    for member in range(doc_count + 1):
        bound = by_row(row_of, member)
        starts = starts | ((bound >= first) & (bound < first + length))
        endings = endings | ((bound > first) & (bound <= first + length))
    blocks_ref[0] = jnp.where(starts, 0.0, 1.0)
    blocks_ref[1] = jnp.where(endings, 0.0, 1.0)


def chunk_keeps(flags_ref):
    span = flags_ref.shape[1] // chunk_count
    ahead = flags_ref[0, :chunk_count, :]
    behind = flags_ref[1, :chunk_count, :]
    for step in range(1, span):
        window = pl.ds(chunk_count * step, chunk_count)
        ahead = ahead * flags_ref[0, window, :]
        behind = behind * flags_ref[1, window, :]
    return ahead, behind


def toward(array, distance, reverse):
    return pltpu.roll(array, chunk_count - distance if reverse else distance, axis=0)


def chunk_prefix(ends, factor, entering, per_row, reverse):
    width = ends[0].shape[1]
    chunk = lax.broadcasted_iota(jnp.int32, (chunk_count, width), 0)
    within = lax.rem(chunk, per_row)
    within = per_row - 1 - within if reverse else within
    first = within == 0
    total_real, total_imag = ends
    if entering is not None:
        moved_real, moved_imag = complex_mul(*factor, *entering)
        total_real = total_real + jnp.where(first, moved_real, 0.0)
        total_imag = total_imag + jnp.where(first, moved_imag, 0.0)
    distance = 1
    while distance < per_row:
        reach = within >= distance
        near_real = toward(total_real, distance, reverse)
        near_imag = toward(total_imag, distance, reverse)
        moved_real, moved_imag = complex_mul(*factor, near_real, near_imag)
        total_real = total_real + jnp.where(reach, moved_real, 0.0)
        total_imag = total_imag + jnp.where(reach, moved_imag, 0.0)
        if 2 * distance < per_row:
            far_real = toward(factor[0], distance, reverse)
            far_imag = toward(factor[1], distance, reverse)
            both_real, both_imag = complex_mul(*factor, far_real, far_imag)
            factor = (
                jnp.where(reach, both_real, factor[0]),
                jnp.where(reach, both_imag, factor[1]),
            )
        distance *= 2
    enter_real = toward(total_real, 1, reverse)
    enter_imag = toward(total_imag, 1, reverse)
    none = (jnp.zeros_like(total_real),) * 2 if entering is None else entering
    return (
        (total_real, total_imag),
        (jnp.where(first, none[0], enter_real), jnp.where(first, none[1], enter_imag)),
    )


def sweep(flags_ref, pole_real, pole_imag, forward_at, reverse_at, start, put_forward, put_reverse):
    width = pole_real.shape[1]
    span = flags_ref.shape[1] // chunk_count

    def one(step, state):
        ahead_real, ahead_imag, behind_real, behind_imag = state
        here = pl.ds(pl.multiple_of(chunk_count * step, chunk_count), chunk_count)
        there = pl.ds(pl.multiple_of(chunk_count * (span - 1 - step), chunk_count), chunk_count)
        keep = spread(flags_ref[0, here, :], width)
        moved_real, moved_imag = complex_mul(pole_real * keep, pole_imag * keep, ahead_real, ahead_imag)
        drive_real, drive_imag = forward_at(here)
        ahead_real = moved_real + drive_real
        ahead_imag = moved_imag + drive_imag
        keep = spread(flags_ref[1, there, :], width)
        moved_real, moved_imag = complex_mul(
            pole_real * keep, pole_imag * keep, behind_real, behind_imag
        )
        drive_real, drive_imag = reverse_at(there)
        behind_real = moved_real + drive_real
        behind_imag = moved_imag + drive_imag
        if put_forward is not None:
            put_forward(here, ahead_real, ahead_imag)
            put_reverse(there, behind_real, behind_imag)
        return (ahead_real, ahead_imag, behind_real, behind_imag)

    return lax.fori_loop(0, span, one, start, unroll=4)


def local_totals(flags_ref, pole_real, pole_imag, forward_at, reverse_at, ends_ref, totals_ref):
    width = pole_real.shape[1]
    span = flags_ref.shape[1] // chunk_count
    row_count = totals_ref.shape[0] // 4
    per_row = chunk_count // row_count
    pole_real = jnp.broadcast_to(pole_real, (chunk_count, width))
    pole_imag = jnp.broadcast_to(pole_imag, (chunk_count, width))
    zero = jnp.zeros((chunk_count, width), f32)
    ends = sweep(
        flags_ref, pole_real, pole_imag, forward_at, reverse_at, (zero,) * 4, None, None
    )
    for member in range(4):
        ends_ref[:, member * width : (member + 1) * width] = ends[member]
    power_real, power_imag = complex_power(pole_real, pole_imag, span)
    for direction, keep in enumerate(chunk_keeps(flags_ref)):
        keep = spread(keep, width)
        pair = ends[2 * direction : 2 * direction + 2]
        totals, unused = chunk_prefix(
            pair, (power_real * keep, power_imag * keep), None, per_row, direction == 1
        )
        for part in range(2):
            for row in range(row_count):
                chunk = row * per_row if direction == 1 else (row + 1) * per_row - 1
                entry = (2 * direction + part) * row_count + row
                totals_ref[entry : entry + 1, :] = totals[part][chunk : chunk + 1, :]


def chunk_entrances(place, gathered_ref, flags_ref, blocks_ref, ends_ref, pole_real, pole_imag, length):
    width = pole_real.shape[1]
    span = flags_ref.shape[1] // chunk_count
    row_count = chunk_count * span // length
    per_row = chunk_count // row_count
    device_count = gathered_ref.shape[0] // (4 * row_count)
    pole_real = jnp.broadcast_to(pole_real, (chunk_count, width))
    pole_imag = jnp.broadcast_to(pole_imag, (chunk_count, width))
    power_real, power_imag = complex_power(pole_real, pole_imag, span)
    device_real, device_imag = complex_power(power_real, power_imag, per_row)
    device_real = device_real[:row_count]
    device_imag = device_imag[:row_count]
    entrances = []
    for direction, keep in enumerate(chunk_keeps(flags_ref)):
        real = jnp.zeros((row_count, width), f32)
        imag = real
        for lap in range(device_count):
            source = device_count - 1 - lap if direction == 1 else lap
            live = source > place if direction == 1 else source < place
            open_ = spread(
                blocks_ref[direction, source * row_count : (source + 1) * row_count, :], width
            )
            moved_real, moved_imag = complex_mul(device_real * open_, device_imag * open_, real, imag)
            first = (4 * source + 2 * direction) * row_count
            moved_real = moved_real + gathered_ref[first : first + row_count, :]
            moved_imag = moved_imag + gathered_ref[first + row_count : first + 2 * row_count, :]
            real = jnp.where(live, moved_real, real)
            imag = jnp.where(live, moved_imag, imag)
        entering = tuple(
            jnp.concatenate(
                [
                    jnp.broadcast_to(part[row : row + 1, :], (per_row, width))
                    for row in range(row_count)
                ],
                axis=0,
            )
            for part in (real, imag)
        )
        keep = spread(keep, width)
        first = 2 * direction * width
        ends = (ends_ref[:, first : first + width], ends_ref[:, first + width : first + 2 * width])
        unused, entrance = chunk_prefix(
            ends, (power_real * keep, power_imag * keep), entering, per_row, direction == 1
        )
        entrances.extend(entrance)
    return tuple(entrances)


def layer_poles(tables_ref, layer):
    return tables_ref[4 * layer : 4 * layer + 1, :], tables_ref[4 * layer + 1 : 4 * layer + 2, :]


def layer_factors(tables_ref, layer):
    return tables_ref[4 * layer + 2 : 4 * layer + 3, :], tables_ref[4 * layer + 3 : 4 * layer + 4, :]


def write_bar(tables_ref, layer, in_ref, bar_ref):
    width = tables_ref.shape[1]
    factor_real, factor_imag = layer_factors(tables_ref, layer)

    def body(rows):
        weight_real = in_ref[rows, :width].astype(f32)
        weight_imag = in_ref[rows, width:].astype(f32)
        real, imag = complex_mul(factor_real, factor_imag, weight_real, weight_imag)
        bar_ref[rows, :width] = real.astype(bf16)
        bar_ref[rows, width:] = imag.astype(bf16)

    over_blocks(in_ref.shape[0], body)


def pair_at(ref, first, width):
    def at(rows):
        return ref[rows, first : first + width], ref[rows, first + width : first + 2 * width]

    return at


def drive_totals(flags_ref, tables_ref, layer, scaled_ref, in_ref, bar_ref, drive_ref, ends_ref, totals_ref):
    width = tables_ref.shape[1]
    write_bar(tables_ref, layer, in_ref.ready(), bar_ref)
    drive_ref[...] = dot(scaled_ref[...], bar_ref[...])
    at = pair_at(drive_ref, 0, width)
    local_totals(flags_ref, *layer_poles(tables_ref, layer), at, at, ends_ref, totals_ref)


def settled_states(
    place, gathered_ref, flags_ref, blocks_ref, tables_ref, layer, drive_ref, ends_ref, length,
    states_ref, low_ref, enter_ref,
):
    width = tables_ref.shape[1]
    pole_real, pole_imag = layer_poles(tables_ref, layer)
    entrances = chunk_entrances(
        place, gathered_ref, flags_ref, blocks_ref, ends_ref, pole_real, pole_imag, length
    )
    for member in range(4):
        enter_ref[:, member * width : (member + 1) * width] = entrances[member]

    def put_forward(rows, real, imag):
        states_ref[rows, :width] = real
        states_ref[rows, width : 2 * width] = imag

    def put_reverse(rows, real, imag):
        states_ref[rows, 2 * width : 3 * width] = real
        states_ref[rows, 3 * width :] = imag

    at = pair_at(drive_ref, 0, width)
    sweep(
        flags_ref,
        jnp.broadcast_to(pole_real, (chunk_count, width)),
        jnp.broadcast_to(pole_imag, (chunk_count, width)),
        at, at, entrances, put_forward, put_reverse,
    )

    def body(rows):
        low_ref[rows, :] = states_ref[rows, :].astype(bf16)

    over_blocks(states_ref.shape[0], body)


def mix_and_gate(layer, low_ref, scaled_ref, out_ref, glu_ref, skip_ref, mixed_ref, act_ref, gate_ref):
    mixed_ref[...] = dot(low_ref[...], out_ref.ready()[...])
    skip = skip_ref[layer : layer + 1, :]

    def body(rows):
        mixed = mixed_ref[rows, :] + skip * scaled_ref[rows, :].astype(f32)
        mixed_ref[rows, :] = mixed
        act_ref[rows, :] = gelu_parts(mixed)[0].astype(bf16)

    over_blocks(mixed_ref.shape[0], body)
    gate_ref[...] = dot(act_ref[...], glu_ref.ready()[...])


def back_tail(
    layer, flags_ref, tables_ref, grad_ref, mixed_ref, act_ref, gate_ref, scaled_ref, low_ref,
    out_ref, glu_ref, skip_ref, logits_ref, work_ref, mixed_low_ref,
    d_mixed_ref, d_states_ref, glu_grad_ref, out_grad_ref, skip_grad_ref, ends_ref, totals_ref,
):
    width = tables_ref.shape[1]
    model = mixed_ref.shape[1]

    def first(rows):
        valid = spread(flags_ref[2, rows, :], model)
        gate = gate_ref[rows, :]
        rate = grad_ref[rows, :] * valid * gate
        logits_ref[rows, :] = (rate * act_ref[rows, :].astype(f32) * (1.0 - gate)).astype(bf16)

    over_blocks(mixed_ref.shape[0], first)
    glu_grad_ref[...] = dot_left(act_ref[...], logits_ref[...])
    work_ref[...] = dot_right(logits_ref[...], glu_ref.ready()[...])
    skip_grad_ref[...] = jnp.zeros(skip_grad_ref.shape, f32)

    def second(rows):
        valid = spread(flags_ref[2, rows, :], model)
        d_act = grad_ref[rows, :] * valid * gate_ref[rows, :] + work_ref[rows, :]
        d_mixed = d_act * gelu_parts(mixed_ref[rows, :])[1]
        d_mixed_ref[rows, :] = d_mixed
        mixed_low_ref[rows, :] = d_mixed.astype(bf16)
        skip_grad_ref[...] += jnp.sum(
            d_mixed * scaled_ref[rows, :].astype(f32), axis=0, keepdims=True
        )

    over_blocks(mixed_ref.shape[0], second)
    d_states_ref[...] = dot_right(mixed_low_ref[...], out_ref.ready()[...])
    out_grad_ref[...] = dot_left(low_ref[...], mixed_low_ref[...])
    pole_real, pole_imag = layer_poles(tables_ref, layer)
    local_totals(
        flags_ref, pole_real, -pole_imag, pair_at(d_states_ref, 2 * width, width),
        pair_at(d_states_ref, 0, width), ends_ref, totals_ref,
    )


def back_front(
    place, layer, length, gathered_ref, flags_ref, blocks_ref, tables_ref, gain_ref, skip_ref, in_ref,
    d_states_ref, ends_ref, states_ref, enter_ref, scaled_ref, values_ref, d_mixed_ref, grad_ref,
    lam_ref, mu_ref, low_ref, bar_ref, work_ref,
    in_grad_ref, gain_grad_ref, rate_grad_ref, put_gradient,
):
    width = tables_ref.shape[1]
    model = values_ref.shape[1]
    count = values_ref.shape[0]
    pole_real, pole_imag = layer_poles(tables_ref, layer)
    entrances = chunk_entrances(
        place, gathered_ref, flags_ref, blocks_ref, ends_ref, pole_real, -pole_imag, length
    )

    def put_forward(rows, real, imag):
        mu_ref[rows, :width] = real
        mu_ref[rows, width:] = imag

    def put_reverse(rows, real, imag):
        lam_ref[rows, :width] = real
        lam_ref[rows, width:] = imag

    sweep(
        flags_ref,
        jnp.broadcast_to(pole_real, (chunk_count, width)),
        jnp.broadcast_to(-pole_imag, (chunk_count, width)),
        pair_at(d_states_ref, 2 * width, width), pair_at(d_states_ref, 0, width),
        entrances, put_forward, put_reverse,
    )
    span = count // chunk_count

    def decay_terms(here, before_real, before_imag, after_real, after_imag, sums):
        keep = spread(flags_ref[0, here, :], width)
        lam_real, lam_imag = lam_ref[here, :width], lam_ref[here, width:]
        mu_real, mu_imag = mu_ref[here, :width], mu_ref[here, width:]
        real = keep * (lam_real * before_real + lam_imag * before_imag)
        imag = keep * (lam_imag * before_real - lam_real * before_imag)
        keep = spread(flags_ref[1, here, :], width)
        real = real + keep * (mu_real * after_real + mu_imag * after_imag)
        imag = imag + keep * (mu_imag * after_real - mu_real * after_imag)
        return sums[0] + real, sums[1] + imag

    def window(step):
        start = chunk_count * step
        return pl.ds(start if isinstance(step, int) else pl.multiple_of(start, chunk_count), chunk_count)

    def before_at(step):
        rows = window(step)
        return states_ref[rows, :width], states_ref[rows, width : 2 * width]

    def after_at(step):
        rows = window(step)
        return states_ref[rows, 2 * width : 3 * width], states_ref[rows, 3 * width :]

    def middle(step, sums):
        return decay_terms(window(step), *before_at(step - 1), *after_at(step + 1), sums)

    zero = jnp.zeros((chunk_count, width), f32)
    sums = decay_terms(
        window(0), enter_ref[:, :width], enter_ref[:, width : 2 * width], *after_at(1), (zero, zero)
    )
    sums = lax.fori_loop(1, span - 1, middle, sums, unroll=2)
    sums = decay_terms(
        window(span - 1), *before_at(span - 2),
        enter_ref[:, 2 * width : 3 * width], enter_ref[:, 3 * width :], sums,
    )
    rate_grad_ref[0:1, :] = jnp.sum(sums[0], axis=0, keepdims=True)
    rate_grad_ref[1:2, :] = jnp.sum(sums[1], axis=0, keepdims=True)

    def narrow(rows):
        low_ref[rows, :] = (lam_ref[rows, :] + mu_ref[rows, :]).astype(bf16)

    over_blocks(count, narrow)
    in_ref = in_ref.ready()
    write_bar(tables_ref, layer, in_ref, bar_ref)
    work_ref[...] = dot_right(low_ref[...], bar_ref[...])
    skip = skip_ref[layer : layer + 1, :]
    gain = gain_ref[layer : layer + 1, :]
    gain_grad_ref[...] = jnp.zeros(gain_grad_ref.shape, f32)

    def norm_back(rows):
        valid = spread(flags_ref[2, rows, :], model)
        normed, inverse = normalize(values_ref[rows, :].astype(f32))
        d_scaled = (work_ref[rows, :] + d_mixed_ref[rows, :] * skip) * valid
        gain_grad_ref[...] += jnp.sum(d_scaled * normed, axis=0, keepdims=True)
        d_normed = d_scaled * gain
        put_gradient(
            rows,
            inverse
            * (
                d_normed
                - jnp.mean(d_normed, axis=-1, keepdims=True)
                - normed * jnp.mean(d_normed * normed, axis=-1, keepdims=True)
            )
            + grad_ref[rows, :].astype(f32),
        )

    over_blocks(count, norm_back)
    in_grad_ref[...] = dot_left(scaled_ref[...], low_ref[...])
    factor_real, factor_imag = layer_factors(tables_ref, layer)
    rate_grad_ref[2:4, :] = jnp.zeros((2, width), f32)

    def weigh(rows):
        grad_real, grad_imag = in_grad_ref[rows, :width], in_grad_ref[rows, width:]
        weight_real = in_ref[rows, :width].astype(f32)
        weight_imag = in_ref[rows, width:].astype(f32)
        rate_grad_ref[2:3, :] += jnp.sum(
            grad_real * weight_real + grad_imag * weight_imag, axis=0, keepdims=True
        )
        rate_grad_ref[3:4, :] += jnp.sum(
            grad_imag * weight_real - grad_real * weight_imag, axis=0, keepdims=True
        )
        in_grad_ref[rows, :width] = factor_real * grad_real + factor_imag * grad_imag
        in_grad_ref[rows, width:] = factor_real * grad_imag - factor_imag * grad_real

    over_blocks(in_ref.shape[0], weigh)


def first_kernel(
    length, place_ref, docs_ref, inputs_ref, gain_ref, tables_ref, in_ref,
    flags_ref, blocks_ref, values_ref, scaled_ref, drive_ref, ends_ref, totals_ref, bar_ref,
):
    write_flags(place_ref[0], docs_ref, flags_ref, blocks_ref, length)
    count, model = values_ref.shape
    values_ref[...] = dot(
        order_matrix(count, False), inputs_ref[...].reshape(count, model)
    ).astype(bf16)
    gain = gain_ref[0:1, :]

    def body(rows):
        normed, unused = normalize(values_ref[rows, :].astype(f32))
        valid = spread(flags_ref[2, rows, :], model)
        scaled_ref[rows, :] = (normed * gain * valid).astype(bf16)

    over_blocks(count, body)
    drive_totals(
        flags_ref, tables_ref, 0, scaled_ref, in_ref, bar_ref, drive_ref, ends_ref, totals_ref
    )


def middle_kernel(
    layer, length, place_ref, gathered_ref, flags_ref, blocks_ref, tables_ref, gain_ref, skip_ref,
    drive_ref, ends_ref, values_ref, scaled_ref, out_ref, glu_ref, in_ref,
    states_ref, low_ref, enter_ref, mixed_ref, act_ref, gate_ref,
    next_values_ref, next_scaled_ref, next_drive_ref, next_ends_ref, next_totals_ref, bar_ref,
):
    settled_states(
        place_ref[0], gathered_ref, flags_ref, blocks_ref, tables_ref, layer, drive_ref, ends_ref, length,
        states_ref, low_ref, enter_ref,
    )
    mix_and_gate(
        layer, low_ref, scaled_ref, out_ref, glu_ref, skip_ref, mixed_ref, act_ref, gate_ref
    )
    model = values_ref.shape[1]
    gain = gain_ref[layer + 1 : layer + 2, :]

    def body(rows):
        valid = spread(flags_ref[2, rows, :], model)
        gate = jax.nn.sigmoid(gate_ref[rows, :])
        gate_ref[rows, :] = gate
        result = values_ref[rows, :].astype(f32) + valid * act_ref[rows, :].astype(f32) * gate
        next_values_ref[rows, :] = result
        normed, unused = normalize(result)
        next_scaled_ref[rows, :] = (normed * gain * valid).astype(bf16)

    over_blocks(values_ref.shape[0], body)
    drive_totals(
        flags_ref, tables_ref, layer + 1, next_scaled_ref, in_ref, bar_ref, next_drive_ref,
        next_ends_ref, next_totals_ref,
    )


def turn_kernel(
    layer, length, place_ref, gathered_ref, flags_ref, blocks_ref, tables_ref, skip_ref,
    drive_ref, ends_ref, values_ref, scaled_ref, out_ref, glu_ref, cotangent_ref,
    output_ref, grad_ref, states_ref, enter_ref, d_mixed_ref, d_states_ref,
    glu_grad_ref, out_grad_ref, skip_grad_ref, back_ends_ref, back_totals_ref,
    low_ref, mixed_ref, act_ref, gate_ref, result_ref, logits_ref, work_ref, mixed_low_ref,
):
    settled_states(
        place_ref[0], gathered_ref, flags_ref, blocks_ref, tables_ref, layer, drive_ref, ends_ref, length,
        states_ref, low_ref, enter_ref,
    )
    mix_and_gate(
        layer, low_ref, scaled_ref, out_ref, glu_ref, skip_ref, mixed_ref, act_ref, gate_ref
    )
    count, model = values_ref.shape

    def body(rows):
        valid = spread(flags_ref[2, rows, :], model)
        gate = jax.nn.sigmoid(gate_ref[rows, :])
        gate_ref[rows, :] = gate
        result = values_ref[rows, :] + valid * act_ref[rows, :].astype(f32) * gate
        result_ref[rows, :] = result.astype(bf16)

    over_blocks(count, body)
    output_ref[...] = (
        dot(order_matrix(count, True), result_ref[...]).astype(bf16).reshape(output_ref.shape)
    )
    grad_ref[...] = dot(order_matrix(count, False), cotangent_ref[...].reshape(count, model))
    back_tail(
        layer, flags_ref, tables_ref, grad_ref, mixed_ref, act_ref, gate_ref, scaled_ref, low_ref,
        out_ref, glu_ref, skip_ref, logits_ref, work_ref, mixed_low_ref,
        d_mixed_ref, d_states_ref, glu_grad_ref, out_grad_ref, skip_grad_ref, back_ends_ref,
        back_totals_ref,
    )


def back_middle_kernel(
    layer, length, place_ref, gathered_ref, flags_ref, blocks_ref, tables_ref, gain_ref, skip_ref, in_ref,
    d_states_ref, ends_ref, states_ref, enter_ref, scaled_ref, values_ref, d_mixed_ref, grad_ref,
    out_ref, glu_ref, below_mixed_ref, below_act_ref, below_gate_ref, below_scaled_ref, below_low_ref,
    in_grad_ref, gain_grad_ref, rate_grad_ref, next_grad_ref, below_d_mixed_ref, below_d_states_ref,
    glu_grad_ref, out_grad_ref, skip_grad_ref, below_ends_ref, below_totals_ref,
    lam_ref, mu_ref, low_ref, bar_ref, work_ref, logits_ref, mixed_low_ref,
):
    def put_gradient(rows, gradient):
        next_grad_ref[rows, :] = gradient

    back_front(
        place_ref[0], layer, length, gathered_ref, flags_ref, blocks_ref, tables_ref, gain_ref, skip_ref,
        in_ref, d_states_ref, ends_ref, states_ref, enter_ref, scaled_ref, values_ref, d_mixed_ref,
        grad_ref, lam_ref, mu_ref, low_ref, bar_ref, work_ref,
        in_grad_ref, gain_grad_ref, rate_grad_ref, put_gradient,
    )
    back_tail(
        layer - 1, flags_ref, tables_ref, next_grad_ref, below_mixed_ref, below_act_ref, below_gate_ref,
        below_scaled_ref, below_low_ref, out_ref, glu_ref, skip_ref, logits_ref, work_ref, mixed_low_ref,
        below_d_mixed_ref, below_d_states_ref, glu_grad_ref, out_grad_ref, skip_grad_ref,
        below_ends_ref, below_totals_ref,
    )


def back_last_kernel(
    length, place_ref, gathered_ref, flags_ref, blocks_ref, tables_ref, gain_ref, skip_ref, in_ref,
    d_states_ref, ends_ref, states_ref, enter_ref, scaled_ref, values_ref, d_mixed_ref, grad_ref,
    in_grad_ref, gain_grad_ref, rate_grad_ref, input_grad_ref,
    lam_ref, mu_ref, low_ref, bar_ref, work_ref, result_ref,
):
    def put_gradient(rows, gradient):
        result_ref[rows, :] = gradient.astype(bf16)

    back_front(
        place_ref[0], 0, length, gathered_ref, flags_ref, blocks_ref, tables_ref, gain_ref, skip_ref,
        in_ref, d_states_ref, ends_ref, states_ref, enter_ref, scaled_ref, values_ref, d_mixed_ref,
        grad_ref, lam_ref, mu_ref, low_ref, bar_ref, work_ref,
        in_grad_ref, gain_grad_ref, rate_grad_ref, put_gradient,
    )
    count = result_ref.shape[0]
    input_grad_ref[...] = (
        dot(order_matrix(count, True), result_ref[...]).astype(bf16).reshape(input_grad_ref.shape)
    )


class Fetch:
    def __init__(self, stack_ref, layer, target, semaphore):
        self.copy = pltpu.make_async_copy(stack_ref.at[layer], target, semaphore)
        self.target = target
        self.waiting = True
        self.copy.start()

    def ready(self):
        if self.waiting:
            self.copy.wait()
            self.waiting = False
        return self.target


def call(body, name, operands, outs, scratch):
    scalars = {"place", "docs"}
    arrays = []
    specs = []
    layers = {}
    for position, (key, operand) in enumerate(operands):
        space = pltpu.SMEM if key in scalars else pltpu.VMEM
        if isinstance(operand, tuple):
            operand, layers[position] = operand
            space = pl.ANY
        specs.append(pl.BlockSpec(memory_space=space))
        arrays.append(operand)
    fetched = [
        pltpu.VMEM(arrays[position].shape[1:], arrays[position].dtype) for position in layers
    ]

    def kernel(*refs):
        given = list(refs[: len(arrays)])
        rest = refs[len(arrays) : len(refs) - len(fetched) - 1]
        targets = refs[len(refs) - len(fetched) - 1 : -1]
        for index, (position, layer) in enumerate(layers.items()):
            given[position] = Fetch(given[position], layer, targets[index], refs[-1].at[index])
        body(*given, *rest)

    return pl.pallas_call(
        kernel,
        name=name,
        in_specs=specs,
        out_specs=[pl.BlockSpec(memory_space=pltpu.VMEM)] * len(outs),
        out_shape=[jax.ShapeDtypeStruct(shape, kind) for shape, kind in outs],
        scratch_shapes=[pltpu.VMEM(shape, kind) for shape, kind in scratch]
        + fetched
        + [pltpu.SemaphoreType.DMA((max(1, len(fetched)),))],
        compiler_params=pltpu.CompilerParams(vmem_limit_bytes=vmem_bytes),
    )(*arrays)


def on_device(
    inputs,
    doc_lengths,
    norm_gain,
    decay_log,
    frequency,
    step_log,
    in_weight,
    skip_weight,
    out_weight,
    glu_weight,
    cotangent,
):
    row_count, length, model = inputs.shape
    layer_count, width = decay_log.shape
    count = row_count * length
    device_count = lax.axis_size("seq")
    place = lax.axis_index("seq").astype(jnp.int32).reshape(1)
    rate_tables, rates_back = jax.vjp(rates, decay_log, frequency, step_log)
    tables = jnp.stack(rate_tables, axis=1).reshape(4 * layer_count, width)

    def gather(totals):
        return lax.all_gather(totals, "seq", axis=0, tiled=True)

    flags_out = ((3, count, lane_count), f32)
    blocks_out = ((2, device_count * row_count, lane_count), f32)
    wide_out = ((count, 4 * width), f32)
    ends_out = ((chunk_count, 4 * width), f32)
    totals_out = ((4 * row_count, width), f32)
    tokens = ((count, model), f32)
    tokens_low = ((count, model), bf16)
    drive_out = ((count, 2 * width), f32)
    bar_out = ((model, 2 * width), bf16)
    glu_out = ((model, model), f32)
    out_out = ((4 * width, model), f32)
    in_out = ((model, 2 * width), f32)
    vector = ((1, model), f32)

    flags, blocks, values, scaled, drive, ends, totals = call(
        functools.partial(first_kernel, length),
        "first",
        (
            ("place", place),
            ("docs", doc_lengths),
            ("inputs", inputs),
            ("gain", norm_gain),
            ("tables", tables),
            ("in", (in_weight, 0)),
        ),
        (flags_out, blocks_out, tokens_low, tokens_low, drive_out, ends_out, totals_out),
        (bar_out,),
    )
    shared = (("flags", flags), ("blocks", blocks), ("tables", tables))
    kept = []
    for layer in range(layer_count - 1):
        gathered = gather(totals)
        (
            states, low, enter, mixed, act, gate, next_values, next_scaled, drive, ends, totals,
        ) = call(
            functools.partial(middle_kernel, layer, length),
            "middle",
            (
                ("place", place),
                ("gathered", gathered),
                *shared,
                ("gain", norm_gain),
                ("skip", skip_weight),
                ("drive", drive),
                ("ends", ends),
                ("values", values),
                ("scaled", scaled),
                ("out", (out_weight, layer)),
                ("glu", (glu_weight, layer)),
                ("in", (in_weight, layer + 1)),
            ),
            (
                wide_out, ((count, 4 * width), bf16), ends_out, tokens, tokens_low, tokens,
                tokens, tokens_low, drive_out, ends_out, totals_out,
            ),
            (bar_out,),
        )
        kept.append((states, low, enter, mixed, act, gate, values, scaled))
        values, scaled = next_values, next_scaled
    layer = layer_count - 1
    gathered = gather(totals)
    (
        output, grad, states, enter, d_mixed, d_states, glu_grad, out_grad, skip_grad, ends, totals,
    ) = call(
        functools.partial(turn_kernel, layer, length),
        "turn",
        (
            ("place", place),
            ("gathered", gathered),
            *shared,
            ("skip", skip_weight),
            ("drive", drive),
            ("ends", ends),
            ("values", values),
            ("scaled", scaled),
            ("out", (out_weight, layer)),
            ("glu", (glu_weight, layer)),
            ("cotangent", cotangent),
        ),
        (
            (inputs.shape, bf16), tokens, wide_out, ends_out, tokens, wide_out,
            glu_out, out_out, vector, ends_out, totals_out,
        ),
        (
            ((count, 4 * width), bf16), tokens, tokens_low, tokens, tokens_low, tokens_low, tokens,
            tokens_low,
        ),
    )
    glu_grads, out_grads, skip_grads = [glu_grad], [out_grad], [skip_grad]
    in_grads, gain_grads, rate_grads = [], [], []
    back_scratch = (
        drive_out, drive_out, ((count, 2 * width), bf16), bar_out, tokens,
    )
    rate_out = ((4, width), f32)
    for layer in reversed(range(1, layer_count)):
        gathered = gather(totals)
        low_states, low, low_enter, mixed, act, gate, low_values, low_scaled = kept[layer - 1]
        (
            in_grad, gain_grad, rate_grad, grad, d_mixed, d_states, glu_grad, out_grad, skip_grad, ends,
            totals,
        ) = call(
            functools.partial(back_middle_kernel, layer, length),
            "back_middle",
            (
                ("place", place),
                ("gathered", gathered),
                *shared,
                ("gain", norm_gain),
                ("skip", skip_weight),
                ("in", (in_weight, layer)),
                ("d_states", d_states),
                ("ends", ends),
                ("states", states),
                ("enter", enter),
                ("scaled", scaled),
                ("values", values),
                ("d_mixed", d_mixed),
                ("grad", grad),
                ("out", (out_weight, layer - 1)),
                ("glu", (glu_weight, layer - 1)),
                ("mixed", mixed),
                ("act", act),
                ("gate", gate),
                ("below_scaled", low_scaled),
                ("low", low),
            ),
            (
                in_out, vector, rate_out, tokens, tokens, wide_out, glu_out, out_out, vector, ends_out,
                totals_out,
            ),
            back_scratch + (tokens_low, tokens_low),
        )
        in_grads.append(in_grad)
        gain_grads.append(gain_grad)
        rate_grads.append(rate_grad)
        glu_grads.append(glu_grad)
        out_grads.append(out_grad)
        skip_grads.append(skip_grad)
        states, enter, values, scaled = low_states, low_enter, low_values, low_scaled
    gathered = gather(totals)
    in_grad, gain_grad, rate_grad, input_grad = call(
        functools.partial(back_last_kernel, length),
        "back_last",
        (
            ("place", place),
            ("gathered", gathered),
            *shared,
            ("gain", norm_gain),
            ("skip", skip_weight),
            ("in", (in_weight, 0)),
            ("d_states", d_states),
            ("ends", ends),
            ("states", states),
            ("enter", enter),
            ("scaled", scaled),
            ("values", values),
            ("d_mixed", d_mixed),
            ("grad", grad),
        ),
        (in_out, vector, rate_out, (inputs.shape, bf16)),
        back_scratch + (tokens_low,),
    )
    in_grads.append(in_grad)
    gain_grads.append(gain_grad)
    rate_grads.append(rate_grad)

    def stack(terms):
        return jnp.stack(terms[::-1])

    in_sum, out_sum, glu_sum, rate_sum, gain_sum, skip_sum = lax.psum(
        (
            stack(in_grads),
            stack(out_grads),
            stack(glu_grads),
            stack(rate_grads),
            stack(gain_grads),
            stack(skip_grads),
        ),
        ("seq", "batch"),
    )
    decay_grad, frequency_grad, step_grad = rates_back(
        tuple(rate_sum[:, member] for member in range(4))
    )
    return (
        output,
        input_grad,
        gain_sum[:, 0],
        decay_grad,
        frequency_grad,
        step_grad,
        in_sum,
        skip_sum[:, 0],
        out_sum,
        glu_sum,
    )


def solution(mesh):
    in_specs = (
        P("batch", "seq", None),
        P("batch", None),
        P(),
        P(),
        P(),
        P(),
        P(),
        P(),
        P(),
        P(),
        P("batch", "seq", None),
    )
    out_specs = (
        P("batch", "seq", None),
        P("batch", "seq", None),
        P(),
        P(),
        P(),
        P(),
        P(),
        P(),
        P(),
        P(),
    )
    return jax.shard_map(
        on_device, mesh=mesh, in_specs=in_specs, out_specs=out_specs, check_vma=False
    )
```

profile of v0, /device:TPU:0, one launch (start us, length us, event | category | flops | bytes accessed | tf_op | source)
XLA Modules:
  0.0 350.3 jit_solution(8368136428491603175)
XLA Ops:
  7.2 0.0 all-reduce.4.cloned.1.call-start
  7.2 0.8 multiply_bitcast_fusion
  8.1 0.6 reshape.27.refs_4_
  8.7 5.2 %first.1 = (f32[3,256,128]{2,1,0:T(8,128)}, f32[2,16,128]{2,1,0:T(8,128)}, bf16[256,512]{1,0:T(8,128)(2,1)}, bf16[256,512]{1,0:T(8,128)(2,1)}, f32[256,768]{1,0:...) custom-call(s32[1]{0:T(128)} %bitcast.refs_0_, s32[2,8]{1,0:T(2,128)} %refs_1_.1, bf16[2,128,512]{2,1,0:T(8,128)(2,1)} %refs_2_.1, ...), custom_call_target="tpu_custom_call" | custom-call | tf_op jit(solution)/shard_map/first/pallas_call | solution.py:720
  13.9 12.4 %all_gather.12.refs_1_ = f32[64,384]{1,0:T(8,128)} all-gather(f32[8,384]{1,0:T(8,128)} %get-tuple-element.54), channel_id=1, replica_groups=mesh['seq'=8,'batch'=4] {'seq'}, dimensions={0}, use_global_device_ids=true | all-gather | bytes 110592 | tf_op jit(solution)/shard_map/all_gather | solution.py:755
  26.3 9.1 %middle.1 = (f32[256,1536]{1,0:T(8,128)}, bf16[256,1536]{1,0:T(8,128)(2,1)}, f32[8,1536]{1,0:T(8,128)}, f32[256,512]{1,0:T(8,128)}, bf16[256,512]{1,0:T(8,128)(2...) custom-call(s32[1]{0:T(128)} %bitcast.refs_0_, ...), custom_call_target="tpu_custom_call" | custom-call | tf_op jit(solution)/shard_map/middle/pallas_call | solution.py:720
  35.5 10.0 %all_gather.13.refs_1_ = f32[64,384]{1,0:T(8,128)} all-gather(f32[8,384]{1,0:T(8,128)} %get-tuple-element.61), channel_id=1, replica_groups=mesh['seq'=8,'batch'=4] {'seq'}, dimensions={0}, use_global_device_ids=true | all-gather | bytes 110592 | tf_op jit(solution)/shard_map/all_gather | solution.py:755
  45.4 10.6 %turn.1 = (bf16[2,128,512]{2,1,0:T(8,128)(2,1)}, f32[256,512]{1,0:T(8,128)}, f32[256,1536]{1,0:T(8,128)}, f32[8,1536]{1,0:T(8,128)}, f32[256,512]{1,0:T(8,128)},...) custom-call(s32[1]{0:T(128)} %bitcast.refs_0_, ...), custom_call_target="tpu_custom_call" | custom-call | tf_op jit(solution)/shard_map/turn/pallas_call | solution.py:720
  56.0 10.0 %all_gather.14.refs_1_ = f32[64,384]{1,0:T(8,128)} all-gather(f32[8,384]{1,0:T(8,128)} %get-tuple-element.67), channel_id=1, replica_groups=mesh['seq'=8,'batch'=4] {'seq'}, dimensions={0}, use_global_device_ids=true | all-gather | bytes 110592 | tf_op jit(solution)/shard_map/all_gather | solution.py:755
  66.0 14.7 %back_middle.1 = (f32[512,768]{1,0:T(8,128)}, f32[1,512]{1,0:T(1,128)}, f32[4,384]{1,0:T(4,128)}, f32[256,512]{1,0:T(8,128)}, f32[256,512]{1,0:T(8,128)}, /*inde...) custom-call(s32[1]{0:T(128)} %bitcast.refs_0_, ...), custom_call_target="tpu_custom_call" | custom-call | tf_op jit(solution)/shard_map/back_middle/pallas_call | solution.py:720
  80.7 10.1 %all_gather.15.refs_1_ = f32[64,384]{1,0:T(8,128)} all-gather(f32[8,384]{1,0:T(8,128)} %get-tuple-element.78), channel_id=1, replica_groups=mesh['seq'=8,'batch'=4] {'seq'}, dimensions={0}, use_global_device_ids=true | all-gather | bytes 110592 | tf_op jit(solution)/shard_map/all_gather | solution.py:755
  90.9 2.7 pad_maximum_fusion.2
  93.6 9.1 %back_last.1 = (f32[512,768]{1,0:T(8,128)}, f32[1,512]{1,0:T(1,128)}, f32[4,384]{1,0:T(4,128)}, bf16[2,128,512]{2,1,0:T(8,128)(2,1)}) custom-call(s32[1]{0:T(128)} %bitcast.refs_0_, f32[64,384]{1,0:T(8,128)} %all_gather.15.refs_1_, f32[3,256,128]{2,1,0:T(8,128)} %get-tuple-element.55.refs_2_, f32[2,16,128]{2,1,0:T(8,128)} %get-tuple-element.56.refs_3_, ...), custom_call_target="tpu_custom_call" | custom-call | tf_op jit(solution)/shard_map/back_last/pallas_call | solution.py:720
  102.7 0.0 copy-start.2
  102.7 3.5 pad_maximum_fusion.1
  106.2 1.0 copy-done.2
  107.1 3.4 pad_maximum_fusion
  110.6 0.0 all-reduce.4.cloned.1.call-update
  110.6 0.6 copy-done.11
  111.2 0.0 copy-done.12
  111.2 0.0 copy-done.13
  111.2 0.0 copy-done.14
  111.3 0.0 copy-done.9
  111.3 0.0 copy-done.10
  111.3 41.2 %all-reduce = (f32[2,512]{1,0:T(2,128)}, f32[2,4,384]{2,1,0:T(4,128)S(1)}, f32[2,512]{1,0:T(2,128)}) all-reduce(f32[2,512]{1,0:T(2,128)S(1)} %get-tuple-element.115, f32[2,4,384]{2,1,0:T(4,128)S(1)} %pad_maximum_fusion.4, f32[2,512]{1,0:T(2,128)S(1)} %get-tuple-element.116), channel_id=1, replica_groups=mesh['seq'=8,'batch'=4] {'seq','batch'}, use_global_device_ids=true, to_apply=%region_0.0 | all-reduce | flops 5120 | bytes 40960 | tf_op jit(solution)/shard_map/psum | solution.py:926
  152.6 0.7 add_multiply_fusion
  153.3 180.8 %all-reduce.4.cloned.1.call-done = (f32[2,512,768]{2,1,0:T(8,128)}, f32[2,1536,512]{2,1,0:T(8,128)}, f32[2,512,512]{2,1,0:T(8,128)}) async-done(((f32[2,512,768]{2,1,0:T(8,128)}, f32[2,1536,512]{2,1,0:T(8,128)}, f32[2,512,512]{2,1,0:T(8,128)}), (f32[2,512,768]{2,1,0:T(8,128)}, f32[2,1536,512]{2,1,0:T(8,128)}, f32[2,512,512]{2,1,0:T(8,128)})) %all-reduce.4.cloned.1.call-update) | async-done | bytes 11534352 | tf_op jit(solution)/shard_map/psum | solution.py:926
  334.1 3.9 %copy.83 = f32[2,512,768]{2,1,0:T(8,128)} copy(f32[2,512,768]{2,1,0:T(8,128)} %get-tuple-element.123) | data formatting | bytes 6291456
  338.0 1.0 copy-done
  339.0 2.8 copy.84
  341.8 0.3 copy-done.3
  342.1 1.3 copy.85
  (25 shorter events, 0.1 us)
Async XLA Ops:
  7.2 326.9 %all-reduce.4.cloned.1.call-start = ((), (), s32[]{:S(2)}) async-start(), calls=%async_computation | async-start | bytes 23068672 | tf_op jit(solution)/shard_map/psum | solution.py:926
  66.0 24.8 %copy-start.5 = (f32[512,512]{1,0:T(8,128)S(1)}, f32[512,512]{1,0:T(8,128)}, u32[]{:S(2)}) copy-start(f32[512,512]{1,0:T(8,128)} %get-tuple-element.97) | copy-start | bytes 3145732
  93.6 9.1 %copy-start.4 = (f32[512,768]{1,0:T(8,128)S(1)}, f32[512,768]{1,0:T(8,128)}, u32[]{:S(2)}) copy-start(f32[512,768]{1,0:T(8,128)} %get-tuple-element.91) | copy-start | bytes 4718596
  102.7 3.5 copy-start.1
  102.7 4.4 %copy-start.2 = (f32[1536,512]{1,0:T(8,128)S(1)}, f32[1536,512]{1,0:T(8,128)}, u32[]{:S(2)}) copy-start(f32[1536,512]{1,0:T(8,128)} %get-tuple-element.94) | copy-start | bytes 9437188
  110.5 0.7 copy-start.11
  110.5 0.7 copy-start.12
  110.5 0.7 copy-start.13
  110.5 0.7 copy-start.14
  110.5 0.7 copy-start.9
  110.6 0.8 copy-start.10
  110.6 42.0 %copy-start.6 = (f32[2,384]{1,0:T(2,128)S(1)}, f32[2,384]{1,0:T(2,128)}, u32[]{:S(2)}) copy-start(f32[2,384]{1,0:T(2,128)} %param.15) | copy-start | bytes 9220
  110.6 42.0 %copy-start.7 = (f32[2,384]{1,0:T(2,128)S(1)}, f32[2,384]{1,0:T(2,128)}, u32[]{:S(2)}) copy-start(f32[2,384]{1,0:T(2,128)} %param.16) | copy-start | bytes 9220
  110.6 42.0 %copy-start.8 = (f32[2,384]{1,0:T(2,128)S(1)}, f32[2,384]{1,0:T(2,128)}, u32[]{:S(2)}) copy-start(f32[2,384]{1,0:T(2,128)} %param.14) | copy-start | bytes 9220
  334.1 4.9 %copy-start = (f32[2,1536,512]{2,1,0:T(8,128)S(1)}, f32[2,1536,512]{2,1,0:T(8,128)}, u32[]{:S(2)}) copy-start(f32[2,1536,512]{2,1,0:T(8,128)} %get-tuple-element.125) | copy-start | bytes 18874372
  339.0 3.1 copy-start.3
Sparse Core Ops, SparseCore 0:
  110.7 223.3 all-reduce.3
where the time goes:
time: 351 us; the launch traced here: 350 us
  waiting for transfers between devices  181 us (52%)
  blocking collectives  83.7 us (24%)
  Pallas kernels  48.7 us (14%)
  between operations  14.2 us (4%)
  local copies, waits for them, and re-layouts  11.6 us (3%)
  other arithmetic  11.2 us (3%)
    psum x1, waiting for transfers between devices, on_device(): lax.psum((stack(in_grads), stack(out_grads), stack(glu_grads), stack(rate...  181 us
    pallas_call x5, Pallas kernels, call(): pl.pallas_call(kernel, name=name, in_specs=specs, out_specs=[pl.BlockSpec...  48.7 us
    all_gather x4, blocking collectives, gather(): return lax.all_gather(totals, 'seq', axis=0, tiled=True)  42.5 us
    psum x1, blocking collectives, on_device(): lax.psum((stack(in_grads), stack(out_grads), stack(glu_grads), stack(rate...  41.2 us
    unnamed x33, local copies, waits for them, and re-layouts  11 us
    another operation x4, other arithmetic, stack(): return jnp.stack(terms[::-1])  9.6 us
  transfers between devices with their start and end apart: 1, of which 1 were waited for; matrix products, arithmetic and copies ran while one was open for 0% of the time, Pallas kernels for 0%

commit v1 on v0

--- a/solution.py
+++ b/solution.py
@@ -12,7 +12,7 @@
 chunk_count = 8
 lane_count = 128
 block_rows = 32
-vmem_bytes = 56 * 1024 * 1024
+vmem_bytes = 32 * 1024 * 1024
 gelu_scale = math.sqrt(2.0 / math.pi)
 gelu_cubic = 0.044715
 f32 = jnp.float32
@@ -389,7 +389,7 @@
 def back_tail(
     layer, flags_ref, tables_ref, grad_ref, mixed_ref, act_ref, gate_ref, scaled_ref, low_ref,
     out_ref, glu_ref, skip_ref, logits_ref, work_ref, mixed_low_ref,
-    d_mixed_ref, d_states_ref, glu_grad_ref, out_grad_ref, skip_grad_ref, ends_ref, totals_ref,
+    d_mixed_ref, d_states_ref, glu_grad_ref, out_grad_ref, skip_grad_ref, ends_ref, totals_ref, emit,
 ):
     width = tables_ref.shape[1]
     model = mixed_ref.shape[1]
@@ -402,6 +402,7 @@
 
     over_blocks(mixed_ref.shape[0], first)
     glu_grad_ref[...] = dot_left(act_ref[...], logits_ref[...])
+    emit.put("glu", glu_grad_ref)
     work_ref[...] = dot_right(logits_ref[...], glu_ref.ready()[...])
     skip_grad_ref[...] = jnp.zeros(skip_grad_ref.shape, f32)
 
@@ -416,8 +417,9 @@
         )
 
     over_blocks(mixed_ref.shape[0], second)
+    out_grad_ref[...] = dot_left(low_ref[...], mixed_low_ref[...])
+    emit.put("out", out_grad_ref)
     d_states_ref[...] = dot_right(mixed_low_ref[...], out_ref.ready()[...])
-    out_grad_ref[...] = dot_left(low_ref[...], mixed_low_ref[...])
     pole_real, pole_imag = layer_poles(tables_ref, layer)
     local_totals(
         flags_ref, pole_real, -pole_imag, pair_at(d_states_ref, 2 * width, width),
@@ -429,7 +431,7 @@
     place, layer, length, gathered_ref, flags_ref, blocks_ref, tables_ref, gain_ref, skip_ref, in_ref,
     d_states_ref, ends_ref, states_ref, enter_ref, scaled_ref, values_ref, d_mixed_ref, grad_ref,
     lam_ref, mu_ref, low_ref, bar_ref, work_ref,
-    in_grad_ref, gain_grad_ref, rate_grad_ref, put_gradient,
+    in_grad_ref, gain_grad_ref, rate_grad_ref, put_gradient, emit,
 ):
     width = tables_ref.shape[1]
     model = values_ref.shape[1]
@@ -541,6 +543,7 @@
         in_grad_ref[rows, width:] = factor_real * grad_imag - factor_imag * grad_real
 
     over_blocks(in_ref.shape[0], weigh)
+    emit.put("in", in_grad_ref)
 
 
 def first_kernel(
@@ -601,9 +604,11 @@
     layer, length, place_ref, gathered_ref, flags_ref, blocks_ref, tables_ref, skip_ref,
     drive_ref, ends_ref, values_ref, scaled_ref, out_ref, glu_ref, cotangent_ref,
     output_ref, grad_ref, states_ref, enter_ref, d_mixed_ref, d_states_ref,
-    glu_grad_ref, out_grad_ref, skip_grad_ref, back_ends_ref, back_totals_ref,
+    keep_ref, send_ref, skip_grad_ref, back_ends_ref, back_totals_ref,
     low_ref, mixed_ref, act_ref, gate_ref, result_ref, logits_ref, work_ref, mixed_low_ref,
+    glu_grad_ref, out_grad_ref,
 ):
+    emit = Emit(tail_layout(values_ref.shape[1], tables_ref.shape[1]), keep_ref, send_ref)
     settled_states(
         place_ref[0], gathered_ref, flags_ref, blocks_ref, tables_ref, layer, drive_ref, ends_ref, length,
         states_ref, low_ref, enter_ref,
@@ -629,7 +634,7 @@
         layer, flags_ref, tables_ref, grad_ref, mixed_ref, act_ref, gate_ref, scaled_ref, low_ref,
         out_ref, glu_ref, skip_ref, logits_ref, work_ref, mixed_low_ref,
         d_mixed_ref, d_states_ref, glu_grad_ref, out_grad_ref, skip_grad_ref, back_ends_ref,
-        back_totals_ref,
+        back_totals_ref, emit,
     )
 
 
@@ -637,10 +642,16 @@
     layer, length, place_ref, gathered_ref, flags_ref, blocks_ref, tables_ref, gain_ref, skip_ref, in_ref,
     d_states_ref, ends_ref, states_ref, enter_ref, scaled_ref, values_ref, d_mixed_ref, grad_ref,
     out_ref, glu_ref, below_mixed_ref, below_act_ref, below_gate_ref, below_scaled_ref, below_low_ref,
-    in_grad_ref, gain_grad_ref, rate_grad_ref, next_grad_ref, below_d_mixed_ref, below_d_states_ref,
-    glu_grad_ref, out_grad_ref, skip_grad_ref, below_ends_ref, below_totals_ref,
+    keep_ref, send_ref, in_keep_ref, in_send_ref, gain_grad_ref, rate_grad_ref, next_grad_ref,
+    below_d_mixed_ref,
+    below_d_states_ref, skip_grad_ref, below_ends_ref, below_totals_ref,
     lam_ref, mu_ref, low_ref, bar_ref, work_ref, logits_ref, mixed_low_ref,
+    in_grad_ref, glu_grad_ref, out_grad_ref,
 ):
+    model, width = values_ref.shape[1], tables_ref.shape[1]
+    emit = Emit(tail_layout(model, width), keep_ref, send_ref)
+    in_emit = Emit(in_layout(model, width), in_keep_ref, in_send_ref)
+
     def put_gradient(rows, gradient):
         next_grad_ref[rows, :] = gradient
 
@@ -648,22 +659,32 @@
         place_ref[0], layer, length, gathered_ref, flags_ref, blocks_ref, tables_ref, gain_ref, skip_ref,
         in_ref, d_states_ref, ends_ref, states_ref, enter_ref, scaled_ref, values_ref, d_mixed_ref,
         grad_ref, lam_ref, mu_ref, low_ref, bar_ref, work_ref,
-        in_grad_ref, gain_grad_ref, rate_grad_ref, put_gradient,
+        in_grad_ref, gain_grad_ref, rate_grad_ref, put_gradient, in_emit,
     )
     back_tail(
         layer - 1, flags_ref, tables_ref, next_grad_ref, below_mixed_ref, below_act_ref, below_gate_ref,
         below_scaled_ref, below_low_ref, out_ref, glu_ref, skip_ref, logits_ref, work_ref, mixed_low_ref,
         below_d_mixed_ref, below_d_states_ref, glu_grad_ref, out_grad_ref, skip_grad_ref,
-        below_ends_ref, below_totals_ref,
+        below_ends_ref, below_totals_ref, emit,
     )
 
 
 def back_last_kernel(
     length, place_ref, gathered_ref, flags_ref, blocks_ref, tables_ref, gain_ref, skip_ref, in_ref,
     d_states_ref, ends_ref, states_ref, enter_ref, scaled_ref, values_ref, d_mixed_ref, grad_ref,
-    in_grad_ref, gain_grad_ref, rate_grad_ref, input_grad_ref,
-    lam_ref, mu_ref, low_ref, bar_ref, work_ref, result_ref,
+    *rest,
 ):
+    layer_count = gain_ref.shape[0]
+    skip_grads = rest[:layer_count]
+    rest = rest[layer_count:]
+    gain_grads = rest[: layer_count - 1]
+    rate_grads = rest[layer_count - 1 : 2 * layer_count - 2]
+    (
+        keep_ref, send_ref, input_grad_ref,
+        lam_ref, mu_ref, low_ref, bar_ref, work_ref, result_ref,
+        in_grad_ref, gain_grad_ref, rate_grad_ref, small_ref,
+    ) = rest[2 * layer_count - 2 :]
+    emit = Emit(last_layout(values_ref.shape[1], tables_ref.shape[1]), keep_ref, send_ref)
     def put_gradient(rows, gradient):
         result_ref[rows, :] = gradient.astype(bf16)
 
@@ -671,12 +692,250 @@
         place_ref[0], 0, length, gathered_ref, flags_ref, blocks_ref, tables_ref, gain_ref, skip_ref,
         in_ref, d_states_ref, ends_ref, states_ref, enter_ref, scaled_ref, values_ref, d_mixed_ref,
         grad_ref, lam_ref, mu_ref, low_ref, bar_ref, work_ref,
-        in_grad_ref, gain_grad_ref, rate_grad_ref, put_gradient,
-    )
+        in_grad_ref, gain_grad_ref, rate_grad_ref, put_gradient, emit,
+    )
+    small_ref[...] = jnp.zeros(small_ref.shape, f32)
+    row = 0
+    for vectors in ((gain_grad_ref, *gain_grads), skip_grads, (rate_grad_ref, *rate_grads)):
+        for vector_ref in vectors:
+            for line in range(vector_ref.shape[0]):
+                for first in range(0, vector_ref.shape[1], lane_count):
+                    small_ref[row : row + 1, :] = vector_ref[line : line + 1, first : first + lane_count]
+                    row += 1
+    emit.put("small", small_ref)
     count = result_ref.shape[0]
     input_grad_ref[...] = (
         dot(order_matrix(count, True), result_ref[...]).astype(bf16).reshape(input_grad_ref.shape)
     )
+
+
+halvings = 3
+half_blocks = 1 << halvings
+tail_kind = "plane"
+in_kind = "plane"
+last_kind = "plane"
+round_order = "bacdbacdbcadbcadbcadbcdacbdcdc"
+
+
+def mesh_bits():
+    seq_bits = lax.axis_size("seq").bit_length() - 1
+    batch_bits = lax.axis_size("batch").bit_length() - 1
+    deep = [1 << place for place in range(batch_bits)]
+    core = 1 << batch_bits
+    plane = [core << place for place in range(1, seq_bits)]
+    return deep, core, plane[: len(plane) // 2], plane[len(plane) // 2 :]
+
+
+def axis_orders(kind):
+    deep, core, across, along = mesh_bits()
+    orders = {
+        "plane": (across + along + deep, along + across + deep),
+        "deep": (deep + across + along, deep + along + across),
+        "mixed": (across + along + deep, along + deep + across),
+    }
+    return core, orders[kind]
+
+
+def half_bases(kind):
+    core, orders = axis_orders(kind)
+    index = lax.axis_index("seq") * lax.axis_size("batch") + lax.axis_index("batch")
+    side = lax.rem(lax.div(index, core), 2)
+    numbers = []
+    for order in orders:
+        number = 0
+        for bit in order[:halvings]:
+            number = 2 * number + lax.rem(lax.div(index, bit), 2)
+        numbers.append(number)
+    keep = (1 - side) * numbers[0] + side * numbers[1]
+    send = (1 - side) * numbers[1] + side * numbers[0]
+    return side * half_blocks + keep, (1 - side) * half_blocks + send
+
+
+def swap(array, first, second):
+    core = mesh_bits()[1]
+    total = lax.axis_size("seq") * lax.axis_size("batch")
+    pairs = [(index, index ^ (second if index & core else first)) for index in range(total)]
+    return lax.ppermute(array, ("seq", "batch"), pairs)
+
+
+class UnitSum:
+    def __init__(self, keep, send, kind):
+        self.core, orders = axis_orders(kind)
+        self.steps = list(zip(*orders))
+        self.parts = [keep]
+        self.top = keep.shape[0]
+        self.runs = None
+        self.rounds = self.plan(send)
+        self.outgoing = next(self.rounds)
+
+    def added(self, low, high):
+        total = self.parts[0][low:high]
+        for part in self.parts[1:]:
+            total = total + part[low:high]
+        return total
+
+    def plan(self, send):
+        sent = yield send
+        self.parts.append(swap(sent, self.core, self.core))
+        for step, (first, second) in enumerate(self.steps):
+            if step < halvings:
+                self.top //= 2
+                sent = yield self.added(self.top, 2 * self.top)
+                self.parts.append(swap(sent, first, second))
+            else:
+                own = yield self.added(0, self.top)
+                self.parts = [own, swap(own, first, second)]
+        full = self.added(0, self.top)
+        for first, second in self.steps[halvings - 1 : 0 : -1]:
+            full = yield full
+            full = jnp.concatenate([full, swap(full, first, second)])
+        full = yield full
+        rest = swap(full, *self.steps[0])
+        other = swap(full, self.core, self.core)
+        rest = yield rest
+        self.runs = (full, rest, other, swap(rest, self.core, self.core))
+        yield None
+
+    def launch(self, sent):
+        self.outgoing = self.rounds.send(sent)
+
+
+class Line:
+    def __init__(self):
+        self.last = ()
+
+    def advance(self, units, payload=()):
+        units = [unit for unit in units if unit.runs is None]
+        sends, payload, unused = lax.optimization_barrier(
+            ([unit.outgoing for unit in units], payload, self.last)
+        )
+        for unit, sent in zip(units, sends):
+            unit.launch(sent)
+        self.last = sends
+        return payload
+
+
+def aligned(first, rows):
+    return pl.ds(pl.multiple_of(first, 8), rows)
+
+
+class Layout:
+    def __init__(self, rows, columns, kind):
+        self.rows, self.columns, self.kind = rows, columns, kind
+        self.sections = {}
+
+    def add(self, key, array_rows, array_first, block_first, count, columns=slice(None)):
+        self.sections.setdefault(key, []).append(
+            (
+                lambda owner: (aligned(owner * array_rows + array_first, count), slice(None)),
+                lambda place: (aligned(place * self.rows + block_first, count), columns),
+            )
+        )
+
+    def half(self):
+        return ((half_blocks * self.rows, self.columns), f32)
+
+
+def tail_layout(model, width):
+    out_rows = 4 * width // (2 * half_blocks)
+    glu_rows = model // (2 * half_blocks)
+    layout = Layout(out_rows + glu_rows, model, tail_kind)
+    layout.add("out", out_rows, 0, 0, out_rows)
+    layout.add("glu", glu_rows, 0, out_rows, glu_rows)
+    return layout
+
+
+def in_layout(model, width):
+    rows = model // (2 * half_blocks)
+    layout = Layout(rows, 2 * width, in_kind)
+    layout.add("in", rows, 0, 0, rows)
+    return layout
+
+
+def last_layout(model, width):
+    rows = model // (2 * half_blocks)
+    pieces = rows // 8
+    wide = 2 * width
+    layout = Layout(8, pieces * wide + lane_count, last_kind)
+    for piece in range(pieces):
+        layout.add("in", rows, 8 * piece, 0, 8, slice(piece * wide, (piece + 1) * wide))
+    layout.add("small", 8, 0, 0, 8, slice(pieces * wide, pieces * wide + lane_count))
+    return layout
+
+
+class Emit:
+    def __init__(self, layout, keep_ref, send_ref):
+        self.sections = layout.sections
+        self.halves = (keep_ref, send_ref)
+        self.bases = half_bases(layout.kind)
+
+    def put(self, key, array_ref):
+        def one(place, carry):
+            for half in (1, 0):
+                owner = lax.bitwise_xor(self.bases[half], place)
+                for array_at, block_at in self.sections[key]:
+                    self.halves[half][block_at(place)] = array_ref[array_at(owner)]
+            return carry
+
+        lax.fori_loop(0, half_blocks, one, 0)
+
+
+run_places = ((0, 0), (0, half_blocks // 2), (1, 0), (1, half_blocks // 2))
+
+
+def place_kernel(layouts, goals, *refs):
+    outs = refs[len(refs) - 1 - len(goals) : -1]
+    semaphores = refs[-1]
+    targets = []
+    for out, writes in zip(outs, goals):
+        targets.append([out if layer is None else out.at[layer] for unused, unused_too, layer in writes])
+    for unit, layout in enumerate(layouts):
+        bases = half_bases(layout.kind)
+        for run, (half, first) in zip(refs[4 * unit : 4 * unit + 4], run_places):
+
+            def one(place, carry, run=run, half=half, first=first, unit=unit, layout=layout):
+                owner = lax.bitwise_xor(bases[half], first + place)
+                for index, writes in enumerate(goals):
+                    for target, (source, key, unused) in zip(targets[index], writes):
+                        if source != unit:
+                            continue
+                        for array_at, block_at in layout.sections[key]:
+                            pltpu.make_async_copy(
+                                run.at[block_at(place)],
+                                target.at[array_at(owner)],
+                                semaphores.at[index],
+                            ).start()
+                return carry
+
+            lax.fori_loop(0, half_blocks // 2, one, 0)
+    for index, group in enumerate(targets):
+        for target in group:
+            pltpu.make_async_copy(target, target, semaphores.at[index]).wait()
+
+
+def place_units(name, units, goals, sums):
+    operands = []
+    aliases = {}
+    for unit, unused in units:
+        operands.extend(("run", run) for run in unit.runs)
+    for index, (key, unused, unused_too) in enumerate(goals):
+        if key in sums:
+            aliases[len(operands)] = index
+            operands.append(("before", (sums[key], None)))
+    outs = call(
+        functools.partial(
+            place_kernel, [layout for unused, layout in units], [writes for *unused, writes in goals]
+        ),
+        name,
+        operands,
+        tuple((shape, f32) for unused, shape, unused_too in goals),
+        (pltpu.SemaphoreType.DMA((len(goals),)),),
+        written=range(len(goals)),
+        aliases=aliases,
+        plain=True,
+    )
+    for (key, unused, unused_too), out in zip(goals, outs):
+        sums[key] = out
 
 
 class Fetch:
@@ -693,7 +952,7 @@
         return self.target
 
 
-def call(body, name, operands, outs, scratch):
+def call(body, name, operands, outs, scratch, written=(), aliases=None, plain=False, micros=4, final=()):
     scalars = {"place", "docs"}
     arrays = []
     specs = []
@@ -701,7 +960,9 @@
     for position, (key, operand) in enumerate(operands):
         space = pltpu.SMEM if key in scalars else pltpu.VMEM
         if isinstance(operand, tuple):
-            operand, layers[position] = operand
+            operand, layer = operand
+            if layer is not None:
+                layers[position] = layer
             space = pl.ANY
         specs.append(pl.BlockSpec(memory_space=space))
         arrays.append(operand)
@@ -710,6 +971,9 @@
     ]
 
     def kernel(*refs):
+        if plain:
+            body(*refs)
+            return
         given = list(refs[: len(arrays)])
         rest = refs[len(arrays) : len(refs) - len(fetched) - 1]
         targets = refs[len(refs) - len(fetched) - 1 : -1]
@@ -721,11 +985,25 @@
         kernel,
         name=name,
         in_specs=specs,
-        out_specs=[pl.BlockSpec(memory_space=pltpu.VMEM)] * len(outs),
-        out_shape=[jax.ShapeDtypeStruct(shape, kind) for shape, kind in outs],
-        scratch_shapes=[pltpu.VMEM(shape, kind) for shape, kind in scratch]
+        out_specs=[
+            pl.BlockSpec(memory_space=pl.ANY if place in written else pltpu.VMEM)
+            for place in range(len(outs))
+        ],
+        out_shape=[
+            jax.ShapeDtypeStruct(shape, kind)
+            if place in written or place in final
+            else pltpu.VMEM(shape, kind)
+            for place, (shape, kind) in enumerate(outs)
+        ],
+        scratch_shapes=[
+            entry if not isinstance(entry, tuple) else pltpu.VMEM(*entry) for entry in scratch
+        ]
         + fetched
-        + [pltpu.SemaphoreType.DMA((max(1, len(fetched)),))],
+        + ([] if plain else [pltpu.SemaphoreType.DMA((max(1, len(fetched)),))]),
+        input_output_aliases=aliases or {},
+        cost_estimate=pl.CostEstimate(
+            flops=micros * 1_000_000_000, bytes_accessed=micros * 3_600_000, transcendentals=0
+        ),
         compiler_params=pltpu.CompilerParams(vmem_limit_bytes=vmem_bytes),
     )(*arrays)
 
@@ -815,8 +1093,16 @@
         values, scaled = next_values, next_scaled
     layer = layer_count - 1
     gathered = gather(totals)
+
+    whole = {"out": (layer_count, 4 * width, model), "glu": (layer_count, model, model)}
+    whole["in"] = (layer_count, model, 2 * width)
+    sums = {}
+    tail_part = tail_layout(model, width)
+    in_part = in_layout(model, width)
+    last_part = last_layout(model, width)
+    line = Line()
     (
-        output, grad, states, enter, d_mixed, d_states, glu_grad, out_grad, skip_grad, ends, totals,
+        output, grad, states, enter, d_mixed, d_states, keep, send, skip_grad, ends, totals,
     ) = call(
         functools.partial(turn_kernel, layer, length),
         "turn",
@@ -835,24 +1121,33 @@
         ),
         (
             (inputs.shape, bf16), tokens, wide_out, ends_out, tokens, wide_out,
-            glu_out, out_out, vector, ends_out, totals_out,
+            tail_part.half(), tail_part.half(), vector, ends_out, totals_out,
         ),
         (
             ((count, 4 * width), bf16), tokens, tokens_low, tokens, tokens_low, tokens_low, tokens,
-            tokens_low,
+            tokens_low, glu_out, out_out,
         ),
-    )
-    glu_grads, out_grads, skip_grads = [glu_grad], [out_grad], [skip_grad]
-    in_grads, gain_grads, rate_grads = [], [], []
+        final=(0,),
+        micros=10,
+    )
+    units = [UnitSum(keep, send, tail_kind)]
+    tail_units = [units[0]]
+    in_units = []
+    skip_grads = [skip_grad]
+    gain_grads, rate_grads = [], []
     back_scratch = (
         drive_out, drive_out, ((count, 2 * width), bf16), bar_out, tokens,
     )
     rate_out = ((4, width), f32)
+    small_out = ((8 * 2 * half_blocks, lane_count), f32)
     for layer in reversed(range(1, layer_count)):
+        if layer == layer_count - 1:
+            totals = line.advance(units, totals)
         gathered = gather(totals)
+        gathered = line.advance(units, gathered)
         low_states, low, low_enter, mixed, act, gate, low_values, low_scaled = kept[layer - 1]
         (
-            in_grad, gain_grad, rate_grad, grad, d_mixed, d_states, glu_grad, out_grad, skip_grad, ends,
+            keep, send, in_keep, in_send, gain_grad, rate_grad, grad, d_mixed, d_states, skip_grad, ends,
             totals,
         ) = call(
             functools.partial(back_middle_kernel, layer, length),
@@ -881,20 +1176,25 @@
                 ("low", low),
             ),
             (
-                in_out, vector, rate_out, tokens, tokens, wide_out, glu_out, out_out, vector, ends_out,
-                totals_out,
+                tail_part.half(), tail_part.half(), in_part.half(), in_part.half(), vector, rate_out,
+                tokens, tokens, wide_out, vector, ends_out, totals_out,
             ),
-            back_scratch + (tokens_low, tokens_low),
+            back_scratch + (tokens_low, tokens_low, in_out, glu_out, out_out),
+            micros=14,
         )
-        in_grads.append(in_grad)
-        gain_grads.append(gain_grad)
-        rate_grads.append(rate_grad)
-        glu_grads.append(glu_grad)
-        out_grads.append(out_grad)
-        skip_grads.append(skip_grad)
+        fresh = [UnitSum(keep, send, tail_kind), UnitSum(in_keep, in_send, in_kind)]
+        line.advance(fresh)
+        tail_units.append(fresh[0])
+        in_units.append(fresh[1])
+        gain_grads.insert(0, gain_grad)
+        rate_grads.insert(0, rate_grad)
+        skip_grads.insert(0, skip_grad)
         states, enter, values, scaled = low_states, low_enter, low_values, low_scaled
+        totals = line.advance(units, totals)
+        units = fresh + units
     gathered = gather(totals)
-    in_grad, gain_grad, rate_grad, input_grad = call(
+    gathered = line.advance(units, gathered)
+    keep, send, input_grad = call(
         functools.partial(back_last_kernel, length),
         "back_last",
         (
@@ -912,42 +1212,71 @@
             ("values", values),
             ("d_mixed", d_mixed),
             ("grad", grad),
+            *(("skip_grad", term) for term in skip_grads),
+            *(("gain_grad", term) for term in gain_grads),
+            *(("rate_grad", term) for term in rate_grads),
         ),
-        (in_out, vector, rate_out, (inputs.shape, bf16)),
-        back_scratch + (tokens_low,),
-    )
-    in_grads.append(in_grad)
-    gain_grads.append(gain_grad)
-    rate_grads.append(rate_grad)
-
-    def stack(terms):
-        return jnp.stack(terms[::-1])
-
-    in_sum, out_sum, glu_sum, rate_sum, gain_sum, skip_sum = lax.psum(
-        (
-            stack(in_grads),
-            stack(out_grads),
-            stack(glu_grads),
-            stack(rate_grads),
-            stack(gain_grads),
-            stack(skip_grads),
+        (last_part.half(), last_part.half(), (inputs.shape, bf16)),
+        back_scratch
+        + (
+            tokens_low, in_out, vector, rate_out, small_out,
         ),
-        ("seq", "batch"),
-    )
+        final=(2,),
+        micros=10,
+    )
+    last_unit = UnitSum(keep, send, last_kind)
+    line.advance([last_unit])
+    named = {"a": tail_units[0], "b": tail_units[-1], "c": last_unit, "d": (in_units or [last_unit])[-1]}
+    for name in round_order:
+        line.advance([named[name]])
+    for unit in tail_units + in_units + [last_unit]:
+        while unit.runs is None:
+            line.advance([unit])
+    for index, unit in enumerate(tail_units):
+        layer = layer_count - 1 - index
+        place_units(
+            "place_tail",
+            [(unit, tail_part)],
+            [("out", whole["out"], [(0, "out", layer)]), ("glu", whole["glu"], [(0, "glu", layer)])],
+            sums,
+        )
+    ends = [(unit, in_part) for unit in in_units] + [(last_unit, last_part)]
+    place_units(
+        "place_last",
+        ends,
+        [
+            (
+                "in",
+                whole["in"],
+                [(index, "in", layer_count - 1 - index) for index in range(layer_count)],
+            ),
+            ("small", small_out[0], [(len(ends) - 1, "small", None)]),
+        ],
+        sums,
+    )
+    small = sums["small"]
+
+    def taken(first, shape):
+        rows = math.prod(shape) // lane_count
+        return small[first : first + rows].reshape(shape), first + rows
+
+    gain_sum, row = taken(0, (layer_count, model))
+    skip_sum, row = taken(row, (layer_count, model))
+    rate_sum, row = taken(row, (layer_count, 4, width))
     decay_grad, frequency_grad, step_grad = rates_back(
         tuple(rate_sum[:, member] for member in range(4))
     )
     return (
         output,
         input_grad,
-        gain_sum[:, 0],
+        gain_sum,
         decay_grad,
         frequency_grad,
         step_grad,
-        in_sum,
-        skip_sum[:, 0],
-        out_sum,
-        glu_sum,
+        sums["in"],
+        skip_sum,
+        sums["out"],
+        sums["glu"],
     )
 
 

time: 351 us -> 214 us (0.61)
  waiting for transfers between devices: 181 us -> 88.6 us
  blocking collectives: 83.7 us -> 40.2 us
  starting transfers between devices: 0.04 us -> 34.3 us
  between operations: 14.2 us -> 1.23 us
  Pallas kernels: 48.7 us -> 36.9 us
  local copies, waits for them, and re-layouts: 11.6 us -> 6.24 us
  other arithmetic: 11.2 us -> 6.56 us
    psum x1 -> x0, waiting for transfers between devices: 181 us -> none  [on_device(): lax.psum((stack(in_grads), stack(out_grads), stack(glu_grads), stack(rate...]
    ppermute x0 -> x40, waiting for transfers between devices: none -> 88.6 us  [swap(): return lax.ppermute(array, ('seq', 'batch'), pairs)]
    psum x1 -> x0, blocking collectives: 41.2 us -> none  [on_device(): lax.psum((stack(in_grads), stack(out_grads), stack(glu_grads), stack(rate...]
    ppermute x0 -> x40, starting transfers between devices: none -> 34.3 us  [swap(): return lax.ppermute(array, ('seq', 'batch'), pairs)]
    pallas_call x5 -> x8, Pallas kernels: 48.7 us -> 36.9 us  [call(): pl.pallas_call(kernel, name=name, in_specs=specs, out_specs=[pl.BlockSpec...]
    another operation x4 -> x0, other arithmetic: 9.6 us -> none  [stack(): return jnp.stack(terms[::-1])]
    unnamed x33 -> x34, local copies, waits for them, and re-layouts: 11 us -> 5 us
    add x0 -> x20, other arithmetic: none -> 4.69 us  [added(): total = total + part[low:high]]
  transfers between devices with their start and end apart: 1 -> 40, of which waited for: 1 -> 18; matrix products, arithmetic and copies ran while one was open for 0% -> 3% of each run, Pallas kernels for 0% -> 6%
where the time goes in v1:
time: 214 us
  waiting for transfers between devices  88.6 us (41%)
  blocking collectives  40.2 us (19%)
  Pallas kernels  36.9 us (17%)
  starting transfers between devices  34.3 us (16%)
  other arithmetic  6.56 us (3%)
  local copies, waits for them, and re-layouts  6.24 us (3%)
    ppermute x40, waiting for transfers between devices, swap(): return lax.ppermute(array, ('seq', 'batch'), pairs)  88.6 us
    all_gather x4, blocking collectives, gather(): return lax.all_gather(totals, 'seq', axis=0, tiled=True)  40.2 us
    pallas_call x8, Pallas kernels, call(): pl.pallas_call(kernel, name=name, in_specs=specs, out_specs=[pl.BlockSpec...  36.9 us
    ppermute x40, starting transfers between devices, swap(): return lax.ppermute(array, ('seq', 'batch'), pairs)  34.3 us
    unnamed x34, local copies, waits for them, and re-layouts  5 us
    add x20, other arithmetic, added(): total = total + part[low:high]  4.69 us
  transfers between devices with their start and end apart: 40, of which 18 were waited for; matrix products, arithmetic and copies ran while one was open for 3% of the time, Pallas kernels for 6%

profile of v1, /device:TPU:0, one launch (start us, length us, event | category | flops | bytes accessed | tf_op | source)
XLA Modules:
  0.0 214.0 jit_solution(17733483022252584291)
XLA Ops:
  5.3 3.8 %first.1 = (f32[3,256,128]{2,1,0:T(8,128)S(1)}, f32[2,16,128]{2,1,0:T(8,128)S(1)}, bf16[256,512]{1,0:T(8,128)(2,1)S(1)}, bf16[256,512]{1,0:T(8,128)(2,1)S(1)}, f...) custom-call(s32[1]{0:T(128)} %bitcast.refs_0_, s32[2,8]{1,0:T(2,128)S(1)} %copy-done.9, ...), custom_call_target="tpu_custom_call" | custom-call | flops 4000000000 | bytes 14400000 | tf_op jit(solution)/shard_map/first/pallas_call | solution.py:984
  9.0 10.7 %all_gather.12.refs_1_ = f32[64,384]{1,0:T(8,128)S(1)} all-gather(f32[8,384]{1,0:T(8,128)S(1)} %get-tuple-element.99), channel_id=1, replica_groups=mesh['seq'=8,'batch'=4] {'seq'}, dimensions={0}, use_global_device_ids=true | all-gather | bytes 110592 | tf_op jit(solution)/shard_map/all_gather | solution.py:1033
  19.8 4.8 %middle.1 = (f32[256,1536]{1,0:T(8,128)S(1)}, bf16[256,1536]{1,0:T(8,128)(2,1)S(1)}, f32[8,1536]{1,0:T(8,128)S(1)}, f32[256,512]{1,0:T(8,128)S(1)}, bf16[256,512...) custom-call(s32[1]{0:T(128)} %bitcast.refs_0_, ...), custom_call_target="tpu_custom_call" | custom-call | flops 4000000000 | bytes 14400000 | tf_op jit(solution)/shard_map/middle/pallas_call | solution.py:984
  25.8 9.2 %all_gather.13.refs_1_ = f32[64,384]{1,0:T(8,128)S(1)} all-gather(f32[8,384]{1,0:T(8,128)S(1)} %get-tuple-element.106), channel_id=1, replica_groups=mesh['seq'=8,'batch'=4] {'seq'}, dimensions={0}, use_global_device_ids=true | all-gather | bytes 110592 | tf_op jit(solution)/shard_map/all_gather | solution.py:1033
  35.0 6.4 %turn.1 = (bf16[2,128,512]{2,1,0:T(8,128)(2,1)}, f32[256,512]{1,0:T(8,128)S(1)}, f32[256,1536]{1,0:T(8,128)S(1)}, f32[8,1536]{1,0:T(8,128)S(1)}, f32[256,512]{1,...) custom-call(s32[1]{0:T(128)} %bitcast.refs_0_, ...), custom_call_target="tpu_custom_call" | custom-call | flops 10000000000 | bytes 36000000 | tf_op jit(solution)/shard_map/turn/pallas_call | solution.py:984
  41.7 8.2 %all_gather.14.refs_1_ = f32[64,384]{1,0:T(8,128)S(1)} all-gather(f32[8,384]{1,0:T(8,128)S(1)} %get-tuple-element.116), channel_id=1, replica_groups=mesh['seq'=8,'batch'=4] {'seq'}, dimensions={0}, use_global_device_ids=true | all-gather | bytes 110592 | tf_op jit(solution)/shard_map/all_gather | solution.py:1033
  51.8 8.8 %back_middle.1 = (f32[1024,512]{1,0:T(8,128)S(1)}, f32[1024,512]{1,0:T(8,128)S(1)}, f32[256,768]{1,0:T(8,128)S(1)}, f32[256,768]{1,0:T(8,128)S(1)}, f32[1,512]{1...) custom-call(s32[1]{0:T(128)} %bitcast.refs_0_, ...), custom_call_target="tpu_custom_call" | custom-call | flops 14000000000 | bytes 50400000 | tf_op jit(solution)/shard_map/back_middle/pallas_call | solution.py:984
  61.1 4.1 %collective-permute-done.3 = f32[512,512]{1,0:T(8,128)} collective-permute-done((f32[512,512]{1,0:T(8,128)S(1)}, f32[512,512]{1,0:T(8,128)}, u32[]{:S(2)}, u32[]{:S(2)}) %collective-permute-start.3) | collective-permute-done | bytes 1048608 | tf_op jit(solution)/shard_map/ppermute | solution.py:758
  68.0 12.0 %all_gather.15.refs_1_ = f32[64,384]{1,0:T(8,128)S(1)} all-gather(f32[8,384]{1,0:T(8,128)S(1)} %get-tuple-element.137), channel_id=1, replica_groups=mesh['seq'=8,'batch'=4] {'seq'}, dimensions={0}, use_global_device_ids=true | all-gather | bytes 110592 | tf_op jit(solution)/shard_map/all_gather | solution.py:1033
  81.5 6.3 %back_last.1 = (f32[64,3200]{1,0:T(8,128)S(1)}, f32[64,3200]{1,0:T(8,128)S(1)}, bf16[2,128,512]{2,1,0:T(8,128)(2,1)}) custom-call(s32[1]{0:T(128)} %bitcast.refs_0_, f32[64,384]{1,0:T(8,128)S(1)} %all_gather.15.refs_1_, f32[3,256,128]{2,1,0:T(8,128)S(1)} %get-tuple-element.100.refs_2_, f32[2,16,128]{2,1,0:T(8,128)S(1)} %get-tuple-element.101.refs_3_, ...), custom_call_target="tpu_custom_call" | custom-call | flops 10000000000 | bytes 36000000 | tf_op jit(solution)/shard_map/back_last/pallas_call | solution.py:984
  91.8 4.8 %collective-permute-done.7 = f32[128,512]{1,0:T(8,128)S(1)} collective-permute-done((f32[128,512]{1,0:T(8,128)S(1)}, f32[128,512]{1,0:T(8,128)S(1)}, u32[]{:S(2)}, u32[]{:S(2)}) %collective-permute-start.7) | collective-permute-done | bytes 262176 | tf_op jit(solution)/shard_map/ppermute | solution.py:758
  97.8 11.0 %collective-permute-done.8 = f32[512,512]{1,0:T(8,128)S(1)} collective-permute-done((f32[512,512]{1,0:T(8,128)S(1)}, f32[512,512]{1,0:T(8,128)S(1)}, u32[]{:S(2)}, u32[]{:S(2)}) %collective-permute-start.8) | collective-permute-done | bytes 1048608 | tf_op jit(solution)/shard_map/ppermute | solution.py:758
  111.1 2.6 %collective-permute-start.11 = (f32[128,512]{1,0:T(8,128)S(1)}, f32[128,512]{1,0:T(8,128)S(1)}, u32[]{:S(2)}, u32[]{:S(2)}) collective-permute-start(f32[128,512]{1,0:T(8,128)S(1)} %fusion.1), channel_id=1, source_target_pairs={{0,2},{1,3},{2,0},{3,1},{4,6},{5,7},{6,4},{7,5},{8,10},{9,11},{10,... | collective-permute-start | bytes 786440 | tf_op jit(solution)/shard_map/ppermute | solution.py:758
  114.2 2.7 %collective-permute-done.9 = f32[64,768]{1,0:T(8,128)S(1)} collective-permute-done((f32[64,768]{1,0:T(8,128)S(1)}, f32[64,768]{1,0:T(8,128)S(1)}, u32[]{:S(2)}, u32[]{:S(2)}) %collective-permute-start.9) | collective-permute-done | bytes 196640 | tf_op jit(solution)/shard_map/ppermute | solution.py:758
  116.9 7.2 %collective-permute-done.11 = f32[128,512]{1,0:T(8,128)S(1)} collective-permute-done((f32[128,512]{1,0:T(8,128)S(1)}, f32[128,512]{1,0:T(8,128)S(1)}, u32[]{:S(2)}, u32[]{:S(2)}) %collective-permute-start.11) | collective-permute-done | bytes 262176 | tf_op jit(solution)/shard_map/ppermute | solution.py:758
  124.4 2.0 collective-permute-start.14
  127.2 2.9 %collective-permute-done.13 = f32[32,768]{1,0:T(8,128)S(1)} collective-permute-done((f32[32,768]{1,0:T(8,128)S(1)}, f32[32,768]{1,0:T(8,128)S(1)}, u32[]{:S(2)}, u32[]{:S(2)}) %collective-permute-start.13) | collective-permute-done | bytes 98336 | tf_op jit(solution)/shard_map/ppermute | solution.py:758
  130.1 2.1 collective-permute-done.15
  132.3 8.1 %collective-permute-done.16 = f32[128,512]{1,0:T(8,128)S(1)} collective-permute-done((f32[128,512]{1,0:T(8,128)S(1)}, f32[128,512]{1,0:T(8,128)S(1)}, u32[]{:S(2)}, u32[]{:S(2)}) %collective-permute-start.16) | collective-permute-done | bytes 262176 | tf_op jit(solution)/shard_map/ppermute | solution.py:758
  143.3 5.4 %collective-permute-done.19 = f32[8,3200]{1,0:T(8,128)S(1)} collective-permute-done((f32[8,3200]{1,0:T(8,128)S(1)}, f32[8,3200]{1,0:T(8,128)S(1)}, u32[]{:S(2)}, u32[]{:S(2)}) %collective-permute-start.19) | collective-permute-done | bytes 102432 | tf_op jit(solution)/shard_map/ppermute | solution.py:758
  148.8 5.7 %collective-permute-done.20 = f32[128,512]{1,0:T(8,128)S(1)} collective-permute-done((f32[128,512]{1,0:T(8,128)S(1)}, f32[128,512]{1,0:T(8,128)S(1)}, u32[]{:S(2)}, u32[]{:S(2)}) %collective-permute-start.20) | collective-permute-done | bytes 262176 | tf_op jit(solution)/shard_map/ppermute | solution.py:758
  156.2 2.0 collective-permute-start.17
  158.2 9.0 %collective-permute-done.17 = f32[32,768]{1,0:T(8,128)S(1)} collective-permute-done((f32[32,768]{1,0:T(8,128)S(1)}, f32[32,768]{1,0:T(8,128)S(1)}, u32[]{:S(2)}, u32[]{:S(2)}) %collective-permute-start.17) | collective-permute-done | bytes 98336 | tf_op jit(solution)/shard_map/ppermute | solution.py:758
  168.9 2.0 collective-permute-start.26
  173.5 3.0 %collective-permute-done.27 = f32[256,512]{1,0:T(8,128)S(1)} collective-permute-done((f32[256,512]{1,0:T(8,128)S(1)}, f32[256,512]{1,0:T(8,128)S(1)}, u32[]{:S(2)}, u32[]{:S(2)}) %collective-permute-start.27) | collective-permute-done | bytes 524320 | tf_op jit(solution)/shard_map/ppermute | solution.py:758
  180.8 4.0 %collective-permute-done.30 = f32[16,3200]{1,0:T(8,128)S(1)} collective-permute-done((f32[16,3200]{1,0:T(8,128)S(1)}, f32[16,3200]{1,0:T(8,128)S(1)}, u32[]{:S(2)}, u32[]{:S(2)}) %collective-permute-start.30) | collective-permute-done | bytes 204832 | tf_op jit(solution)/shard_map/ppermute | solution.py:758
  186.3 2.6 %collective-permute-done.25 = f32[64,768]{1,0:T(8,128)S(1)} collective-permute-done((f32[64,768]{1,0:T(8,128)S(1)}, f32[64,768]{1,0:T(8,128)S(1)}, u32[]{:S(2)}, u32[]{:S(2)}) %collective-permute-start.25) | collective-permute-done | bytes 196640 | tf_op jit(solution)/shard_map/ppermute | solution.py:758
  190.5 4.6 %collective-permute-done.29.refs_1_ = f32[512,512]{1,0:T(8,128)S(1)} collective-permute-done((f32[512,512]{1,0:T(8,128)S(1)}, f32[512,512]{1,0:T(8,128)S(1)}, u32[]{:S(2)}, u32[]{:S(2)}) %collective-permute-start.29) | collective-permute-done | bytes 1048608 | tf_op jit(solution)/shard_map/ppermute | solution.py:758
  195.1 8.6 %collective-permute-done.28.refs_1_ = f32[128,768]{1,0:T(8,128)S(1)} collective-permute-done((f32[128,768]{1,0:T(8,128)S(1)}, f32[128,768]{1,0:T(8,128)S(1)}, u32[]{:S(2)}, u32[]{:S(2)}) %collective-permute-start.28) | collective-permute-done | bytes 393248 | tf_op jit(solution)/shard_map/ppermute | solution.py:758
  204.7 2.0 place_tail.2
  206.9 1.7 place_last.1
  210.6 3.2 %place_tail.3 = (f32[2,1536,512]{2,1,0:T(8,128)}, f32[2,512,512]{2,1,0:T(8,128)}) custom-call(f32[512,512]{1,0:T(8,128)S(1)} %pad_maximum_fusion.1.refs_0_, f32[512,512]{1,0:T(8,128)S(1)} %collective-permute-done.29.refs_1_, f32[512,512]{1,0:T(8,128)S(1)} %collective-permute-done.36.refs_2_, ...), custom_call_target="tpu_custom_call", output_to_operand_aliasing={{0}: (4, {}), {1}: (5, {})} | custom-call | flops 4000000000 | bytes 14400000 | tf_op jit(solution)/shard_map/place_tail/pallas_call | solution.py:984
  (133 shorter events, 41.2 us)
Async XLA Ops:
  41.3 8.7 %collective-permute-start = (f32[1024,512]{1,0:T(8,128)S(1)}, f32[1024,512]{1,0:T(8,128)S(1)}, u32[]{:S(2)}, u32[]{:S(2)}) collective-permute-start(f32[1024,512]{1,0:T(8,128)S(1)} %get-tuple-element.115), channel_id=1, source_target_pairs={{0,4},{1,5},{2,6},{3,7},{4,0},{5,1},{6,2},{7,3},{8,12},{9,13},{10,... | collective-permute-start | bytes 6291464 | tf_op jit(solution)/shard_map/ppermute | solution.py:758
  50.2 15.0 %collective-permute-start.3 = (f32[512,512]{1,0:T(8,128)S(1)}, f32[512,512]{1,0:T(8,128)}, u32[]{:S(2)}, u32[]{:S(2)}) collective-permute-start(f32[512,512]{1,0:T(8,128)S(1)} %slice_add_fusion.1), channel_id=1, source_target_pairs={{0,8},{1,9},{2,10},{3,11},{4,20},{5,21},{6,22},{7,23},{8,0},{9,1},... | collective-permute-start | bytes 3145736 | tf_op jit(solution)/shard_map/ppermute | solution.py:758
  60.5 20.7 %collective-permute-start.1 = (f32[1024,512]{1,0:T(8,128)S(1)}, f32[1024,512]{1,0:T(8,128)S(1)}, u32[]{:S(2)}, u32[]{:S(2)}) collective-permute-start(f32[1024,512]{1,0:T(8,128)S(1)} %get-tuple-element.132), channel_id=1, source_target_pairs={{0,4},{1,5},{2,6},{3,7},{4,0},{5,1},{6,2},{7,3},{8,12},{9,13},{10,... | collective-permute-start | bytes 6291464 | tf_op jit(solution)/shard_map/ppermute | solution.py:758
  60.7 7.3 %collective-permute-start.2 = (f32[256,768]{1,0:T(8,128)S(1)}, f32[256,768]{1,0:T(8,128)S(1)}, u32[]{:S(2)}, u32[]{:S(2)}) collective-permute-start(f32[256,768]{1,0:T(8,128)S(1)} %get-tuple-element.134), channel_id=1, source_target_pairs={{0,4},{1,5},{2,6},{3,7},{4,0},{5,1},{6,2},{7,3},{8,12},{9,13},{10,... | collective-permute-start | bytes 2359304 | tf_op jit(solution)/shard_map/ppermute | solution.py:758
  66.4 13.7 %collective-permute-start.4 = (f32[256,512]{1,0:T(8,128)S(1)}, f32[256,512]{1,0:T(8,128)S(1)}, u32[]{:S(2)}, u32[]{:S(2)}) collective-permute-start(f32[256,512]{1,0:T(8,128)S(1)} %slice_add_fusion.4), channel_id=1, source_target_pairs={{0,16},{1,17},{2,18},{3,19},{4,12},{5,13},{6,14},{7,15},{8,24},{9,... | collective-permute-start | bytes 1572872 | tf_op jit(solution)/shard_map/ppermute | solution.py:758
  87.8 9.9 %collective-permute-start.6 = (f32[64,3200]{1,0:T(8,128)S(1)}, f32[64,3200]{1,0:T(8,128)S(1)}, u32[]{:S(2)}, u32[]{:S(2)}) collective-permute-start(f32[64,3200]{1,0:T(8,128)S(1)} %get-tuple-element.155), channel_id=1, source_target_pairs={{0,4},{1,5},{2,6},{3,7},{4,0},{5,1},{6,2},{7,3},{8,12},{9,13},{10,... | collective-permute-start | bytes 2457608 | tf_op jit(solution)/shard_map/ppermute | solution.py:758
  88.2 8.4 %collective-permute-start.7 = (f32[128,512]{1,0:T(8,128)S(1)}, f32[128,512]{1,0:T(8,128)S(1)}, u32[]{:S(2)}, u32[]{:S(2)}) collective-permute-start(f32[128,512]{1,0:T(8,128)S(1)} %slice_add_fusion.17), channel_id=1, source_target_pairs={{0,1},{1,0},{2,3},{3,2},{4,5},{5,4},{6,7},{7,6},{8,9},{9,8},{10,11... | collective-permute-start | bytes 786440 | tf_op jit(solution)/shard_map/ppermute | solution.py:758
  89.8 7.9 %collective-permute-start.5 = (f32[128,768]{1,0:T(8,128)S(1)}, f32[128,768]{1,0:T(8,128)S(1)}, u32[]{:S(2)}, u32[]{:S(2)}) collective-permute-start(f32[128,768]{1,0:T(8,128)S(1)} %slice_add_fusion.7), channel_id=1, source_target_pairs={{0,8},{1,9},{2,10},{3,11},{4,20},{5,21},{6,22},{7,23},{8,0},{9,1},... | collective-permute-start | bytes 1179656 | tf_op jit(solution)/shard_map/ppermute | solution.py:758
  90.3 18.5 %collective-permute-start.8 = (f32[512,512]{1,0:T(8,128)S(1)}, f32[512,512]{1,0:T(8,128)S(1)}, u32[]{:S(2)}, u32[]{:S(2)}) collective-permute-start(f32[512,512]{1,0:T(8,128)S(1)} %slice_add_fusion), channel_id=1, source_target_pairs={{0,8},{1,9},{2,10},{3,11},{4,20},{5,21},{6,22},{7,23},{8,0},{9,1},... | collective-permute-start | bytes 3145736 | tf_op jit(solution)/shard_map/ppermute | solution.py:758
  109.0 7.9 %collective-permute-start.9 = (f32[64,768]{1,0:T(8,128)S(1)}, f32[64,768]{1,0:T(8,128)S(1)}, u32[]{:S(2)}, u32[]{:S(2)}) collective-permute-start(f32[64,768]{1,0:T(8,128)S(1)} %slice_add_fusion.22), channel_id=1, source_target_pairs={{0,16},{1,17},{2,18},{3,19},{4,12},{5,13},{6,14},{7,15},{8,24},{9,... | collective-permute-start | bytes 589832 | tf_op jit(solution)/shard_map/ppermute | solution.py:758
  109.6 14.6 %collective-permute-start.10 = (f32[32,3200]{1,0:T(8,128)S(1)}, f32[32,3200]{1,0:T(8,128)S(1)}, u32[]{:S(2)}, u32[]{:S(2)}) collective-permute-start(f32[32,3200]{1,0:T(8,128)S(1)} %slice_add_fusion.6), channel_id=1, source_target_pairs={{0,8},{1,9},{2,10},{3,11},{4,20},{5,21},{6,22},{7,23},{8,0},{9,1},... | collective-permute-start | bytes 1228808 | tf_op jit(solution)/shard_map/ppermute | solution.py:758
  111.1 13.1 %collective-permute-start.11 = (f32[128,512]{1,0:T(8,128)S(1)}, f32[128,512]{1,0:T(8,128)S(1)}, u32[]{:S(2)}, u32[]{:S(2)}) collective-permute-start(f32[128,512]{1,0:T(8,128)S(1)} %fusion.1), channel_id=1, source_target_pairs={{0,2},{1,3},{2,0},{3,1},{4,6},{5,7},{6,4},{7,5},{8,10},{9,11},{10,... | collective-permute-start | bytes 786440 | tf_op jit(solution)/shard_map/ppermute | solution.py:758
  113.7 10.6 %collective-permute-start.12 = (f32[256,512]{1,0:T(8,128)S(1)}, f32[256,512]{1,0:T(8,128)S(1)}, u32[]{:S(2)}, u32[]{:S(2)}) collective-permute-start(f32[256,512]{1,0:T(8,128)S(1)} %slice_add_fusion.2), channel_id=1, source_target_pairs={{0,16},{1,17},{2,18},{3,19},{4,12},{5,13},{6,14},{7,15},{8,24},{9,... | collective-permute-start | bytes 1572872 | tf_op jit(solution)/shard_map/ppermute | solution.py:758
  124.4 18.2 %collective-permute-start.14 = (f32[128,512]{1,0:T(8,128)S(1)}, f32[128,512]{1,0:T(8,128)S(1)}, u32[]{:S(2)}, u32[]{:S(2)}) collective-permute-start(f32[128,512]{1,0:T(8,128)S(1)} %add.165), channel_id=1, source_target_pairs={{0,1},{1,0},{2,3},{3,2},{4,5},{5,4},{6,7},{7,6},{8,9},{9,8},{10,11... | collective-permute-start | bytes 786440 | tf_op jit(solution)/shard_map/ppermute | solution.py:758
  127.0 13.4 %collective-permute-start.16 = (f32[128,512]{1,0:T(8,128)S(1)}, f32[128,512]{1,0:T(8,128)S(1)}, u32[]{:S(2)}, u32[]{:S(2)}) collective-permute-start(f32[128,512]{1,0:T(8,128)S(1)} %slice_add_fusion.11), channel_id=1, source_target_pairs={{0,1},{1,0},{2,3},{3,2},{4,5},{5,4},{6,7},{7,6},{8,9},{9,8},{10,11... | collective-permute-start | bytes 786440 | tf_op jit(solution)/shard_map/ppermute | solution.py:758
  140.5 14.0 %collective-permute-start.20 = (f32[128,512]{1,0:T(8,128)S(1)}, f32[128,512]{1,0:T(8,128)S(1)}, u32[]{:S(2)}, u32[]{:S(2)}) collective-permute-start(f32[128,512]{1,0:T(8,128)S(1)} %fusion), channel_id=1, source_target_pairs={{0,2},{1,3},{2,0},{3,1},{4,6},{5,7},{6,4},{7,5},{8,10},{9,11},{10,... | collective-permute-start | bytes 786440 | tf_op jit(solution)/shard_map/ppermute | solution.py:758
  141.8 7.0 %collective-permute-start.19 = (f32[8,3200]{1,0:T(8,128)S(1)}, f32[8,3200]{1,0:T(8,128)S(1)}, u32[]{:S(2)}, u32[]{:S(2)}) collective-permute-start(f32[8,3200]{1,0:T(8,128)S(1)} %slice_add_fusion.27), channel_id=1, source_target_pairs={{0,1},{1,0},{2,3},{3,2},{4,5},{5,4},{6,7},{7,6},{8,9},{9,8},{10,11... | collective-permute-start | bytes 307208 | tf_op jit(solution)/shard_map/ppermute | solution.py:758
  142.7 11.9 %collective-permute-start.18 = (f32[256,512]{1,0:T(8,128)S(1)}, f32[256,512]{1,0:T(8,128)S(1)}, u32[]{:S(2)}, u32[]{:S(2)}) collective-permute-start(f32[256,512]{1,0:T(8,128)S(1)} %pad_maximum_fusion.2), channel_id=1, source_target_pairs={{0,16},{1,17},{2,18},{3,19},{4,12},{5,13},{6,14},{7,15},{8,24},{9,... | collective-permute-start | bytes 1572872 | tf_op jit(solution)/shard_map/ppermute | solution.py:758
  154.5 12.8 %collective-permute-start.24 = (f32[128,512]{1,0:T(8,128)S(1)}, f32[128,512]{1,0:T(8,128)S(1)}, u32[]{:S(2)}, u32[]{:S(2)}) collective-permute-start(f32[128,512]{1,0:T(8,128)S(1)} %add.182), channel_id=1, source_target_pairs={{0,1},{1,0},{2,3},{3,2},{4,5},{5,4},{6,7},{7,6},{8,9},{9,8},{10,11... | collective-permute-start | bytes 786440 | tf_op jit(solution)/shard_map/ppermute | solution.py:758
  154.7 22.0 %collective-permute-start.22 = (f32[512,512]{1,0:T(8,128)S(1)}, f32[512,512]{1,0:T(8,128)S(1)}, u32[]{:S(2)}, u32[]{:S(2)}) collective-permute-start(f32[512,512]{1,0:T(8,128)S(1)} %pad_maximum_fusion.refs_0_), channel_id=1, source_target_pairs={{0,8},{1,9},{2,10},{3,11},{4,20},{5,21},{6,22},{7,23},{8,0},{9,1},... | collective-permute-start | bytes 3145736 | tf_op jit(solution)/shard_map/ppermute | solution.py:758
  155.3 11.9 %collective-permute-start.23 = (f32[8,3200]{1,0:T(8,128)S(1)}, f32[8,3200]{1,0:T(8,128)S(1)}, u32[]{:S(2)}, u32[]{:S(2)}) collective-permute-start(f32[8,3200]{1,0:T(8,128)S(1)} %fusion.2), channel_id=1, source_target_pairs={{0,2},{1,3},{2,0},{3,1},{4,6},{5,7},{6,4},{7,5},{8,10},{9,11},{10,... | collective-permute-start | bytes 307208 | tf_op jit(solution)/shard_map/ppermute | solution.py:758
  156.2 11.0 %collective-permute-start.17 = (f32[32,768]{1,0:T(8,128)S(1)}, f32[32,768]{1,0:T(8,128)S(1)}, u32[]{:S(2)}, u32[]{:S(2)}) collective-permute-start(f32[32,768]{1,0:T(8,128)S(1)} %fusion.3), channel_id=1, source_target_pairs={{0,2},{1,3},{2,0},{3,1},{4,6},{5,7},{6,4},{7,5},{8,10},{9,11},{10,... | collective-permute-start | bytes 294920 | tf_op jit(solution)/shard_map/ppermute | solution.py:758
  167.3 9.2 %collective-permute-start.27 = (f32[256,512]{1,0:T(8,128)S(1)}, f32[256,512]{1,0:T(8,128)S(1)}, u32[]{:S(2)}, u32[]{:S(2)}) collective-permute-start(f32[256,512]{1,0:T(8,128)S(1)} %pad_maximum_fusion.3), channel_id=1, source_target_pairs={{0,16},{1,17},{2,18},{3,19},{4,12},{5,13},{6,14},{7,15},{8,24},{9,... | collective-permute-start | bytes 1572872 | tf_op jit(solution)/shard_map/ppermute | solution.py:758
  176.7 8.1 %collective-permute-start.30 = (f32[16,3200]{1,0:T(8,128)S(1)}, f32[16,3200]{1,0:T(8,128)S(1)}, u32[]{:S(2)}, u32[]{:S(2)}) collective-permute-start(f32[16,3200]{1,0:T(8,128)S(1)} %pad_maximum_fusion.6), channel_id=1, source_target_pairs={{0,16},{1,17},{2,18},{3,19},{4,12},{5,13},{6,14},{7,15},{8,24},{9,... | collective-permute-start | bytes 614408 | tf_op jit(solution)/shard_map/ppermute | solution.py:758
  178.2 16.9 %collective-permute-start.29 = (f32[512,512]{1,0:T(8,128)S(1)}, f32[512,512]{1,0:T(8,128)S(1)}, u32[]{:S(2)}, u32[]{:S(2)}) collective-permute-start(f32[512,512]{1,0:T(8,128)S(1)} %pad_maximum_fusion.1.refs_0_), channel_id=1, source_target_pairs={{0,8},{1,9},{2,10},{3,11},{4,20},{5,21},{6,22},{7,23},{8,0},{9,1},... | collective-permute-start | bytes 3145736 | tf_op jit(solution)/shard_map/ppermute | solution.py:758
  178.7 25.5 %collective-permute-start.38 = (f32[512,512]{1,0:T(8,128)S(1)}, f32[512,512]{1,0:T(8,128)S(1)}, u32[]{:S(2)}, u32[]{:S(2)}) collective-permute-start(f32[512,512]{1,0:T(8,128)S(1)} %pad_maximum_fusion.refs_0_), channel_id=1, source_target_pairs={{0,4},{1,5},{2,6},{3,7},{4,0},{5,1},{6,2},{7,3},{8,12},{9,13},{10,... | collective-permute-start | bytes 3145736 | tf_op jit(solution)/shard_map/ppermute | solution.py:758
  178.7 25.5 %collective-permute-start.39 = (f32[512,512]{1,0:T(8,128)S(1)}, f32[512,512]{1,0:T(8,128)S(1)}, u32[]{:S(2)}, u32[]{:S(2)}) collective-permute-start(f32[512,512]{1,0:T(8,128)S(1)} %collective-permute-done.22.refs_1_), channel_id=1, source_target_pairs={{0,4},{1,5},{2,6},{3,7},{4,0},{5,1},{6,2},{7,3},{8,12},{9,13},{10,... | collective-permute-start | bytes 3145736 | tf_op jit(solution)/shard_map/ppermute | solution.py:758
  179.2 9.7 %collective-permute-start.25 = (f32[64,768]{1,0:T(8,128)S(1)}, f32[64,768]{1,0:T(8,128)S(1)}, u32[]{:S(2)}, u32[]{:S(2)}) collective-permute-start(f32[64,768]{1,0:T(8,128)S(1)} %pad_maximum_fusion.7), channel_id=1, source_target_pairs={{0,16},{1,17},{2,18},{3,19},{4,12},{5,13},{6,14},{7,15},{8,24},{9,... | collective-permute-start | bytes 589832 | tf_op jit(solution)/shard_map/ppermute | solution.py:758
  184.8 18.9 %collective-permute-start.33 = (f32[32,3200]{1,0:T(8,128)S(1)}, f32[32,3200]{1,0:T(8,128)S(1)}, u32[]{:S(2)}, u32[]{:S(2)}) collective-permute-start(f32[32,3200]{1,0:T(8,128)S(1)} %pad_maximum_fusion.4.refs_4_), channel_id=1, source_target_pairs={{0,8},{1,9},{2,10},{3,11},{4,20},{5,21},{6,22},{7,23},{8,0},{9,1},... | collective-permute-start | bytes 1228808 | tf_op jit(solution)/shard_map/ppermute | solution.py:758
  189.0 14.7 %collective-permute-start.28 = (f32[128,768]{1,0:T(8,128)S(1)}, f32[128,768]{1,0:T(8,128)S(1)}, u32[]{:S(2)}, u32[]{:S(2)}) collective-permute-start(f32[128,768]{1,0:T(8,128)S(1)} %pad_maximum_fusion.5.refs_0_), channel_id=1, source_target_pairs={{0,8},{1,9},{2,10},{3,11},{4,20},{5,21},{6,22},{7,23},{8,0},{9,1},... | collective-permute-start | bytes 1179656 | tf_op jit(solution)/shard_map/ppermute | solution.py:758
  195.1 11.8 %collective-permute-start.34 = (f32[32,3200]{1,0:T(8,128)S(1)}, f32[32,3200]{1,0:T(8,128)S(1)}, u32[]{:S(2)}, u32[]{:S(2)}) collective-permute-start(f32[32,3200]{1,0:T(8,128)S(1)} %pad_maximum_fusion.4.refs_4_), channel_id=1, source_target_pairs={{0,4},{1,5},{2,6},{3,7},{4,0},{5,1},{6,2},{7,3},{8,12},{9,13},{10,... | collective-permute-start | bytes 1228808 | tf_op jit(solution)/shard_map/ppermute | solution.py:758
  204.2 6.4 %collective-permute-start.36 = (f32[512,512]{1,0:T(8,128)S(1)}, f32[512,512]{1,0:T(8,128)S(1)}, u32[]{:S(2)}, u32[]{:S(2)}) collective-permute-start(f32[512,512]{1,0:T(8,128)S(1)} %pad_maximum_fusion.1.refs_0_), channel_id=1, source_target_pairs={{0,4},{1,5},{2,6},{3,7},{4,0},{5,1},{6,2},{7,3},{8,12},{9,13},{10,... | collective-permute-start | bytes 3145736 | tf_op jit(solution)/shard_map/ppermute | solution.py:758
  (25 other events, 148.4 us)

commit v2 on v1

--- a/solution.py
+++ b/solution.py
@@ -82,7 +82,7 @@
         body(pl.ds(pl.multiple_of(index * block_rows, block_rows), block_rows))
         return carry
 
-    lax.fori_loop(0, count // block_rows, one, 0)
+    lax.fori_loop(0, count // block_rows, one, 0, unroll=min(8, count // block_rows))
 
 
 def normalize(values):
@@ -603,12 +603,16 @@
 def turn_kernel(
     layer, length, place_ref, gathered_ref, flags_ref, blocks_ref, tables_ref, skip_ref,
     drive_ref, ends_ref, values_ref, scaled_ref, out_ref, glu_ref, cotangent_ref,
-    output_ref, grad_ref, states_ref, enter_ref, d_mixed_ref, d_states_ref,
-    keep_ref, send_ref, skip_grad_ref, back_ends_ref, back_totals_ref,
-    low_ref, mixed_ref, act_ref, gate_ref, result_ref, logits_ref, work_ref, mixed_low_ref,
-    glu_grad_ref, out_grad_ref,
+    *rest,
 ):
-    emit = Emit(tail_layout(values_ref.shape[1], tables_ref.shape[1]), keep_ref, send_ref)
+    unit_refs, rest = rest[: 2 * len(turn_units)], rest[2 * len(turn_units) :]
+    (
+        output_ref, grad_ref, states_ref, enter_ref, d_mixed_ref, d_states_ref,
+        skip_grad_ref, back_ends_ref, back_totals_ref,
+        low_ref, mixed_ref, act_ref, gate_ref, result_ref, logits_ref, work_ref, mixed_low_ref,
+        glu_grad_ref, out_grad_ref,
+    ) = rest
+    emit = Emit(turn_units, unit_refs, values_ref.shape[1], tables_ref.shape[1])
     settled_states(
         place_ref[0], gathered_ref, flags_ref, blocks_ref, tables_ref, layer, drive_ref, ends_ref, length,
         states_ref, low_ref, enter_ref,
@@ -642,15 +646,16 @@
     layer, length, place_ref, gathered_ref, flags_ref, blocks_ref, tables_ref, gain_ref, skip_ref, in_ref,
     d_states_ref, ends_ref, states_ref, enter_ref, scaled_ref, values_ref, d_mixed_ref, grad_ref,
     out_ref, glu_ref, below_mixed_ref, below_act_ref, below_gate_ref, below_scaled_ref, below_low_ref,
-    keep_ref, send_ref, in_keep_ref, in_send_ref, gain_grad_ref, rate_grad_ref, next_grad_ref,
-    below_d_mixed_ref,
-    below_d_states_ref, skip_grad_ref, below_ends_ref, below_totals_ref,
-    lam_ref, mu_ref, low_ref, bar_ref, work_ref, logits_ref, mixed_low_ref,
-    in_grad_ref, glu_grad_ref, out_grad_ref,
+    *rest,
 ):
-    model, width = values_ref.shape[1], tables_ref.shape[1]
-    emit = Emit(tail_layout(model, width), keep_ref, send_ref)
-    in_emit = Emit(in_layout(model, width), in_keep_ref, in_send_ref)
+    unit_refs, rest = rest[: 2 * len(middle_units)], rest[2 * len(middle_units) :]
+    (
+        gain_grad_ref, rate_grad_ref, next_grad_ref, below_d_mixed_ref,
+        below_d_states_ref, skip_grad_ref, below_ends_ref, below_totals_ref,
+        lam_ref, mu_ref, low_ref, bar_ref, work_ref, logits_ref, mixed_low_ref,
+        in_grad_ref, glu_grad_ref, out_grad_ref,
+    ) = rest
+    emit = Emit(middle_units, unit_refs, values_ref.shape[1], tables_ref.shape[1])
 
     def put_gradient(rows, gradient):
         next_grad_ref[rows, :] = gradient
@@ -659,7 +664,7 @@
         place_ref[0], layer, length, gathered_ref, flags_ref, blocks_ref, tables_ref, gain_ref, skip_ref,
         in_ref, d_states_ref, ends_ref, states_ref, enter_ref, scaled_ref, values_ref, d_mixed_ref,
         grad_ref, lam_ref, mu_ref, low_ref, bar_ref, work_ref,
-        in_grad_ref, gain_grad_ref, rate_grad_ref, put_gradient, in_emit,
+        in_grad_ref, gain_grad_ref, rate_grad_ref, put_gradient, emit,
     )
     back_tail(
         layer - 1, flags_ref, tables_ref, next_grad_ref, below_mixed_ref, below_act_ref, below_gate_ref,
@@ -679,12 +684,13 @@
     rest = rest[layer_count:]
     gain_grads = rest[: layer_count - 1]
     rate_grads = rest[layer_count - 1 : 2 * layer_count - 2]
+    unit_refs = rest[2 * layer_count - 2 : 2 * layer_count]
     (
-        keep_ref, send_ref, input_grad_ref,
+        input_grad_ref,
         lam_ref, mu_ref, low_ref, bar_ref, work_ref, result_ref,
         in_grad_ref, gain_grad_ref, rate_grad_ref, small_ref,
-    ) = rest[2 * layer_count - 2 :]
-    emit = Emit(last_layout(values_ref.shape[1], tables_ref.shape[1]), keep_ref, send_ref)
+    ) = rest[2 * layer_count :]
+    emit = Emit(last_units, unit_refs, values_ref.shape[1], tables_ref.shape[1])
     def put_gradient(rows, gradient):
         result_ref[rows, :] = gradient.astype(bf16)
 
@@ -711,10 +717,14 @@
 
 halvings = 3
 half_blocks = 1 << halvings
-tail_kind = "plane"
-in_kind = "plane"
-last_kind = "plane"
-round_order = "bacdbacdbcadbcadbcadbcdacbdcdc"
+turn_units = (("a", ("out", "glu"), "plane"),)
+middle_units = (("b", ("out", "glu"), "plane"), ("d", ("in",), "plane"))
+last_units = (("c", ("in", "small"), "plane"),)
+after_turn = "=a"
+into_middle = "=a"
+after_middle = "bd =a"
+into_last = "=bda"
+after_last = "bc a d c b d a b c d a c a b c d b c d a c b d A c b d B c"
 
 
 def mesh_bits():
@@ -728,10 +738,18 @@
 
 def axis_orders(kind):
     deep, core, across, along = mesh_bits()
+    if kind.endswith(" turned"):
+        kind = kind[: -len(" turned")]
+        across, along = along, across
+    near, far = deep[:1], deep[1:]
     orders = {
         "plane": (across + along + deep, along + across + deep),
-        "deep": (deep + across + along, deep + along + across),
         "mixed": (across + along + deep, along + deep + across),
+        "inner": (across + near + along + far, along + near + across + far),
+        "second": (across + along + deep, near + across + along + far),
+        "late": (across + along + deep, along + near + across + far),
+        "first": (near + across + along + far, near + along + across + far),
+        "cross": (across + along + deep, near + along + across + far),
     }
     return core, orders[kind]
 
@@ -814,6 +832,10 @@
         self.last = sends
         return payload
 
+    def settle(self, arrays):
+        arrays, self.last = lax.optimization_barrier((arrays, self.last))
+        return arrays
+
 
 def aligned(first, rows):
     return pl.ds(pl.multiple_of(first, 8), rows)
@@ -836,45 +858,51 @@
         return ((half_blocks * self.rows, self.columns), f32)
 
 
-def tail_layout(model, width):
-    out_rows = 4 * width // (2 * half_blocks)
-    glu_rows = model // (2 * half_blocks)
-    layout = Layout(out_rows + glu_rows, model, tail_kind)
-    layout.add("out", out_rows, 0, 0, out_rows)
-    layout.add("glu", glu_rows, 0, out_rows, glu_rows)
+def unit_layout(keys, kind, model, width):
+    total = 2 * half_blocks
+    out_rows, rows, wide = 4 * width // total, model // total, 2 * width
+    if keys == ("out",):
+        layout = Layout(out_rows, model, kind)
+        layout.add("out", out_rows, 0, 0, out_rows)
+    elif keys == ("glu",):
+        layout = Layout(rows, model, kind)
+        layout.add("glu", rows, 0, 0, rows)
+    elif keys == ("out", "glu"):
+        layout = Layout(out_rows + rows, model, kind)
+        layout.add("out", out_rows, 0, 0, out_rows)
+        layout.add("glu", rows, 0, out_rows, rows)
+    elif keys == ("in",):
+        layout = Layout(rows, wide, kind)
+        layout.add("in", rows, 0, 0, rows)
+    elif keys == ("glu", "in"):
+        layout = Layout(rows, model + wide, kind)
+        layout.add("glu", rows, 0, 0, rows, slice(0, model))
+        layout.add("in", rows, 0, 0, rows, slice(model, model + wide))
+    else:
+        pieces = rows // 8
+        layout = Layout(8, pieces * wide + lane_count, kind)
+        for piece in range(pieces):
+            layout.add("in", rows, 8 * piece, 0, 8, slice(piece * wide, (piece + 1) * wide))
+        layout.add("small", 8, 0, 0, 8, slice(pieces * wide, pieces * wide + lane_count))
     return layout
 
 
-def in_layout(model, width):
-    rows = model // (2 * half_blocks)
-    layout = Layout(rows, 2 * width, in_kind)
-    layout.add("in", rows, 0, 0, rows)
-    return layout
-
-
-def last_layout(model, width):
-    rows = model // (2 * half_blocks)
-    pieces = rows // 8
-    wide = 2 * width
-    layout = Layout(8, pieces * wide + lane_count, last_kind)
-    for piece in range(pieces):
-        layout.add("in", rows, 8 * piece, 0, 8, slice(piece * wide, (piece + 1) * wide))
-    layout.add("small", 8, 0, 0, 8, slice(pieces * wide, pieces * wide + lane_count))
-    return layout
-
-
 class Emit:
-    def __init__(self, layout, keep_ref, send_ref):
-        self.sections = layout.sections
-        self.halves = (keep_ref, send_ref)
-        self.bases = half_bases(layout.kind)
+    def __init__(self, units, refs, model, width):
+        self.homes = {}
+        for index, (unused, keys, kind) in enumerate(units):
+            layout = unit_layout(keys, kind, model, width)
+            for key in keys:
+                self.homes[key] = (layout, refs[2 * index : 2 * index + 2], half_bases(kind))
 
     def put(self, key, array_ref):
+        layout, halves, bases = self.homes[key]
+
         def one(place, carry):
             for half in (1, 0):
-                owner = lax.bitwise_xor(self.bases[half], place)
-                for array_at, block_at in self.sections[key]:
-                    self.halves[half][block_at(place)] = array_ref[array_at(owner)]
+                owner = lax.bitwise_xor(bases[half], place)
+                for array_at, block_at in layout.sections[key]:
+                    halves[half][block_at(place)] = array_ref[array_at(owner)]
             return carry
 
         lax.fori_loop(0, half_blocks, one, 0)
@@ -883,58 +911,47 @@
 run_places = ((0, 0), (0, half_blocks // 2), (1, 0), (1, half_blocks // 2))
 
 
-def place_kernel(layouts, goals, *refs):
+def place_kernel(layout, goals, *refs):
     outs = refs[len(refs) - 1 - len(goals) : -1]
     semaphores = refs[-1]
-    targets = []
-    for out, writes in zip(outs, goals):
-        targets.append([out if layer is None else out.at[layer] for unused, unused_too, layer in writes])
-    for unit, layout in enumerate(layouts):
-        bases = half_bases(layout.kind)
-        for run, (half, first) in zip(refs[4 * unit : 4 * unit + 4], run_places):
-
-            def one(place, carry, run=run, half=half, first=first, unit=unit, layout=layout):
-                owner = lax.bitwise_xor(bases[half], first + place)
-                for index, writes in enumerate(goals):
-                    for target, (source, key, unused) in zip(targets[index], writes):
-                        if source != unit:
-                            continue
-                        for array_at, block_at in layout.sections[key]:
-                            pltpu.make_async_copy(
-                                run.at[block_at(place)],
-                                target.at[array_at(owner)],
-                                semaphores.at[index],
-                            ).start()
-                return carry
-
-            lax.fori_loop(0, half_blocks // 2, one, 0)
-    for index, group in enumerate(targets):
-        for target in group:
-            pltpu.make_async_copy(target, target, semaphores.at[index]).wait()
-
-
-def place_units(name, units, goals, sums):
-    operands = []
+    bases = half_bases(layout.kind)
+    for index, (half, first) in enumerate(run_places):
+
+        def one(place, carry, run=refs[index], half=half, first=first, index=index):
+            owner = lax.bitwise_xor(bases[half], first + place)
+            for out, (key, layer) in zip(outs, goals):
+                for array_at, block_at in layout.sections[key]:
+                    pltpu.make_async_copy(
+                        run.at[block_at(place)],
+                        (out if layer is None else out.at[layer]).at[array_at(owner)],
+                        semaphores.at[index],
+                    ).start()
+            return carry
+
+        lax.fori_loop(0, half_blocks // 2, one, 0)
+    for index in range(len(run_places)):
+        run = refs[index]
+        pltpu.make_async_copy(run, run, semaphores.at[index]).wait()
+
+
+def place_unit(runs, layout, goals, shapes, sums):
+    operands = [("run", run) for run in runs]
     aliases = {}
-    for unit, unused in units:
-        operands.extend(("run", run) for run in unit.runs)
-    for index, (key, unused, unused_too) in enumerate(goals):
+    for index, (key, unused) in enumerate(goals):
         if key in sums:
             aliases[len(operands)] = index
             operands.append(("before", (sums[key], None)))
     outs = call(
-        functools.partial(
-            place_kernel, [layout for unused, layout in units], [writes for *unused, writes in goals]
-        ),
-        name,
+        functools.partial(place_kernel, layout, goals),
+        "place_" + "_".join(key for key, unused in goals),
         operands,
-        tuple((shape, f32) for unused, shape, unused_too in goals),
-        (pltpu.SemaphoreType.DMA((len(goals),)),),
+        tuple((shapes[key], f32) for key, unused in goals),
+        (pltpu.SemaphoreType.DMA((len(run_places),)),),
         written=range(len(goals)),
         aliases=aliases,
         plain=True,
     )
-    for (key, unused, unused_too), out in zip(goals, outs):
+    for (key, unused), out in zip(goals, outs):
         sums[key] = out
 
 
@@ -957,18 +974,33 @@
     arrays = []
     specs = []
     layers = {}
-    for position, (key, operand) in enumerate(operands):
+    pieces = None
+    flat = []
+    for key, operand in operands:
+        if isinstance(operand, list):
+            pieces = (len(flat), len(operand))
+            flat.extend((key, piece) for piece in operand)
+        else:
+            flat.append((key, operand))
+    for position, (key, operand) in enumerate(flat):
         space = pltpu.SMEM if key in scalars else pltpu.VMEM
         if isinstance(operand, tuple):
             operand, layer = operand
+            space = pl.ANY
             if layer is not None:
                 layers[position] = layer
-            space = pl.ANY
+                operand = pltpu.with_memory_space_constraint(operand, pltpu.HBM)
         specs.append(pl.BlockSpec(memory_space=space))
         arrays.append(operand)
     fetched = [
         pltpu.VMEM(arrays[position].shape[1:], arrays[position].dtype) for position in layers
     ]
+
+    gathered = []
+    if pieces is not None:
+        first, count = pieces
+        rows, columns = arrays[first].shape
+        gathered = [pltpu.VMEM((count * rows, columns), arrays[first].dtype)]
 
     def kernel(*refs):
         if plain:
@@ -979,6 +1011,14 @@
         targets = refs[len(refs) - len(fetched) - 1 : -1]
         for index, (position, layer) in enumerate(layers.items()):
             given[position] = Fetch(given[position], layer, targets[index], refs[-1].at[index])
+        if pieces is not None:
+            first, count = pieces
+            rows = given[first].shape[0]
+            whole, rest = rest[-1], rest[:-1]
+            for offset in range(count):
+                source = lax.bitwise_xor(given[0][0], offset)
+                whole[aligned(source * rows, rows), :] = given[first + offset][...]
+            given[first : first + count] = [whole]
         body(*given, *rest)
 
     return pl.pallas_call(
@@ -998,6 +1038,7 @@
         scratch_shapes=[
             entry if not isinstance(entry, tuple) else pltpu.VMEM(*entry) for entry in scratch
         ]
+        + gathered
         + fetched
         + ([] if plain else [pltpu.SemaphoreType.DMA((max(1, len(fetched)),))]),
         input_output_aliases=aliases or {},
@@ -1030,7 +1071,21 @@
     tables = jnp.stack(rate_tables, axis=1).reshape(4 * layer_count, width)
 
     def gather(totals):
-        return lax.all_gather(totals, "seq", axis=0, tiled=True)
+        if device_count != 8:
+            return lax.all_gather(totals, "seq", axis=0, tiled=True)
+
+        def from_other(array, bits):
+            return lax.ppermute(
+                array, "seq", [(index, index ^ bits) for index in range(device_count)]
+            )
+
+        pieces = [None] * device_count
+        pieces[0] = totals
+        for bits in range(2, device_count, 2):
+            pieces[bits] = from_other(totals, bits)
+        for bits in range(0, device_count, 2):
+            pieces[bits + 1] = from_other(pieces[bits], 1)
+        return pieces
 
     flags_out = ((3, count, lane_count), f32)
     blocks_out = ((2, device_count * row_count, lane_count), f32)
@@ -1046,14 +1101,17 @@
     in_out = ((model, 2 * width), f32)
     vector = ((1, model), f32)
 
+    def in_place(array):
+        return pltpu.with_memory_space_constraint(array, pltpu.HBM)
+
     flags, blocks, values, scaled, drive, ends, totals = call(
         functools.partial(first_kernel, length),
         "first",
         (
             ("place", place),
-            ("docs", doc_lengths),
-            ("inputs", inputs),
-            ("gain", norm_gain),
+            ("docs", in_place(doc_lengths)),
+            ("inputs", in_place(inputs)),
+            ("gain", in_place(norm_gain)),
             ("tables", tables),
             ("in", (in_weight, 0)),
         ),
@@ -1093,17 +1151,50 @@
         values, scaled = next_values, next_scaled
     layer = layer_count - 1
     gathered = gather(totals)
-
-    whole = {"out": (layer_count, 4 * width, model), "glu": (layer_count, model, model)}
-    whole["in"] = (layer_count, model, 2 * width)
+    small_out = ((8 * 2 * half_blocks, lane_count), f32)
+    shapes = {
+        "out": (layer_count, 4 * width, model),
+        "glu": (layer_count, model, model),
+        "in": (layer_count, model, 2 * width),
+        "small": small_out[0],
+    }
     sums = {}
-    tail_part = tail_layout(model, width)
-    in_part = in_layout(model, width)
-    last_part = last_layout(model, width)
     line = Line()
-    (
-        output, grad, states, enter, d_mixed, d_states, keep, send, skip_grad, ends, totals,
-    ) = call(
+    layouts, goals, units = {}, {}, {}
+
+    def unit_outs(entries):
+        outs = []
+        for name, keys, kind in entries:
+            layouts[name] = unit_layout(keys, kind, model, width)
+            outs.extend([((half_blocks * layouts[name].rows, layouts[name].columns), f32)] * 2)
+        return tuple(outs)
+
+    def open_units(entries, halves, layer_of):
+        for index, (name, keys, kind) in enumerate(entries):
+            units[name] = UnitSum(halves[2 * index], halves[2 * index + 1], kind)
+            goals[name] = [(key, layer_of[key]) for key in keys]
+
+    placed = set()
+
+    def place_sums(name):
+        placed.add(name)
+        runs = line.settle(units[name].runs)
+        place_unit(runs, layouts[name], goals[name], shapes, sums)
+        line.last = [sums[key] for key, unused in goals[name]]
+
+    def follow(plan, payload=()):
+        for group in plan.split():
+            if group.isupper():
+                for name in group.lower():
+                    if units[name].runs is not None and name not in placed:
+                        place_sums(name)
+            elif group[0] == "=":
+                payload = line.advance([units[name] for name in group[1:]], payload)
+            else:
+                line.advance([units[name] for name in group])
+        return payload
+
+    results = call(
         functools.partial(turn_kernel, layer, length),
         "turn",
         (
@@ -1120,80 +1211,62 @@
             ("cotangent", cotangent),
         ),
         (
-            (inputs.shape, bf16), tokens, wide_out, ends_out, tokens, wide_out,
-            tail_part.half(), tail_part.half(), vector, ends_out, totals_out,
+            *unit_outs(turn_units), (inputs.shape, bf16), tokens, wide_out, ends_out, tokens, wide_out,
+            vector, ends_out, totals_out,
         ),
         (
             ((count, 4 * width), bf16), tokens, tokens_low, tokens, tokens_low, tokens_low, tokens,
             tokens_low, glu_out, out_out,
         ),
-        final=(0,),
-        micros=10,
-    )
-    units = [UnitSum(keep, send, tail_kind)]
-    tail_units = [units[0]]
-    in_units = []
-    skip_grads = [skip_grad]
-    gain_grads, rate_grads = [], []
+        final=(2 * len(turn_units),),
+        micros=6,
+    )
+    halves, results = results[: 2 * len(turn_units)], results[2 * len(turn_units) :]
+    output, grad, states, enter, d_mixed, d_states, skip_grad, ends, totals = results
+    open_units(turn_units, halves, {"out": layer, "glu": layer})
+    gathered = follow(into_middle, gather(follow(after_turn, totals)))
     back_scratch = (
         drive_out, drive_out, ((count, 2 * width), bf16), bar_out, tokens,
     )
     rate_out = ((4, width), f32)
-    small_out = ((8 * 2 * half_blocks, lane_count), f32)
-    for layer in reversed(range(1, layer_count)):
-        if layer == layer_count - 1:
-            totals = line.advance(units, totals)
-        gathered = gather(totals)
-        gathered = line.advance(units, gathered)
-        low_states, low, low_enter, mixed, act, gate, low_values, low_scaled = kept[layer - 1]
+    low_states, low, low_enter, mixed, act, gate, low_values, low_scaled = kept[0]
+    results = call(
+        functools.partial(back_middle_kernel, layer, length),
+        "back_middle",
         (
-            keep, send, in_keep, in_send, gain_grad, rate_grad, grad, d_mixed, d_states, skip_grad, ends,
-            totals,
-        ) = call(
-            functools.partial(back_middle_kernel, layer, length),
-            "back_middle",
-            (
-                ("place", place),
-                ("gathered", gathered),
-                *shared,
-                ("gain", norm_gain),
-                ("skip", skip_weight),
-                ("in", (in_weight, layer)),
-                ("d_states", d_states),
-                ("ends", ends),
-                ("states", states),
-                ("enter", enter),
-                ("scaled", scaled),
-                ("values", values),
-                ("d_mixed", d_mixed),
-                ("grad", grad),
-                ("out", (out_weight, layer - 1)),
-                ("glu", (glu_weight, layer - 1)),
-                ("mixed", mixed),
-                ("act", act),
-                ("gate", gate),
-                ("below_scaled", low_scaled),
-                ("low", low),
-            ),
-            (
-                tail_part.half(), tail_part.half(), in_part.half(), in_part.half(), vector, rate_out,
-                tokens, tokens, wide_out, vector, ends_out, totals_out,
-            ),
-            back_scratch + (tokens_low, tokens_low, in_out, glu_out, out_out),
-            micros=14,
-        )
-        fresh = [UnitSum(keep, send, tail_kind), UnitSum(in_keep, in_send, in_kind)]
-        line.advance(fresh)
-        tail_units.append(fresh[0])
-        in_units.append(fresh[1])
-        gain_grads.insert(0, gain_grad)
-        rate_grads.insert(0, rate_grad)
-        skip_grads.insert(0, skip_grad)
-        states, enter, values, scaled = low_states, low_enter, low_values, low_scaled
-        totals = line.advance(units, totals)
-        units = fresh + units
-    gathered = gather(totals)
-    gathered = line.advance(units, gathered)
+            ("place", place),
+            ("gathered", gathered),
+            *shared,
+            ("gain", norm_gain),
+            ("skip", skip_weight),
+            ("in", (in_weight, layer)),
+            ("d_states", d_states),
+            ("ends", ends),
+            ("states", states),
+            ("enter", enter),
+            ("scaled", scaled),
+            ("values", values),
+            ("d_mixed", d_mixed),
+            ("grad", grad),
+            ("out", (out_weight, layer - 1)),
+            ("glu", (glu_weight, layer - 1)),
+            ("mixed", mixed),
+            ("act", act),
+            ("gate", gate),
+            ("below_scaled", low_scaled),
+            ("low", low),
+        ),
+        (
+            *unit_outs(middle_units), vector, rate_out, tokens, tokens, wide_out, vector, ends_out,
+            totals_out,
+        ),
+        back_scratch + (tokens_low, tokens_low, in_out, glu_out, out_out),
+        micros=6,
+    )
+    halves, results = results[: 2 * len(middle_units)], results[2 * len(middle_units) :]
+    gain_grad, rate_grad, grad, d_mixed, d_states, low_skip_grad, ends, totals = results
+    open_units(middle_units, halves, {"out": layer - 1, "glu": layer - 1, "in": layer})
+    gathered = follow(into_last, gather(follow(after_middle, totals)))
     keep, send, input_grad = call(
         functools.partial(back_last_kernel, length),
         "back_last",
@@ -1206,54 +1279,30 @@
             ("in", (in_weight, 0)),
             ("d_states", d_states),
             ("ends", ends),
-            ("states", states),
-            ("enter", enter),
-            ("scaled", scaled),
-            ("values", values),
+            ("states", low_states),
+            ("enter", low_enter),
+            ("scaled", low_scaled),
+            ("values", low_values),
             ("d_mixed", d_mixed),
             ("grad", grad),
-            *(("skip_grad", term) for term in skip_grads),
-            *(("gain_grad", term) for term in gain_grads),
-            *(("rate_grad", term) for term in rate_grads),
+            ("skip_grad", low_skip_grad),
+            ("skip_grad", skip_grad),
+            ("gain_grad", gain_grad),
+            ("rate_grad", rate_grad),
         ),
-        (last_part.half(), last_part.half(), (inputs.shape, bf16)),
-        back_scratch
-        + (
-            tokens_low, in_out, vector, rate_out, small_out,
-        ),
+        (*unit_outs(last_units), (inputs.shape, bf16)),
+        back_scratch + (tokens_low, in_out, vector, rate_out, small_out),
         final=(2,),
-        micros=10,
-    )
-    last_unit = UnitSum(keep, send, last_kind)
-    line.advance([last_unit])
-    named = {"a": tail_units[0], "b": tail_units[-1], "c": last_unit, "d": (in_units or [last_unit])[-1]}
-    for name in round_order:
-        line.advance([named[name]])
-    for unit in tail_units + in_units + [last_unit]:
+        micros=4,
+    )
+    open_units(last_units, (keep, send), {"in": 0, "small": None})
+    follow(after_last)
+    for name, unit in units.items():
         while unit.runs is None:
-            line.advance([unit])
-    for index, unit in enumerate(tail_units):
-        layer = layer_count - 1 - index
-        place_units(
-            "place_tail",
-            [(unit, tail_part)],
-            [("out", whole["out"], [(0, "out", layer)]), ("glu", whole["glu"], [(0, "glu", layer)])],
-            sums,
-        )
-    ends = [(unit, in_part) for unit in in_units] + [(last_unit, last_part)]
-    place_units(
-        "place_last",
-        ends,
-        [
-            (
-                "in",
-                whole["in"],
-                [(index, "in", layer_count - 1 - index) for index in range(layer_count)],
-            ),
-            ("small", small_out[0], [(len(ends) - 1, "small", None)]),
-        ],
-        sums,
-    )
+            follow(name)
+    for name in units:
+        if name not in placed:
+            place_sums(name)
     small = sums["small"]
 
     def taken(first, shape):

time: 214 us -> 182 us (0.85)
  blocking collectives: 40.2 us -> 0 us
  starting transfers between devices: 34.3 us -> 49.4 us
  waiting for transfers between devices: 88.6 us -> 96.4 us
  Pallas kernels: 36.9 us -> 29.7 us
  local copies, waits for them, and re-layouts: 6.24 us -> 1.28 us
  other arithmetic: 6.56 us -> 3.41 us
    all_gather x4 -> x0, blocking collectives: 40.2 us -> none  [gather(): return lax.all_gather(totals, 'seq', axis=0, tiled=True)]
    ppermute x0 -> x28, starting transfers between devices: none -> 20.3 us  [from_other(): lax.ppermute(array, 'seq', [(index, index ^ bits) for index in range(devi...]
    ppermute x0 -> x28, waiting for transfers between devices: none -> 15.8 us  [from_other(): lax.ppermute(array, 'seq', [(index, index ^ bits) for index in range(devi...]
    ppermute x40, waiting for transfers between devices: 88.6 us -> 80.6 us  [swap(): return lax.ppermute(array, ('seq', 'batch'), pairs)]
    pallas_call x8 -> x9, Pallas kernels: 36.9 us -> 29.7 us  [call(): pl.pallas_call(kernel, name=name, in_specs=specs, out_specs=[pl.BlockSpec...]
    ppermute x40, starting transfers between devices: 34.3 us -> 29.1 us  [swap(): return lax.ppermute(array, ('seq', 'batch'), pairs)]
    unnamed x34 -> x12, local copies, waits for them, and re-layouts: 5 us -> 0.04 us
    add x20, other arithmetic: 4.69 us -> 1.55 us  [added(): total = total + part[low:high]]
  transfers between devices with their start and end apart: 40 -> 68, of which waited for: 18 -> 37; matrix products, arithmetic and copies ran while one was open for 3% -> 1% of each run, Pallas kernels for 6% -> 8%
where the time goes in v2:
time: 182 us; the launch traced here: 181 us
  waiting for transfers between devices  96.4 us (53%)
  starting transfers between devices  49.4 us (27%)
  Pallas kernels  29.7 us (16%)
  other arithmetic  3.41 us (2%)
    ppermute x40, waiting for transfers between devices, swap(): return lax.ppermute(array, ('seq', 'batch'), pairs)  80.6 us
    pallas_call x9, Pallas kernels, call(): pl.pallas_call(kernel, name=name, in_specs=specs, out_specs=[pl.BlockSpec...  29.7 us
    ppermute x40, starting transfers between devices, swap(): return lax.ppermute(array, ('seq', 'batch'), pairs)  29.1 us
    ppermute x28, starting transfers between devices, from_other(): lax.ppermute(array, 'seq', [(index, index ^ bits) for index in range(devi...  20.3 us
    ppermute x28, waiting for transfers between devices, from_other(): lax.ppermute(array, 'seq', [(index, index ^ bits) for index in range(devi...  15.8 us
  transfers between devices with their start and end apart: 68, of which 37 were waited for; matrix products, arithmetic and copies ran while one was open for 1% of the time, Pallas kernels for 8%

profile of v2, /device:TPU:0, one launch (start us, length us, event | category | flops | bytes accessed | tf_op | source)
XLA Modules:
  0.0 181.4 jit_solution(114030989730558800)
XLA Ops:
  1.6 3.2 %first.1 = (f32[3,256,128]{2,1,0:T(8,128)S(1)}, f32[2,16,128]{2,1,0:T(8,128)S(1)}, bf16[256,512]{1,0:T(8,128)(2,1)S(1)}, bf16[256,512]{1,0:T(8,128)(2,1)S(1)}, f...) custom-call(s32[1]{0:T(128)} %bitcast.refs_0_, s32[2,8]{1,0:T(2,128)} %refs_1_.1, ...), custom_call_target="tpu_custom_call" | custom-call | flops 4000000000 | bytes 14400000 | tf_op jit(solution)/shard_map/first/pallas_call | solution.py:1024
  4.8 3.0 %collective-permute-start.1 = (f32[8,384]{1,0:T(8,128)S(1)}, f32[8,384]{1,0:T(8,128)S(1)}, u32[]{:S(2)}, u32[]{:S(2)}) collective-permute-start(f32[8,384]{1,0:T(8,128)S(1)} %get-tuple-element.130.refs_1_), channel_id=1, source_target_pairs={{0,8},{4,12},{8,0},{12,4},{16,24},{20,28},{24,16},{28,20},{1,9},{5... | collective-permute-start | bytes 36872 | tf_op jit(solution)/shard_map/ppermute | solution.py:1078
  11.5 2.4 %collective-permute-done.5.refs_7_ = f32[8,384]{1,0:T(8,128)S(1)} collective-permute-done((f32[8,384]{1,0:T(8,128)S(1)}, f32[8,384]{1,0:T(8,128)S(1)}, u32[]{:S(2)}, u32[]{:S(2)}) %collective-permute-start.5) | collective-permute-done | bytes 12320 | tf_op jit(solution)/shard_map/ppermute | solution.py:1078
  15.1 3.8 %middle.1 = (f32[256,1536]{1,0:T(8,128)S(1)}, bf16[256,1536]{1,0:T(8,128)(2,1)S(1)}, f32[8,1536]{1,0:T(8,128)S(1)}, f32[256,512]{1,0:T(8,128)S(1)}, bf16[256,512...) custom-call(s32[1]{0:T(128)} %bitcast.refs_0_, ...), custom_call_target="tpu_custom_call" | custom-call | flops 4000000000 | bytes 14400000 | tf_op jit(solution)/shard_map/middle/pallas_call | solution.py:1024
  19.6 2.9 %collective-permute-start.12 = (f32[8,384]{1,0:T(8,128)S(1)}, f32[8,384]{1,0:T(8,128)S(1)}, u32[]{:S(2)}, u32[]{:S(2)}) collective-permute-start(f32[8,384]{1,0:T(8,128)S(1)} %get-tuple-element.137.refs_1_), channel_id=1, source_target_pairs={{0,24},{4,28},{8,16},{12,20},{16,8},{20,12},{24,0},{28,4},{1,25},{... | collective-permute-start | bytes 36872 | tf_op jit(solution)/shard_map/ppermute | solution.py:1078
  25.3 6.2 %turn.1 = (f32[1024,512]{1,0:T(8,128)S(1)}, f32[1024,512]{1,0:T(8,128)S(1)}, bf16[2,128,512]{2,1,0:T(8,128)(2,1)}, f32[256,512]{1,0:T(8,128)S(1)}, f32[256,1536]...) custom-call(s32[1]{0:T(128)} %bitcast.refs_0_, ...), custom_call_target="tpu_custom_call" | custom-call | flops 6000000000 | bytes 21600000 | tf_op jit(solution)/shard_map/turn/pallas_call | solution.py:1024
  31.8 1.9 %collective-permute-start.16 = (f32[8,384]{1,0:T(8,128)S(1)}, f32[8,384]{1,0:T(8,128)S(1)}, u32[]{:S(2)}, u32[]{:S(2)}) collective-permute-start(f32[8,384]{1,0:T(8,128)S(1)} %get-tuple-element.148.refs_1_), channel_id=1, source_target_pairs={{0,8},{4,12},{8,0},{12,4},{16,24},{20,28},{24,16},{28,20},{1,9},{5... | collective-permute-start | bytes 36872 | tf_op jit(solution)/shard_map/ppermute | solution.py:1078
  37.4 2.4 %collective-permute-done.20.refs_7_ = f32[8,384]{1,0:T(8,128)S(1)} collective-permute-done((f32[8,384]{1,0:T(8,128)S(1)}, f32[8,384]{1,0:T(8,128)S(1)}, u32[]{:S(2)}, u32[]{:S(2)}) %collective-permute-start.20) | collective-permute-done | bytes 12320 | tf_op jit(solution)/shard_map/ppermute | solution.py:1078
  41.6 6.1 %back_middle.1 = (f32[1024,512]{1,0:T(8,128)S(1)}, f32[1024,512]{1,0:T(8,128)S(1)}, f32[256,768]{1,0:T(8,128)S(1)}, f32[256,768]{1,0:T(8,128)S(1)}, f32[1,512]{1...) custom-call(s32[1]{0:T(128)} %bitcast.refs_0_, ...), custom_call_target="tpu_custom_call" | custom-call | flops 6000000000 | bytes 21600000 | tf_op jit(solution)/shard_map/back_middle/pallas_call | solution.py:1024
  48.2 7.6 %collective-permute-done.24 = f32[512,512]{1,0:T(8,128)S(1)} collective-permute-done((f32[512,512]{1,0:T(8,128)S(1)}, f32[512,512]{1,0:T(8,128)S(1)}, u32[]{:S(2)}, u32[]{:S(2)}) %collective-permute-start.24) | collective-permute-done | bytes 1048608 | tf_op jit(solution)/shard_map/ppermute | solution.py:776
  56.7 1.9 %collective-permute-start.29 = (f32[8,384]{1,0:T(8,128)S(1)}, f32[8,384]{1,0:T(8,128)S(1)}, u32[]{:S(2)}, u32[]{:S(2)}) collective-permute-start(f32[8,384]{1,0:T(8,128)S(1)} %get-tuple-element.176.refs_1_), channel_id=1, source_target_pairs={{0,16},{4,20},{8,24},{12,28},{16,0},{20,4},{24,8},{28,12},{1,17},{... | collective-permute-start | bytes 36872 | tf_op jit(solution)/shard_map/ppermute | solution.py:1078
  60.4 3.6 %collective-permute-start.26 = (f32[8,384]{1,0:T(8,128)S(1)}, f32[8,384]{1,0:T(8,128)S(1)}, u32[]{:S(2)}, u32[]{:S(2)}) collective-permute-start(f32[8,384]{1,0:T(8,128)S(1)} %get-tuple-element.176.refs_1_), channel_id=1, source_target_pairs={{0,4},{4,0},{8,12},{12,8},{16,20},{20,16},{24,28},{28,24},{1,5},{5... | collective-permute-start | bytes 36872 | tf_op jit(solution)/shard_map/ppermute | solution.py:1078
  70.9 4.0 %back_last.1 = (f32[64,3200]{1,0:T(8,128)S(1)}, f32[64,3200]{1,0:T(8,128)S(1)}, bf16[2,128,512]{2,1,0:T(8,128)(2,1)}) custom-call(s32[1]{0:T(128)} %bitcast.refs_0_, f32[8,384]{1,0:T(8,128)S(1)} %get-tuple-element.176.refs_1_, f32[8,384]{1,0:T(8,128)S(1)} %collective-permute-done.26.refs_2_, f32[8,384]{1,0:T(8,128)S(1)} %collective-permute-done.27.refs_3_, ...), custom_call_target="tpu_custom_call" | custom-call | flops 4000000000 | bytes 14400000 | tf_op jit(solution)/shard_map/back_last/pallas_call | solution.py:1024
  75.0 7.2 %collective-permute-done.33 = f32[512,512]{1,0:T(8,128)S(1)} collective-permute-done((f32[512,512]{1,0:T(8,128)S(1)}, f32[512,512]{1,0:T(8,128)S(1)}, u32[]{:S(2)}, u32[]{:S(2)}) %collective-permute-start.33) | collective-permute-done | bytes 1048608 | tf_op jit(solution)/shard_map/ppermute | solution.py:776
  83.1 4.1 %collective-permute-done.35 = f32[128,768]{1,0:T(8,128)S(1)} collective-permute-done((f32[128,768]{1,0:T(8,128)S(1)}, f32[128,768]{1,0:T(8,128)S(1)}, u32[]{:S(2)}, u32[]{:S(2)}) %collective-permute-start.35) | collective-permute-done | bytes 393248 | tf_op jit(solution)/shard_map/ppermute | solution.py:776
  87.2 2.7 %collective-permute-start.40 = (f32[128,512]{1,0:T(8,128)S(1)}, f32[128,512]{1,0:T(8,128)S(1)}, u32[]{:S(2)}, u32[]{:S(2)}) collective-permute-start(f32[128,512]{1,0:T(8,128)S(1)} %fusion.1), channel_id=1, source_target_pairs={{0,2},{1,3},{2,0},{3,1},{4,6},{5,7},{6,4},{7,5},{8,10},{9,11},{10,... | collective-permute-start | bytes 786440 | tf_op jit(solution)/shard_map/ppermute | solution.py:776
  95.5 5.1 %collective-permute-done.40 = f32[128,512]{1,0:T(8,128)S(1)} collective-permute-done((f32[128,512]{1,0:T(8,128)S(1)}, f32[128,512]{1,0:T(8,128)S(1)}, u32[]{:S(2)}, u32[]{:S(2)}) %collective-permute-start.40) | collective-permute-done | bytes 262176 | tf_op jit(solution)/shard_map/ppermute | solution.py:776
  102.7 2.8 %collective-permute-done.39 = f32[128,512]{1,0:T(8,128)S(1)} collective-permute-done((f32[128,512]{1,0:T(8,128)S(1)}, f32[128,512]{1,0:T(8,128)S(1)}, u32[]{:S(2)}, u32[]{:S(2)}) %collective-permute-start.39) | collective-permute-done | bytes 262176 | tf_op jit(solution)/shard_map/ppermute | solution.py:776
  105.6 2.3 %collective-permute-start.46 = (f32[128,512]{1,0:T(8,128)S(1)}, f32[128,512]{1,0:T(8,128)S(1)}, u32[]{:S(2)}, u32[]{:S(2)}) collective-permute-start(f32[128,512]{1,0:T(8,128)S(1)} %fusion), channel_id=1, source_target_pairs={{0,2},{1,3},{2,0},{3,1},{4,6},{5,7},{6,4},{7,5},{8,10},{9,11},{10,... | collective-permute-start | bytes 786440 | tf_op jit(solution)/shard_map/ppermute | solution.py:776
  108.6 8.0 %collective-permute-done.43 = f32[128,512]{1,0:T(8,128)S(1)} collective-permute-done((f32[128,512]{1,0:T(8,128)S(1)}, f32[128,512]{1,0:T(8,128)S(1)}, u32[]{:S(2)}, u32[]{:S(2)}) %collective-permute-start.43) | collective-permute-done | bytes 262176 | tf_op jit(solution)/shard_map/ppermute | solution.py:776
  117.2 2.9 %collective-permute-done.46 = f32[128,512]{1,0:T(8,128)S(1)} collective-permute-done((f32[128,512]{1,0:T(8,128)S(1)}, f32[128,512]{1,0:T(8,128)S(1)}, u32[]{:S(2)}, u32[]{:S(2)}) %collective-permute-start.46) | collective-permute-done | bytes 262176 | tf_op jit(solution)/shard_map/ppermute | solution.py:776
  121.5 4.4 %collective-permute-done.47 = f32[256,512]{1,0:T(8,128)S(1)} collective-permute-done((f32[256,512]{1,0:T(8,128)S(1)}, f32[256,512]{1,0:T(8,128)S(1)}, u32[]{:S(2)}, u32[]{:S(2)}) %collective-permute-start.47) | collective-permute-done | bytes 524320 | tf_op jit(solution)/shard_map/ppermute | solution.py:776
  126.6 2.0 %collective-permute-start.48 = (f32[8,3200]{1,0:T(8,128)S(1)}, f32[8,3200]{1,0:T(8,128)S(1)}, u32[]{:S(2)}, u32[]{:S(2)}) collective-permute-start(f32[8,3200]{1,0:T(8,128)S(1)} %fusion.2), channel_id=1, source_target_pairs={{0,2},{1,3},{2,0},{3,1},{4,6},{5,7},{6,4},{7,5},{8,10},{9,11},{10,... | collective-permute-start | bytes 307208 | tf_op jit(solution)/shard_map/ppermute | solution.py:776
  129.6 8.4 %collective-permute-done.50 = f32[32,768]{1,0:T(8,128)S(1)} collective-permute-done((f32[32,768]{1,0:T(8,128)S(1)}, f32[32,768]{1,0:T(8,128)S(1)}, u32[]{:S(2)}, u32[]{:S(2)}) %collective-permute-start.50) | collective-permute-done | bytes 98336 | tf_op jit(solution)/shard_map/ppermute | solution.py:776
  140.3 3.4 %collective-permute-done.53 = f32[32,768]{1,0:T(8,128)S(1)} collective-permute-done((f32[32,768]{1,0:T(8,128)S(1)}, f32[32,768]{1,0:T(8,128)S(1)}, u32[]{:S(2)}, u32[]{:S(2)}) %collective-permute-start.53) | collective-permute-done | bytes 98336 | tf_op jit(solution)/shard_map/ppermute | solution.py:776
  145.5 2.2 %collective-permute-done.58 = f32[256,512]{1,0:T(8,128)S(1)} collective-permute-done((f32[256,512]{1,0:T(8,128)S(1)}, f32[256,512]{1,0:T(8,128)S(1)}, u32[]{:S(2)}, u32[]{:S(2)}) %collective-permute-start.58) | collective-permute-done | bytes 524320 | tf_op jit(solution)/shard_map/ppermute | solution.py:776
  150.0 6.4 %collective-permute-done.54 = f32[16,3200]{1,0:T(8,128)S(1)} collective-permute-done((f32[16,3200]{1,0:T(8,128)S(1)}, f32[16,3200]{1,0:T(8,128)S(1)}, u32[]{:S(2)}, u32[]{:S(2)}) %collective-permute-start.54) | collective-permute-done | bytes 204832 | tf_op jit(solution)/shard_map/ppermute | solution.py:776
  156.4 2.0 %place_out_glu.2 = (f32[2,1536,512]{2,1,0:T(8,128)}, f32[2,512,512]{2,1,0:T(8,128)}) custom-call(f32[512,512]{1,0:T(8,128)S(1)} %pad_maximum_fusion.refs_0_, f32[512,512]{1,0:T(8,128)S(1)} %collective-permute-done.52.refs_1_, f32[512,512]{1,0:T(8,128)S(1)} %collective-permute-done.55.refs_2_, f32[512,512]{1,0:T(8,128)S(1)} %collective-permute-done.56.refs_3_), custom_call_target="tpu_custom_call" | custom-call | flops 4000000000 | bytes 14400000 | tf_op jit(solution)/shard_map/place_out_glu/pallas_call | solution.py:1024
  158.5 5.8 %collective-permute-done.60.refs_1_ = f32[512,512]{1,0:T(8,128)S(1)} collective-permute-done((f32[512,512]{1,0:T(8,128)S(1)}, f32[512,512]{1,0:T(8,128)S(1)}, u32[]{:S(2)}, u32[]{:S(2)}) %collective-permute-start.60) | collective-permute-done | bytes 1048608 | tf_op jit(solution)/shard_map/ppermute | solution.py:776
  166.3 5.7 %collective-permute-done.63.refs_1_ = f32[128,768]{1,0:T(8,128)S(1)} collective-permute-done((f32[128,768]{1,0:T(8,128)S(1)}, f32[128,768]{1,0:T(8,128)S(1)}, u32[]{:S(2)}, u32[]{:S(2)}) %collective-permute-start.63) | collective-permute-done | bytes 393248 | tf_op jit(solution)/shard_map/ppermute | solution.py:776
  172.6 2.0 %place_out_glu.3 = (f32[2,1536,512]{2,1,0:T(8,128)}, f32[2,512,512]{2,1,0:T(8,128)}) custom-call(f32[512,512]{1,0:T(8,128)S(1)} %pad_maximum_fusion.1.refs_0_, f32[512,512]{1,0:T(8,128)S(1)} %collective-permute-done.60.refs_1_, f32[512,512]{1,0:T(8,128)S(1)} %collective-permute-done.61.refs_2_, ...), custom_call_target="tpu_custom_call", output_to_operand_aliasing={{0}: (4, {}), {1}: (5, {})} | custom-call | flops 4000000000 | bytes 14400000 | tf_op jit(solution)/shard_map/place_out_glu/pallas_call | solution.py:1024
  174.6 1.9 %collective-permute-done.59.refs_1_ = f32[32,3200]{1,0:T(8,128)S(1)} collective-permute-done((f32[32,3200]{1,0:T(8,128)S(1)}, f32[32,3200]{1,0:T(8,128)S(1)}, u32[]{:S(2)}, u32[]{:S(2)}) %collective-permute-start.59) | collective-permute-done | bytes 409632 | tf_op jit(solution)/shard_map/ppermute | solution.py:776
  (164 shorter events, 52.0 us)
Async XLA Ops:
  31.6 8.3 %collective-permute-start.14 = (f32[1024,512]{1,0:T(8,128)S(1)}, f32[1024,512]{1,0:T(8,128)S(1)}, u32[]{:S(2)}, u32[]{:S(2)}) collective-permute-start(f32[1024,512]{1,0:T(8,128)S(1)} %get-tuple-element.146), channel_id=1, source_target_pairs={{0,4},{1,5},{2,6},{3,7},{4,0},{5,1},{6,2},{7,3},{8,12},{9,13},{10,... | collective-permute-start | bytes 6291464 | tf_op jit(solution)/shard_map/ppermute | solution.py:776
  41.0 14.8 %collective-permute-start.24 = (f32[512,512]{1,0:T(8,128)S(1)}, f32[512,512]{1,0:T(8,128)S(1)}, u32[]{:S(2)}, u32[]{:S(2)}) collective-permute-start(f32[512,512]{1,0:T(8,128)S(1)} %slice_add_fusion.1), channel_id=1, source_target_pairs={{0,8},{1,9},{2,10},{3,11},{4,20},{5,21},{6,22},{7,23},{8,0},{9,1},... | collective-permute-start | bytes 3145736 | tf_op jit(solution)/shard_map/ppermute | solution.py:776
  47.6 18.7 %collective-permute-start.22 = (f32[1024,512]{1,0:T(8,128)S(1)}, f32[1024,512]{1,0:T(8,128)S(1)}, u32[]{:S(2)}, u32[]{:S(2)}) collective-permute-start(f32[1024,512]{1,0:T(8,128)S(1)} %get-tuple-element.170), channel_id=1, source_target_pairs={{0,4},{1,5},{2,6},{3,7},{4,0},{5,1},{6,2},{7,3},{8,12},{9,13},{10,... | collective-permute-start | bytes 6291464 | tf_op jit(solution)/shard_map/ppermute | solution.py:776
  47.7 10.9 %collective-permute-start.23 = (f32[256,768]{1,0:T(8,128)S(1)}, f32[256,768]{1,0:T(8,128)S(1)}, u32[]{:S(2)}, u32[]{:S(2)}) collective-permute-start(f32[256,768]{1,0:T(8,128)S(1)} %get-tuple-element.172), channel_id=1, source_target_pairs={{0,4},{1,5},{2,6},{3,7},{4,0},{5,1},{6,2},{7,3},{8,12},{9,13},{10,... | collective-permute-start | bytes 2359304 | tf_op jit(solution)/shard_map/ppermute | solution.py:776
  56.0 10.2 %collective-permute-start.25 = (f32[256,512]{1,0:T(8,128)S(1)}, f32[256,512]{1,0:T(8,128)S(1)}, u32[]{:S(2)}, u32[]{:S(2)}) collective-permute-start(f32[256,512]{1,0:T(8,128)S(1)} %slice_add_fusion.4), channel_id=1, source_target_pairs={{0,16},{1,17},{2,18},{3,19},{4,12},{5,13},{6,14},{7,15},{8,24},{9,... | collective-permute-start | bytes 1572872 | tf_op jit(solution)/shard_map/ppermute | solution.py:776
  56.7 9.0 %collective-permute-start.29 = (f32[8,384]{1,0:T(8,128)S(1)}, f32[8,384]{1,0:T(8,128)S(1)}, u32[]{:S(2)}, u32[]{:S(2)}) collective-permute-start(f32[8,384]{1,0:T(8,128)S(1)} %get-tuple-element.176.refs_1_), channel_id=1, source_target_pairs={{0,16},{4,20},{8,24},{12,28},{16,0},{20,4},{24,8},{28,12},{1,17},{... | collective-permute-start | bytes 36872 | tf_op jit(solution)/shard_map/ppermute | solution.py:1078
  67.3 14.8 %collective-permute-start.33 = (f32[512,512]{1,0:T(8,128)S(1)}, f32[512,512]{1,0:T(8,128)S(1)}, u32[]{:S(2)}, u32[]{:S(2)}) collective-permute-start(f32[512,512]{1,0:T(8,128)S(1)} %slice_add_fusion), channel_id=1, source_target_pairs={{0,8},{1,9},{2,10},{3,11},{4,20},{5,21},{6,22},{7,23},{8,0},{9,1},... | collective-permute-start | bytes 3145736 | tf_op jit(solution)/shard_map/ppermute | solution.py:776
  67.9 19.3 %collective-permute-start.35 = (f32[128,768]{1,0:T(8,128)S(1)}, f32[128,768]{1,0:T(8,128)S(1)}, u32[]{:S(2)}, u32[]{:S(2)}) collective-permute-start(f32[128,768]{1,0:T(8,128)S(1)} %slice_add_fusion.7), channel_id=1, source_target_pairs={{0,8},{1,9},{2,10},{3,11},{4,20},{5,21},{6,22},{7,23},{8,0},{9,1},... | collective-permute-start | bytes 1179656 | tf_op jit(solution)/shard_map/ppermute | solution.py:776
  69.3 13.6 %collective-permute-start.36 = (f32[128,512]{1,0:T(8,128)S(1)}, f32[128,512]{1,0:T(8,128)S(1)}, u32[]{:S(2)}, u32[]{:S(2)}) collective-permute-start(f32[128,512]{1,0:T(8,128)S(1)} %slice_add_fusion.17), channel_id=1, source_target_pairs={{0,1},{1,0},{2,3},{3,2},{4,5},{5,4},{6,7},{7,6},{8,9},{9,8},{10,11... | collective-permute-start | bytes 786440 | tf_op jit(solution)/shard_map/ppermute | solution.py:776
  82.3 9.4 %collective-permute-start.34 = (f32[64,3200]{1,0:T(8,128)S(1)}, f32[64,3200]{1,0:T(8,128)S(1)}, u32[]{:S(2)}, u32[]{:S(2)}) collective-permute-start(f32[64,3200]{1,0:T(8,128)S(1)} %get-tuple-element.200), channel_id=1, source_target_pairs={{0,4},{1,5},{2,6},{3,7},{4,0},{5,1},{6,2},{7,3},{8,12},{9,13},{10,... | collective-permute-start | bytes 2457608 | tf_op jit(solution)/shard_map/ppermute | solution.py:776
  82.4 9.2 %collective-permute-start.38 = (f32[256,512]{1,0:T(8,128)S(1)}, f32[256,512]{1,0:T(8,128)S(1)}, u32[]{:S(2)}, u32[]{:S(2)}) collective-permute-start(f32[256,512]{1,0:T(8,128)S(1)} %slice_add_fusion.2), channel_id=1, source_target_pairs={{0,16},{1,17},{2,18},{3,19},{4,12},{5,13},{6,14},{7,15},{8,24},{9,... | collective-permute-start | bytes 1572872 | tf_op jit(solution)/shard_map/ppermute | solution.py:776
  87.2 13.4 %collective-permute-start.40 = (f32[128,512]{1,0:T(8,128)S(1)}, f32[128,512]{1,0:T(8,128)S(1)}, u32[]{:S(2)}, u32[]{:S(2)}) collective-permute-start(f32[128,512]{1,0:T(8,128)S(1)} %fusion.1), channel_id=1, source_target_pairs={{0,2},{1,3},{2,0},{3,1},{4,6},{5,7},{6,4},{7,5},{8,10},{9,11},{10,... | collective-permute-start | bytes 786440 | tf_op jit(solution)/shard_map/ppermute | solution.py:776
  91.8 13.7 %collective-permute-start.39 = (f32[128,512]{1,0:T(8,128)S(1)}, f32[128,512]{1,0:T(8,128)S(1)}, u32[]{:S(2)}, u32[]{:S(2)}) collective-permute-start(f32[128,512]{1,0:T(8,128)S(1)} %slice_add_fusion.8), channel_id=1, source_target_pairs={{0,1},{1,0},{2,3},{3,2},{4,5},{5,4},{6,7},{7,6},{8,9},{9,8},{10,11... | collective-permute-start | bytes 786440 | tf_op jit(solution)/shard_map/ppermute | solution.py:776
  93.4 14.5 %collective-permute-start.37 = (f32[32,3200]{1,0:T(8,128)S(1)}, f32[32,3200]{1,0:T(8,128)S(1)}, u32[]{:S(2)}, u32[]{:S(2)}) collective-permute-start(f32[32,3200]{1,0:T(8,128)S(1)} %slice_add_fusion.6), channel_id=1, source_target_pairs={{0,8},{1,9},{2,10},{3,11},{4,20},{5,21},{6,22},{7,23},{8,0},{9,1},... | collective-permute-start | bytes 1228808 | tf_op jit(solution)/shard_map/ppermute | solution.py:776
  100.6 7.9 %collective-permute-start.44 = (f32[32,768]{1,0:T(8,128)S(1)}, f32[32,768]{1,0:T(8,128)S(1)}, u32[]{:S(2)}, u32[]{:S(2)}) collective-permute-start(f32[32,768]{1,0:T(8,128)S(1)} %slice_add_fusion.33), channel_id=1, source_target_pairs={{0,1},{1,0},{2,3},{3,2},{4,5},{5,4},{6,7},{7,6},{8,9},{9,8},{10,11... | collective-permute-start | bytes 294920 | tf_op jit(solution)/shard_map/ppermute | solution.py:776
  101.3 15.3 %collective-permute-start.43 = (f32[128,512]{1,0:T(8,128)S(1)}, f32[128,512]{1,0:T(8,128)S(1)}, u32[]{:S(2)}, u32[]{:S(2)}) collective-permute-start(f32[128,512]{1,0:T(8,128)S(1)} %add.168), channel_id=1, source_target_pairs={{0,1},{1,0},{2,3},{3,2},{4,5},{5,4},{6,7},{7,6},{8,9},{9,8},{10,11... | collective-permute-start | bytes 786440 | tf_op jit(solution)/shard_map/ppermute | solution.py:776
  105.6 14.5 %collective-permute-start.46 = (f32[128,512]{1,0:T(8,128)S(1)}, f32[128,512]{1,0:T(8,128)S(1)}, u32[]{:S(2)}, u32[]{:S(2)}) collective-permute-start(f32[128,512]{1,0:T(8,128)S(1)} %fusion), channel_id=1, source_target_pairs={{0,2},{1,3},{2,0},{3,1},{4,6},{5,7},{6,4},{7,5},{8,10},{9,11},{10,... | collective-permute-start | bytes 786440 | tf_op jit(solution)/shard_map/ppermute | solution.py:776
  108.0 12.1 %collective-permute-start.42 = (f32[16,3200]{1,0:T(8,128)S(1)}, f32[16,3200]{1,0:T(8,128)S(1)}, u32[]{:S(2)}, u32[]{:S(2)}) collective-permute-start(f32[16,3200]{1,0:T(8,128)S(1)} %slice_add_fusion.20), channel_id=1, source_target_pairs={{0,16},{1,17},{2,18},{3,19},{4,12},{5,13},{6,14},{7,15},{8,24},{9,... | collective-permute-start | bytes 614408 | tf_op jit(solution)/shard_map/ppermute | solution.py:776
  116.6 9.2 %collective-permute-start.47 = (f32[256,512]{1,0:T(8,128)S(1)}, f32[256,512]{1,0:T(8,128)S(1)}, u32[]{:S(2)}, u32[]{:S(2)}) collective-permute-start(f32[256,512]{1,0:T(8,128)S(1)} %pad_maximum_fusion.2), channel_id=1, source_target_pairs={{0,16},{1,17},{2,18},{3,19},{4,12},{5,13},{6,14},{7,15},{8,24},{9,... | collective-permute-start | bytes 1572872 | tf_op jit(solution)/shard_map/ppermute | solution.py:776
  125.9 17.9 %collective-permute-start.52 = (f32[512,512]{1,0:T(8,128)S(1)}, f32[512,512]{1,0:T(8,128)S(1)}, u32[]{:S(2)}, u32[]{:S(2)}) collective-permute-start(f32[512,512]{1,0:T(8,128)S(1)} %pad_maximum_fusion.refs_0_), channel_id=1, source_target_pairs={{0,8},{1,9},{2,10},{3,11},{4,20},{5,21},{6,22},{7,23},{8,0},{9,1},... | collective-permute-start | bytes 3145736 | tf_op jit(solution)/shard_map/ppermute | solution.py:776
  126.5 11.9 %collective-permute-start.49 = (f32[128,512]{1,0:T(8,128)S(1)}, f32[128,512]{1,0:T(8,128)S(1)}, u32[]{:S(2)}, u32[]{:S(2)}) collective-permute-start(f32[128,512]{1,0:T(8,128)S(1)} %add.181), channel_id=1, source_target_pairs={{0,1},{1,0},{2,3},{3,2},{4,5},{5,4},{6,7},{7,6},{8,9},{9,8},{10,11... | collective-permute-start | bytes 786440 | tf_op jit(solution)/shard_map/ppermute | solution.py:776
  126.6 11.8 %collective-permute-start.48 = (f32[8,3200]{1,0:T(8,128)S(1)}, f32[8,3200]{1,0:T(8,128)S(1)}, u32[]{:S(2)}, u32[]{:S(2)}) collective-permute-start(f32[8,3200]{1,0:T(8,128)S(1)} %fusion.2), channel_id=1, source_target_pairs={{0,2},{1,3},{2,0},{3,1},{4,6},{5,7},{6,4},{7,5},{8,10},{9,11},{10,... | collective-permute-start | bytes 307208 | tf_op jit(solution)/shard_map/ppermute | solution.py:776
  128.6 9.4 %collective-permute-start.50 = (f32[32,768]{1,0:T(8,128)S(1)}, f32[32,768]{1,0:T(8,128)S(1)}, u32[]{:S(2)}, u32[]{:S(2)}) collective-permute-start(f32[32,768]{1,0:T(8,128)S(1)} %fusion.3), channel_id=1, source_target_pairs={{0,2},{1,3},{2,0},{3,1},{4,6},{5,7},{6,4},{7,5},{8,10},{9,11},{10,... | collective-permute-start | bytes 294920 | tf_op jit(solution)/shard_map/ppermute | solution.py:776
  138.0 18.5 %collective-permute-start.55 = (f32[512,512]{1,0:T(8,128)S(1)}, f32[512,512]{1,0:T(8,128)S(1)}, u32[]{:S(2)}, u32[]{:S(2)}) collective-permute-start(f32[512,512]{1,0:T(8,128)S(1)} %pad_maximum_fusion.refs_0_), channel_id=1, source_target_pairs={{0,4},{1,5},{2,6},{3,7},{4,0},{5,1},{6,2},{7,3},{8,12},{9,13},{10,... | collective-permute-start | bytes 3145736 | tf_op jit(solution)/shard_map/ppermute | solution.py:776
  138.5 9.2 %collective-permute-start.58 = (f32[256,512]{1,0:T(8,128)S(1)}, f32[256,512]{1,0:T(8,128)S(1)}, u32[]{:S(2)}, u32[]{:S(2)}) collective-permute-start(f32[256,512]{1,0:T(8,128)S(1)} %pad_maximum_fusion.3), channel_id=1, source_target_pairs={{0,16},{1,17},{2,18},{3,19},{4,12},{5,13},{6,14},{7,15},{8,24},{9,... | collective-permute-start | bytes 1572872 | tf_op jit(solution)/shard_map/ppermute | solution.py:776
  143.8 12.6 %collective-permute-start.56 = (f32[512,512]{1,0:T(8,128)S(1)}, f32[512,512]{1,0:T(8,128)S(1)}, u32[]{:S(2)}, u32[]{:S(2)}) collective-permute-start(f32[512,512]{1,0:T(8,128)S(1)} %collective-permute-done.52.refs_1_), channel_id=1, source_target_pairs={{0,4},{1,5},{2,6},{3,7},{4,0},{5,1},{6,2},{7,3},{8,12},{9,13},{10,... | collective-permute-start | bytes 3145736 | tf_op jit(solution)/shard_map/ppermute | solution.py:776
  147.8 16.5 %collective-permute-start.60 = (f32[512,512]{1,0:T(8,128)S(1)}, f32[512,512]{1,0:T(8,128)S(1)}, u32[]{:S(2)}, u32[]{:S(2)}) collective-permute-start(f32[512,512]{1,0:T(8,128)S(1)} %pad_maximum_fusion.1.refs_0_), channel_id=1, source_target_pairs={{0,8},{1,9},{2,10},{3,11},{4,20},{5,21},{6,22},{7,23},{8,0},{9,1},... | collective-permute-start | bytes 3145736 | tf_op jit(solution)/shard_map/ppermute | solution.py:776
  148.4 8.0 %collective-permute-start.54 = (f32[16,3200]{1,0:T(8,128)S(1)}, f32[16,3200]{1,0:T(8,128)S(1)}, u32[]{:S(2)}, u32[]{:S(2)}) collective-permute-start(f32[16,3200]{1,0:T(8,128)S(1)} %pad_maximum_fusion.6), channel_id=1, source_target_pairs={{0,16},{1,17},{2,18},{3,19},{4,12},{5,13},{6,14},{7,15},{8,24},{9,... | collective-permute-start | bytes 614408 | tf_op jit(solution)/shard_map/ppermute | solution.py:776
  149.9 22.2 %collective-permute-start.61 = (f32[512,512]{1,0:T(8,128)S(1)}, f32[512,512]{1,0:T(8,128)S(1)}, u32[]{:S(2)}, u32[]{:S(2)}) collective-permute-start(f32[512,512]{1,0:T(8,128)S(1)} %pad_maximum_fusion.1.refs_0_), channel_id=1, source_target_pairs={{0,4},{1,5},{2,6},{3,7},{4,0},{5,1},{6,2},{7,3},{8,12},{9,13},{10,... | collective-permute-start | bytes 3145736 | tf_op jit(solution)/shard_map/ppermute | solution.py:776
  164.3 8.3 %collective-permute-start.62 = (f32[512,512]{1,0:T(8,128)S(1)}, f32[512,512]{1,0:T(8,128)S(1)}, u32[]{:S(2)}, u32[]{:S(2)}) collective-permute-start(f32[512,512]{1,0:T(8,128)S(1)} %collective-permute-done.60.refs_1_), channel_id=1, source_target_pairs={{0,4},{1,5},{2,6},{3,7},{4,0},{5,1},{6,2},{7,3},{8,12},{9,13},{10,... | collective-permute-start | bytes 3145736 | tf_op jit(solution)/shard_map/ppermute | solution.py:776
  165.0 11.5 %collective-permute-start.59 = (f32[32,3200]{1,0:T(8,128)S(1)}, f32[32,3200]{1,0:T(8,128)S(1)}, u32[]{:S(2)}, u32[]{:S(2)}) collective-permute-start(f32[32,3200]{1,0:T(8,128)S(1)} %pad_maximum_fusion.4.refs_0_), channel_id=1, source_target_pairs={{0,8},{1,9},{2,10},{3,11},{4,20},{5,21},{6,22},{7,23},{8,0},{9,1},... | collective-permute-start | bytes 1228808 | tf_op jit(solution)/shard_map/ppermute | solution.py:776
  166.3 10.1 %collective-permute-start.66 = (f32[128,768]{1,0:T(8,128)S(1)}, f32[128,768]{1,0:T(8,128)S(1)}, u32[]{:S(2)}, u32[]{:S(2)}) collective-permute-start(f32[128,768]{1,0:T(8,128)S(1)} %pad_maximum_fusion.5.refs_0_), channel_id=1, source_target_pairs={{0,4},{1,5},{2,6},{3,7},{4,0},{5,1},{6,2},{7,3},{8,12},{9,13},{10,... | collective-permute-start | bytes 1179656 | tf_op jit(solution)/shard_map/ppermute | solution.py:776
  (42 other events, 184.2 us)

commit v3 on v2

--- a/solution.py
+++ b/solution.py
@@ -608,9 +608,9 @@
     unit_refs, rest = rest[: 2 * len(turn_units)], rest[2 * len(turn_units) :]
     (
         output_ref, grad_ref, states_ref, enter_ref, d_mixed_ref, d_states_ref,
-        skip_grad_ref, back_ends_ref, back_totals_ref,
+        skip_grad_ref, back_ends_ref, back_totals_ref, glu_grad_ref,
         low_ref, mixed_ref, act_ref, gate_ref, result_ref, logits_ref, work_ref, mixed_low_ref,
-        glu_grad_ref, out_grad_ref,
+        out_grad_ref,
     ) = rest
     emit = Emit(turn_units, unit_refs, values_ref.shape[1], tables_ref.shape[1])
     settled_states(
@@ -646,7 +646,7 @@
     layer, length, place_ref, gathered_ref, flags_ref, blocks_ref, tables_ref, gain_ref, skip_ref, in_ref,
     d_states_ref, ends_ref, states_ref, enter_ref, scaled_ref, values_ref, d_mixed_ref, grad_ref,
     out_ref, glu_ref, below_mixed_ref, below_act_ref, below_gate_ref, below_scaled_ref, below_low_ref,
-    *rest,
+    over_grad_ref, *rest,
 ):
     unit_refs, rest = rest[: 2 * len(middle_units)], rest[2 * len(middle_units) :]
     (
@@ -656,6 +656,7 @@
         in_grad_ref, glu_grad_ref, out_grad_ref,
     ) = rest
     emit = Emit(middle_units, unit_refs, values_ref.shape[1], tables_ref.shape[1])
+    emit.put("over", over_grad_ref)
 
     def put_gradient(rows, gradient):
         next_grad_ref[rows, :] = gradient
@@ -720,11 +721,11 @@
 turn_units = (("a", ("out", "glu"), "plane"),)
 middle_units = (("b", ("out", "glu"), "plane"), ("d", ("in",), "plane"))
 last_units = (("c", ("in", "small"), "plane"),)
-after_turn = "=a"
-into_middle = "=a"
-after_middle = "bd =a"
-into_last = "=bda"
-after_last = "bc a d c b d a b c d a c a b c d b c d a c b d A c b d B c"
+after_turn = ("=a",)
+into_middle = ("=a",)
+after_middle = ("bd", "=a")
+into_last = ("=bda",)
+after_last = ("a", "bc", "d", "cb", *"dabcdacadbcbcdacbd", "A", "cb", "d", "B", "c")
 
 
 def mesh_bits():
@@ -874,9 +875,9 @@
     elif keys == ("in",):
         layout = Layout(rows, wide, kind)
         layout.add("in", rows, 0, 0, rows)
-    elif keys == ("glu", "in"):
+    elif keys[1:] == ("in",):
         layout = Layout(rows, model + wide, kind)
-        layout.add("glu", rows, 0, 0, rows, slice(0, model))
+        layout.add(keys[0], rows, 0, 0, rows, slice(0, model))
         layout.add("in", rows, 0, 0, rows, slice(model, model + wide))
     else:
         pieces = rows // 8
@@ -896,6 +897,8 @@
                 self.homes[key] = (layout, refs[2 * index : 2 * index + 2], half_bases(kind))
 
     def put(self, key, array_ref):
+        if key not in self.homes:
+            return
         layout, halves, bases = self.homes[key]
 
         def one(place, carry):
@@ -911,48 +914,109 @@
 run_places = ((0, 0), (0, half_blocks // 2), (1, 0), (1, half_blocks // 2))
 
 
-def place_kernel(layout, goals, *refs):
-    outs = refs[len(refs) - 1 - len(goals) : -1]
-    semaphores = refs[-1]
+def start_places(layout, goals, runs, outs, semaphores):
     bases = half_bases(layout.kind)
     for index, (half, first) in enumerate(run_places):
 
-        def one(place, carry, run=refs[index], half=half, first=first, index=index):
+        def one(place, carry, run=runs[index], half=half, first=first, index=index):
             owner = lax.bitwise_xor(bases[half], first + place)
-            for out, (key, layer) in zip(outs, goals):
+            for key, which, layer in goals:
                 for array_at, block_at in layout.sections[key]:
                     pltpu.make_async_copy(
                         run.at[block_at(place)],
-                        (out if layer is None else out.at[layer]).at[array_at(owner)],
+                        outs[which].at[layer].at[array_at(owner)],
                         semaphores.at[index],
                     ).start()
             return carry
 
         lax.fori_loop(0, half_blocks // 2, one, 0)
-    for index in range(len(run_places)):
-        run = refs[index]
+
+
+def place_kernel(layout, goals, out_count, *refs):
+    runs, semaphores = refs[: len(run_places)], refs[-1]
+    start_places(layout, goals, runs, refs[len(refs) - 1 - out_count : -1], semaphores)
+    for index, run in enumerate(runs):
         pltpu.make_async_copy(run, run, semaphores.at[index]).wait()
 
 
+def finish_kernel(layout, goals, fixed, *refs):
+    runs = refs[: len(run_places)]
+    slopes_ref, unused, out_ref, gain_ref, skip_ref, decay_ref, frequency_ref, step_ref = refs[4:12]
+    small_ref, semaphores = refs[12:]
+    start_places(layout, goals, runs, (out_ref,), semaphores)
+    bases = half_bases(layout.kind)
+    for run, (half, first) in zip(runs, run_places):
+        for place in range(half_blocks // 2):
+            owner = lax.bitwise_xor(bases[half], first + place)
+            for array_at, block_at in layout.sections["small"]:
+                small_ref[array_at(owner)] = run[block_at(place)]
+    row = 0
+    for ref in (gain_ref, skip_ref):
+        for layer in range(ref.shape[0]):
+            for column in range(0, ref.shape[1], lane_count):
+                ref[layer : layer + 1, column : column + lane_count] = small_ref[row : row + 1, :]
+                row += 1
+    layer_count, width = decay_ref.shape
+    steps = width // lane_count
+    for layer in range(layer_count):
+        for piece in range(steps):
+            columns = slice(piece * lane_count, (piece + 1) * lane_count)
+            for index, ref in enumerate((decay_ref, frequency_ref, step_ref)):
+                total = None
+                for member in range(4):
+                    line = row + member * steps + piece
+                    slope = slopes_ref[
+                        (4 * index + member) * layer_count + layer : (4 * index + member) * layer_count
+                        + layer + 1,
+                        columns,
+                    ]
+                    term = slope * small_ref[line : line + 1, :]
+                    total = term if total is None else total + term
+                ref[layer : layer + 1, columns] = total
+        row += 4 * steps
+    for index, run in enumerate(runs):
+        moved = run.at[:, fixed]
+        pltpu.make_async_copy(moved, moved, semaphores.at[index]).wait()
+
+
 def place_unit(runs, layout, goals, shapes, sums):
+    arrays = sorted({array for unused, array, unused_too in goals})
     operands = [("run", run) for run in runs]
     aliases = {}
-    for index, (key, unused) in enumerate(goals):
-        if key in sums:
+    for index, array in enumerate(arrays):
+        if array in sums:
             aliases[len(operands)] = index
-            operands.append(("before", (sums[key], None)))
+            operands.append(("before", (sums[array], None)))
     outs = call(
-        functools.partial(place_kernel, layout, goals),
-        "place_" + "_".join(key for key, unused in goals),
+        functools.partial(
+            place_kernel, layout, [(key, arrays.index(array), layer) for key, array, layer in goals],
+            len(arrays),
+        ),
+        "place_" + "_".join(arrays),
         operands,
-        tuple((shapes[key], f32) for key, unused in goals),
+        tuple((shapes[array], f32) for array in arrays),
         (pltpu.SemaphoreType.DMA((len(run_places),)),),
-        written=range(len(goals)),
+        written=range(len(arrays)),
         aliases=aliases,
         plain=True,
     )
-    for (key, unused), out in zip(goals, outs):
-        sums[key] = out
+    sums.update(zip(arrays, outs))
+
+
+def finish_unit(runs, layout, slopes, shape, before, vectors, small_out):
+    return call(
+        functools.partial(
+            finish_kernel, layout, [("in", 0, 0)], slice(0, layout.columns - lane_count)
+        ),
+        "place_last",
+        [("run", run) for run in runs] + [("slopes", slopes), ("before", (before, None))],
+        ((shape, f32),) + tuple((each, f32) for each in vectors),
+        (small_out, pltpu.SemaphoreType.DMA((len(run_places),))),
+        written=(0,),
+        final=range(1, 1 + len(vectors)),
+        aliases={len(runs) + 1: 0},
+        plain=True,
+    )
 
 
 class Fetch:
@@ -1069,6 +1133,14 @@
     place = lax.axis_index("seq").astype(jnp.int32).reshape(1)
     rate_tables, rates_back = jax.vjp(rates, decay_log, frequency, step_log)
     tables = jnp.stack(rate_tables, axis=1).reshape(4 * layer_count, width)
+    none = jnp.zeros((layer_count, width), f32)
+    by_rate = [
+        rates_back(tuple(none + 1.0 if member == rate else none for member in range(4)))
+        for rate in range(4)
+    ]
+    slopes = jnp.concatenate(
+        [by_rate[rate][parameter] for parameter in range(3) for rate in range(4)], axis=0
+    )
 
     def gather(totals):
         if device_count != 8:
@@ -1172,7 +1244,7 @@
     def open_units(entries, halves, layer_of):
         for index, (name, keys, kind) in enumerate(entries):
             units[name] = UnitSum(halves[2 * index], halves[2 * index + 1], kind)
-            goals[name] = [(key, layer_of[key]) for key in keys]
+            goals[name] = [(key, "glu" if key == "over" else key, layer_of[key]) for key in keys]
 
     placed = set()
 
@@ -1180,10 +1252,10 @@
         placed.add(name)
         runs = line.settle(units[name].runs)
         place_unit(runs, layouts[name], goals[name], shapes, sums)
-        line.last = [sums[key] for key, unused in goals[name]]
+        line.last = [sums[array] for unused, array, unused_too in goals[name]]
 
     def follow(plan, payload=()):
-        for group in plan.split():
+        for group in plan:
             if group.isupper():
                 for name in group.lower():
                     if units[name].runs is not None and name not in placed:
@@ -1212,17 +1284,17 @@
         ),
         (
             *unit_outs(turn_units), (inputs.shape, bf16), tokens, wide_out, ends_out, tokens, wide_out,
-            vector, ends_out, totals_out,
+            vector, ends_out, totals_out, glu_out,
         ),
         (
             ((count, 4 * width), bf16), tokens, tokens_low, tokens, tokens_low, tokens_low, tokens,
-            tokens_low, glu_out, out_out,
+            tokens_low, out_out,
         ),
         final=(2 * len(turn_units),),
         micros=6,
     )
     halves, results = results[: 2 * len(turn_units)], results[2 * len(turn_units) :]
-    output, grad, states, enter, d_mixed, d_states, skip_grad, ends, totals = results
+    output, grad, states, enter, d_mixed, d_states, skip_grad, ends, totals, over_grad = results
     open_units(turn_units, halves, {"out": layer, "glu": layer})
     gathered = follow(into_middle, gather(follow(after_turn, totals)))
     back_scratch = (
@@ -1255,6 +1327,7 @@
             ("gate", gate),
             ("below_scaled", low_scaled),
             ("low", low),
+            ("over", over_grad),
         ),
         (
             *unit_outs(middle_units), vector, rate_out, tokens, tokens, wide_out, vector, ends_out,
@@ -1265,7 +1338,7 @@
     )
     halves, results = results[: 2 * len(middle_units)], results[2 * len(middle_units) :]
     gain_grad, rate_grad, grad, d_mixed, d_states, low_skip_grad, ends, totals = results
-    open_units(middle_units, halves, {"out": layer - 1, "glu": layer - 1, "in": layer})
+    open_units(middle_units, halves, {"out": layer - 1, "glu": layer - 1, "over": layer, "in": layer})
     gathered = follow(into_last, gather(follow(after_middle, totals)))
     keep, send, input_grad = call(
         functools.partial(back_last_kernel, length),
@@ -1301,19 +1374,12 @@
         while unit.runs is None:
             follow(name)
     for name in units:
-        if name not in placed:
+        if name not in placed and name != last_units[0][0]:
             place_sums(name)
-    small = sums["small"]
-
-    def taken(first, shape):
-        rows = math.prod(shape) // lane_count
-        return small[first : first + rows].reshape(shape), first + rows
-
-    gain_sum, row = taken(0, (layer_count, model))
-    skip_sum, row = taken(row, (layer_count, model))
-    rate_sum, row = taken(row, (layer_count, 4, width))
-    decay_grad, frequency_grad, step_grad = rates_back(
-        tuple(rate_sum[:, member] for member in range(4))
+    name = last_units[0][0]
+    in_sum, gain_sum, skip_sum, decay_grad, frequency_grad, step_grad = finish_unit(
+        line.settle(units[name].runs), layouts[name], slopes, shapes["in"], sums["in"],
+        ((layer_count, model),) * 2 + ((layer_count, width),) * 3, small_out,
     )
     return (
         output,
@@ -1322,7 +1388,7 @@
         decay_grad,
         frequency_grad,
         step_grad,
-        sums["in"],
+        in_sum,
         skip_sum,
         sums["out"],
         sums["glu"],

time: 182 us -> 178 us (0.978)
  waiting for transfers between devices: 96.4 us -> 90 us
  starting transfers between devices: 49.4 us -> 53 us
    ppermute x40, waiting for transfers between devices: 80.6 us -> 74.3 us  [swap(): return lax.ppermute(array, ('seq', 'batch'), pairs)]
    ppermute x40, starting transfers between devices: 29.1 us -> 32.7 us  [swap(): return lax.ppermute(array, ('seq', 'batch'), pairs)]
  transfers between devices with their start and end apart: 68 -> 68, of which waited for: 37 -> 40; matrix products, arithmetic and copies ran while one was open for 1% -> 1% of each run, Pallas kernels for 8% -> 9%
where the time goes in v3:
time: 178 us
  waiting for transfers between devices  90 us (51%)
  starting transfers between devices  53 us (30%)
  Pallas kernels  30.3 us (17%)
  other arithmetic  2.99 us (2%)
    ppermute x40, waiting for transfers between devices, swap(): return lax.ppermute(array, ('seq', 'batch'), pairs)  74.3 us
    ppermute x40, starting transfers between devices, swap(): return lax.ppermute(array, ('seq', 'batch'), pairs)  32.7 us
    pallas_call x9, Pallas kernels, call(): pl.pallas_call(kernel, name=name, in_specs=specs, out_specs=[pl.BlockSpec...  30.3 us
    ppermute x28, starting transfers between devices, from_other(): lax.ppermute(array, 'seq', [(index, index ^ bits) for index in range(devi...  20.3 us
    ppermute x28, waiting for transfers between devices, from_other(): lax.ppermute(array, 'seq', [(index, index ^ bits) for index in range(devi...  15.8 us
  transfers between devices with their start and end apart: 68, of which 40 were waited for; matrix products, arithmetic and copies ran while one was open for 1% of the time, Pallas kernels for 9%

profile of v3, /device:TPU:0, one launch (start us, length us, event | category | flops | bytes accessed | tf_op | source)
XLA Modules:
  0.0 177.7 jit_solution(13303650430911900916)
XLA Ops:
  1.6 3.2 %first.1 = (f32[3,256,128]{2,1,0:T(8,128)S(1)}, f32[2,16,128]{2,1,0:T(8,128)S(1)}, bf16[256,512]{1,0:T(8,128)(2,1)S(1)}, bf16[256,512]{1,0:T(8,128)(2,1)S(1)}, f...) custom-call(s32[1]{0:T(128)} %bitcast.refs_0_, s32[2,8]{1,0:T(2,128)} %refs_1_.1, ...), custom_call_target="tpu_custom_call" | custom-call | flops 4000000000 | bytes 14400000 | tf_op jit(solution)/shard_map/first/pallas_call | solution.py:1088
  4.8 3.0 %collective-permute-start.1 = (f32[8,384]{1,0:T(8,128)S(1)}, f32[8,384]{1,0:T(8,128)S(1)}, u32[]{:S(2)}, u32[]{:S(2)}) collective-permute-start(f32[8,384]{1,0:T(8,128)S(1)} %get-tuple-element.135.refs_1_), channel_id=1, source_target_pairs={{0,8},{4,12},{8,0},{12,4},{16,24},{20,28},{24,16},{28,20},{1,9},{5... | collective-permute-start | bytes 36872 | tf_op jit(solution)/shard_map/ppermute | solution.py:1150
  11.5 2.4 %collective-permute-done.5.refs_7_ = f32[8,384]{1,0:T(8,128)S(1)} collective-permute-done((f32[8,384]{1,0:T(8,128)S(1)}, f32[8,384]{1,0:T(8,128)S(1)}, u32[]{:S(2)}, u32[]{:S(2)}) %collective-permute-start.5) | collective-permute-done | bytes 12320 | tf_op jit(solution)/shard_map/ppermute | solution.py:1150
  15.1 3.8 %middle.1 = (f32[256,1536]{1,0:T(8,128)S(1)}, bf16[256,1536]{1,0:T(8,128)(2,1)S(1)}, f32[8,1536]{1,0:T(8,128)S(1)}, f32[256,512]{1,0:T(8,128)S(1)}, bf16[256,512...) custom-call(s32[1]{0:T(128)} %bitcast.refs_0_, ...), custom_call_target="tpu_custom_call" | custom-call | flops 4000000000 | bytes 14400000 | tf_op jit(solution)/shard_map/middle/pallas_call | solution.py:1088
  19.6 2.9 %collective-permute-start.12 = (f32[8,384]{1,0:T(8,128)S(1)}, f32[8,384]{1,0:T(8,128)S(1)}, u32[]{:S(2)}, u32[]{:S(2)}) collective-permute-start(f32[8,384]{1,0:T(8,128)S(1)} %get-tuple-element.142.refs_1_), channel_id=1, source_target_pairs={{0,24},{4,28},{8,16},{12,20},{16,8},{20,12},{24,0},{28,4},{1,25},{... | collective-permute-start | bytes 36872 | tf_op jit(solution)/shard_map/ppermute | solution.py:1150
  25.4 6.2 %turn.1 = (f32[1024,512]{1,0:T(8,128)S(1)}, f32[1024,512]{1,0:T(8,128)S(1)}, bf16[2,128,512]{2,1,0:T(8,128)(2,1)}, f32[256,512]{1,0:T(8,128)S(1)}, f32[256,1536]...) custom-call(s32[1]{0:T(128)} %bitcast.refs_0_, ...), custom_call_target="tpu_custom_call" | custom-call | flops 6000000000 | bytes 21600000 | tf_op jit(solution)/shard_map/turn/pallas_call | solution.py:1088
  31.9 1.9 %collective-permute-start.16 = (f32[8,384]{1,0:T(8,128)S(1)}, f32[8,384]{1,0:T(8,128)S(1)}, u32[]{:S(2)}, u32[]{:S(2)}) collective-permute-start(f32[8,384]{1,0:T(8,128)S(1)} %get-tuple-element.153.refs_1_), channel_id=1, source_target_pairs={{0,8},{4,12},{8,0},{12,4},{16,24},{20,28},{24,16},{28,20},{1,9},{5... | collective-permute-start | bytes 36872 | tf_op jit(solution)/shard_map/ppermute | solution.py:1150
  37.5 2.4 %collective-permute-done.20.refs_7_ = f32[8,384]{1,0:T(8,128)S(1)} collective-permute-done((f32[8,384]{1,0:T(8,128)S(1)}, f32[8,384]{1,0:T(8,128)S(1)}, u32[]{:S(2)}, u32[]{:S(2)}) %collective-permute-start.20) | collective-permute-done | bytes 12320 | tf_op jit(solution)/shard_map/ppermute | solution.py:1150
  41.6 6.1 %back_middle.1 = (f32[1024,512]{1,0:T(8,128)S(1)}, f32[1024,512]{1,0:T(8,128)S(1)}, f32[256,768]{1,0:T(8,128)S(1)}, f32[256,768]{1,0:T(8,128)S(1)}, f32[1,512]{1...) custom-call(s32[1]{0:T(128)} %bitcast.refs_0_, ...), custom_call_target="tpu_custom_call" | custom-call | flops 6000000000 | bytes 21600000 | tf_op jit(solution)/shard_map/back_middle/pallas_call | solution.py:1088
  48.3 7.6 %collective-permute-done.24 = f32[512,512]{1,0:T(8,128)S(1)} collective-permute-done((f32[512,512]{1,0:T(8,128)S(1)}, f32[512,512]{1,0:T(8,128)S(1)}, u32[]{:S(2)}, u32[]{:S(2)}) %collective-permute-start.24) | collective-permute-done | bytes 1048608 | tf_op jit(solution)/shard_map/ppermute | solution.py:777
  56.7 1.9 %collective-permute-start.29 = (f32[8,384]{1,0:T(8,128)S(1)}, f32[8,384]{1,0:T(8,128)S(1)}, u32[]{:S(2)}, u32[]{:S(2)}) collective-permute-start(f32[8,384]{1,0:T(8,128)S(1)} %get-tuple-element.182.refs_1_), channel_id=1, source_target_pairs={{0,16},{4,20},{8,24},{12,28},{16,0},{20,4},{24,8},{28,12},{1,17},{... | collective-permute-start | bytes 36872 | tf_op jit(solution)/shard_map/ppermute | solution.py:1150
  60.5 3.6 %collective-permute-start.26 = (f32[8,384]{1,0:T(8,128)S(1)}, f32[8,384]{1,0:T(8,128)S(1)}, u32[]{:S(2)}, u32[]{:S(2)}) collective-permute-start(f32[8,384]{1,0:T(8,128)S(1)} %get-tuple-element.182.refs_1_), channel_id=1, source_target_pairs={{0,4},{4,0},{8,12},{12,8},{16,20},{20,16},{24,28},{28,24},{1,5},{5... | collective-permute-start | bytes 36872 | tf_op jit(solution)/shard_map/ppermute | solution.py:1150
  71.0 4.0 %back_last.1 = (f32[64,3200]{1,0:T(8,128)S(1)}, f32[64,3200]{1,0:T(8,128)S(1)}, bf16[2,128,512]{2,1,0:T(8,128)(2,1)}) custom-call(s32[1]{0:T(128)} %bitcast.refs_0_, f32[8,384]{1,0:T(8,128)S(1)} %get-tuple-element.182.refs_1_, f32[8,384]{1,0:T(8,128)S(1)} %collective-permute-done.26.refs_2_, f32[8,384]{1,0:T(8,128)S(1)} %collective-permute-done.27.refs_3_, ...), custom_call_target="tpu_custom_call" | custom-call | flops 4000000000 | bytes 14400000 | tf_op jit(solution)/shard_map/back_last/pallas_call | solution.py:1088
  76.1 6.1 %collective-permute-done.33 = f32[512,512]{1,0:T(8,128)S(1)} collective-permute-done((f32[512,512]{1,0:T(8,128)S(1)}, f32[512,512]{1,0:T(8,128)S(1)}, u32[]{:S(2)}, u32[]{:S(2)}) %collective-permute-start.33) | collective-permute-done | bytes 1048608 | tf_op jit(solution)/shard_map/ppermute | solution.py:777
  83.0 2.6 %collective-permute-start.40 = (f32[128,512]{1,0:T(8,128)S(1)}, f32[128,512]{1,0:T(8,128)S(1)}, u32[]{:S(2)}, u32[]{:S(2)}) collective-permute-start(f32[128,512]{1,0:T(8,128)S(1)} %fusion.1), channel_id=1, source_target_pairs={{0,2},{1,3},{2,0},{3,1},{4,6},{5,7},{6,4},{7,5},{8,10},{9,11},{10,... | collective-permute-start | bytes 786440 | tf_op jit(solution)/shard_map/ppermute | solution.py:777
  87.8 3.9 %collective-permute-done.36 = f32[256,512]{1,0:T(8,128)S(1)} collective-permute-done((f32[256,512]{1,0:T(8,128)S(1)}, f32[256,512]{1,0:T(8,128)S(1)}, u32[]{:S(2)}, u32[]{:S(2)}) %collective-permute-start.36) | collective-permute-done | bytes 524320 | tf_op jit(solution)/shard_map/ppermute | solution.py:777
  93.5 4.5 %collective-permute-done.40 = f32[128,512]{1,0:T(8,128)S(1)} collective-permute-done((f32[128,512]{1,0:T(8,128)S(1)}, f32[128,512]{1,0:T(8,128)S(1)}, u32[]{:S(2)}, u32[]{:S(2)}) %collective-permute-start.40) | collective-permute-done | bytes 262176 | tf_op jit(solution)/shard_map/ppermute | solution.py:777
  100.8 2.7 %collective-permute-done.39 = f32[128,512]{1,0:T(8,128)S(1)} collective-permute-done((f32[128,512]{1,0:T(8,128)S(1)}, f32[128,512]{1,0:T(8,128)S(1)}, u32[]{:S(2)}, u32[]{:S(2)}) %collective-permute-start.39) | collective-permute-done | bytes 262176 | tf_op jit(solution)/shard_map/ppermute | solution.py:777
  107.4 7.5 %collective-permute-done.43 = f32[128,512]{1,0:T(8,128)S(1)} collective-permute-done((f32[128,512]{1,0:T(8,128)S(1)}, f32[128,512]{1,0:T(8,128)S(1)}, u32[]{:S(2)}, u32[]{:S(2)}) %collective-permute-start.43) | collective-permute-done | bytes 262176 | tf_op jit(solution)/shard_map/ppermute | solution.py:777
  116.2 6.6 %collective-permute-done.47 = f32[32,768]{1,0:T(8,128)S(1)} collective-permute-done((f32[32,768]{1,0:T(8,128)S(1)}, f32[32,768]{1,0:T(8,128)S(1)}, u32[]{:S(2)}, u32[]{:S(2)}) %collective-permute-start.47) | collective-permute-done | bytes 98336 | tf_op jit(solution)/shard_map/ppermute | solution.py:777
  126.1 2.2 %collective-permute-done.45 = f32[8,3200]{1,0:T(8,128)S(1)} collective-permute-done((f32[8,3200]{1,0:T(8,128)S(1)}, f32[8,3200]{1,0:T(8,128)S(1)}, u32[]{:S(2)}, u32[]{:S(2)}) %collective-permute-start.45) | collective-permute-done | bytes 102432 | tf_op jit(solution)/shard_map/ppermute | solution.py:777
  130.0 2.5 %collective-permute-start.53 = (f32[32,768]{1,0:T(8,128)S(1)}, f32[32,768]{1,0:T(8,128)S(1)}, u32[]{:S(2)}, u32[]{:S(2)}) collective-permute-start(f32[32,768]{1,0:T(8,128)S(1)} %add.182), channel_id=1, source_target_pairs={{0,1},{1,0},{2,3},{3,2},{4,5},{5,4},{6,7},{7,6},{8,9},{9,8},{10,11... | collective-permute-start | bytes 294920 | tf_op jit(solution)/shard_map/ppermute | solution.py:777
  132.5 2.2 %collective-permute-done.49 = f32[8,3200]{1,0:T(8,128)S(1)} collective-permute-done((f32[8,3200]{1,0:T(8,128)S(1)}, f32[8,3200]{1,0:T(8,128)S(1)}, u32[]{:S(2)}, u32[]{:S(2)}) %collective-permute-start.49) | collective-permute-done | bytes 102432 | tf_op jit(solution)/shard_map/ppermute | solution.py:777
  134.8 1.7 collective-permute-done.50
  137.1 2.4 %collective-permute-start.51 = (f32[8,3200]{1,0:T(8,128)S(1)}, f32[8,3200]{1,0:T(8,128)S(1)}, u32[]{:S(2)}, u32[]{:S(2)}) collective-permute-start(f32[8,3200]{1,0:T(8,128)S(1)} %add.183), channel_id=1, source_target_pairs={{0,1},{1,0},{2,3},{3,2},{4,5},{5,4},{6,7},{7,6},{8,9},{9,8},{10,11... | collective-permute-start | bytes 307208 | tf_op jit(solution)/shard_map/ppermute | solution.py:777
  142.2 3.6 %collective-permute-done.55 = f32[256,512]{1,0:T(8,128)S(1)} collective-permute-done((f32[256,512]{1,0:T(8,128)S(1)}, f32[256,512]{1,0:T(8,128)S(1)}, u32[]{:S(2)}, u32[]{:S(2)}) %collective-permute-start.55) | collective-permute-done | bytes 524320 | tf_op jit(solution)/shard_map/ppermute | solution.py:777
  148.2 6.7 %collective-permute-done.54 = f32[16,3200]{1,0:T(8,128)S(1)} collective-permute-done((f32[16,3200]{1,0:T(8,128)S(1)}, f32[16,3200]{1,0:T(8,128)S(1)}, u32[]{:S(2)}, u32[]{:S(2)}) %collective-permute-start.54) | collective-permute-done | bytes 204832 | tf_op jit(solution)/shard_map/ppermute | solution.py:777
  155.0 2.0 %place_glu_out.2 = (f32[2,512,512]{2,1,0:T(8,128)}, f32[2,1536,512]{2,1,0:T(8,128)}) custom-call(f32[512,512]{1,0:T(8,128)S(1)} %pad_maximum_fusion.refs_0_, f32[512,512]{1,0:T(8,128)S(1)} %collective-permute-done.52.refs_1_, f32[512,512]{1,0:T(8,128)S(1)} %collective-permute-done.57.refs_2_, f32[512,512]{1,0:T(8,128)S(1)} %collective-permute-done.58.refs_3_), custom_call_target="tpu_custom_call" | custom-call | flops 4000000000 | bytes 14400000 | tf_op jit(solution)/shard_map/place_glu_out/pallas_call | solution.py:1088
  157.1 4.8 %collective-permute-done.56.refs_1_ = f32[512,512]{1,0:T(8,128)S(1)} collective-permute-done((f32[512,512]{1,0:T(8,128)S(1)}, f32[512,512]{1,0:T(8,128)S(1)}, u32[]{:S(2)}, u32[]{:S(2)}) %collective-permute-start.56) | collective-permute-done | bytes 1048608 | tf_op jit(solution)/shard_map/ppermute | solution.py:777
  164.1 5.5 %collective-permute-done.63.refs_1_ = f32[128,768]{1,0:T(8,128)S(1)} collective-permute-done((f32[128,768]{1,0:T(8,128)S(1)}, f32[128,768]{1,0:T(8,128)S(1)}, u32[]{:S(2)}, u32[]{:S(2)}) %collective-permute-start.63) | collective-permute-done | bytes 393248 | tf_op jit(solution)/shard_map/ppermute | solution.py:777
  170.2 2.0 %place_glu_out.3 = (f32[2,512,512]{2,1,0:T(8,128)}, f32[2,1536,512]{2,1,0:T(8,128)}) custom-call(f32[512,512]{1,0:T(8,128)S(1)} %pad_maximum_fusion.1.refs_0_, f32[512,512]{1,0:T(8,128)S(1)} %collective-permute-done.56.refs_1_, f32[512,512]{1,0:T(8,128)S(1)} %collective-permute-done.61.refs_2_, ...), custom_call_target="tpu_custom_call", output_to_operand_aliasing={{0}: (4, {}), {1}: (5, {})} | custom-call | flops 4000000000 | bytes 14400000 | tf_op jit(solution)/shard_map/place_glu_out/pallas_call | solution.py:1088
  172.2 1.9 %collective-permute-done.60.refs_1_ = f32[32,3200]{1,0:T(8,128)S(1)} collective-permute-done((f32[32,3200]{1,0:T(8,128)S(1)}, f32[32,3200]{1,0:T(8,128)S(1)}, u32[]{:S(2)}, u32[]{:S(2)}) %collective-permute-start.60) | collective-permute-done | bytes 409632 | tf_op jit(solution)/shard_map/ppermute | solution.py:777
  (160 shorter events, 55.6 us)
Async XLA Ops:
  31.6 8.3 %collective-permute-start.14 = (f32[1024,512]{1,0:T(8,128)S(1)}, f32[1024,512]{1,0:T(8,128)S(1)}, u32[]{:S(2)}, u32[]{:S(2)}) collective-permute-start(f32[1024,512]{1,0:T(8,128)S(1)} %get-tuple-element.151), channel_id=1, source_target_pairs={{0,4},{1,5},{2,6},{3,7},{4,0},{5,1},{6,2},{7,3},{8,12},{9,13},{10,... | collective-permute-start | bytes 6291464 | tf_op jit(solution)/shard_map/ppermute | solution.py:777
  41.1 14.8 %collective-permute-start.24 = (f32[512,512]{1,0:T(8,128)S(1)}, f32[512,512]{1,0:T(8,128)S(1)}, u32[]{:S(2)}, u32[]{:S(2)}) collective-permute-start(f32[512,512]{1,0:T(8,128)S(1)} %slice_add_fusion.1), channel_id=1, source_target_pairs={{0,8},{1,9},{2,10},{3,11},{4,20},{5,21},{6,22},{7,23},{8,0},{9,1},... | collective-permute-start | bytes 3145736 | tf_op jit(solution)/shard_map/ppermute | solution.py:777
  47.7 18.7 %collective-permute-start.22 = (f32[1024,512]{1,0:T(8,128)S(1)}, f32[1024,512]{1,0:T(8,128)S(1)}, u32[]{:S(2)}, u32[]{:S(2)}) collective-permute-start(f32[1024,512]{1,0:T(8,128)S(1)} %get-tuple-element.176), channel_id=1, source_target_pairs={{0,4},{1,5},{2,6},{3,7},{4,0},{5,1},{6,2},{7,3},{8,12},{9,13},{10,... | collective-permute-start | bytes 6291464 | tf_op jit(solution)/shard_map/ppermute | solution.py:777
  47.8 10.9 %collective-permute-start.23 = (f32[256,768]{1,0:T(8,128)S(1)}, f32[256,768]{1,0:T(8,128)S(1)}, u32[]{:S(2)}, u32[]{:S(2)}) collective-permute-start(f32[256,768]{1,0:T(8,128)S(1)} %get-tuple-element.178), channel_id=1, source_target_pairs={{0,4},{1,5},{2,6},{3,7},{4,0},{5,1},{6,2},{7,3},{8,12},{9,13},{10,... | collective-permute-start | bytes 2359304 | tf_op jit(solution)/shard_map/ppermute | solution.py:777
  56.1 10.2 %collective-permute-start.25 = (f32[256,512]{1,0:T(8,128)S(1)}, f32[256,512]{1,0:T(8,128)S(1)}, u32[]{:S(2)}, u32[]{:S(2)}) collective-permute-start(f32[256,512]{1,0:T(8,128)S(1)} %slice_add_fusion.4), channel_id=1, source_target_pairs={{0,16},{1,17},{2,18},{3,19},{4,12},{5,13},{6,14},{7,15},{8,24},{9,... | collective-permute-start | bytes 1572872 | tf_op jit(solution)/shard_map/ppermute | solution.py:777
  56.7 9.0 %collective-permute-start.29 = (f32[8,384]{1,0:T(8,128)S(1)}, f32[8,384]{1,0:T(8,128)S(1)}, u32[]{:S(2)}, u32[]{:S(2)}) collective-permute-start(f32[8,384]{1,0:T(8,128)S(1)} %get-tuple-element.182.refs_1_), channel_id=1, source_target_pairs={{0,16},{4,20},{8,24},{12,28},{16,0},{20,4},{24,8},{28,12},{1,17},{... | collective-permute-start | bytes 36872 | tf_op jit(solution)/shard_map/ppermute | solution.py:1150
  67.4 14.8 %collective-permute-start.33 = (f32[512,512]{1,0:T(8,128)S(1)}, f32[512,512]{1,0:T(8,128)S(1)}, u32[]{:S(2)}, u32[]{:S(2)}) collective-permute-start(f32[512,512]{1,0:T(8,128)S(1)} %slice_add_fusion), channel_id=1, source_target_pairs={{0,8},{1,9},{2,10},{3,11},{4,20},{5,21},{6,22},{7,23},{8,0},{9,1},... | collective-permute-start | bytes 3145736 | tf_op jit(solution)/shard_map/ppermute | solution.py:777
  67.9 8.1 %collective-permute-start.34 = (f32[128,512]{1,0:T(8,128)S(1)}, f32[128,512]{1,0:T(8,128)S(1)}, u32[]{:S(2)}, u32[]{:S(2)}) collective-permute-start(f32[128,512]{1,0:T(8,128)S(1)} %slice_add_fusion.17), channel_id=1, source_target_pairs={{0,1},{1,0},{2,3},{3,2},{4,5},{5,4},{6,7},{7,6},{8,9},{9,8},{10,11... | collective-permute-start | bytes 786440 | tf_op jit(solution)/shard_map/ppermute | solution.py:777
  69.5 17.7 %collective-permute-start.37 = (f32[128,768]{1,0:T(8,128)S(1)}, f32[128,768]{1,0:T(8,128)S(1)}, u32[]{:S(2)}, u32[]{:S(2)}) collective-permute-start(f32[128,768]{1,0:T(8,128)S(1)} %slice_add_fusion.7), channel_id=1, source_target_pairs={{0,8},{1,9},{2,10},{3,11},{4,20},{5,21},{6,22},{7,23},{8,0},{9,1},... | collective-permute-start | bytes 1179656 | tf_op jit(solution)/shard_map/ppermute | solution.py:777
  82.4 9.4 %collective-permute-start.35 = (f32[64,3200]{1,0:T(8,128)S(1)}, f32[64,3200]{1,0:T(8,128)S(1)}, u32[]{:S(2)}, u32[]{:S(2)}) collective-permute-start(f32[64,3200]{1,0:T(8,128)S(1)} %get-tuple-element.207), channel_id=1, source_target_pairs={{0,4},{1,5},{2,6},{3,7},{4,0},{5,1},{6,2},{7,3},{8,12},{9,13},{10,... | collective-permute-start | bytes 2457608 | tf_op jit(solution)/shard_map/ppermute | solution.py:777
  82.4 9.2 %collective-permute-start.36 = (f32[256,512]{1,0:T(8,128)S(1)}, f32[256,512]{1,0:T(8,128)S(1)}, u32[]{:S(2)}, u32[]{:S(2)}) collective-permute-start(f32[256,512]{1,0:T(8,128)S(1)} %slice_add_fusion.2), channel_id=1, source_target_pairs={{0,16},{1,17},{2,18},{3,19},{4,12},{5,13},{6,14},{7,15},{8,24},{9,... | collective-permute-start | bytes 1572872 | tf_op jit(solution)/shard_map/ppermute | solution.py:777
  83.0 15.0 %collective-permute-start.40 = (f32[128,512]{1,0:T(8,128)S(1)}, f32[128,512]{1,0:T(8,128)S(1)}, u32[]{:S(2)}, u32[]{:S(2)}) collective-permute-start(f32[128,512]{1,0:T(8,128)S(1)} %fusion.1), channel_id=1, source_target_pairs={{0,2},{1,3},{2,0},{3,1},{4,6},{5,7},{6,4},{7,5},{8,10},{9,11},{10,... | collective-permute-start | bytes 786440 | tf_op jit(solution)/shard_map/ppermute | solution.py:777
  87.3 11.5 %collective-permute-start.41 = (f32[64,768]{1,0:T(8,128)S(1)}, f32[64,768]{1,0:T(8,128)S(1)}, u32[]{:S(2)}, u32[]{:S(2)}) collective-permute-start(f32[64,768]{1,0:T(8,128)S(1)} %slice_add_fusion.22), channel_id=1, source_target_pairs={{0,16},{1,17},{2,18},{3,19},{4,12},{5,13},{6,14},{7,15},{8,24},{9,... | collective-permute-start | bytes 589832 | tf_op jit(solution)/shard_map/ppermute | solution.py:777
  91.9 11.7 %collective-permute-start.39 = (f32[128,512]{1,0:T(8,128)S(1)}, f32[128,512]{1,0:T(8,128)S(1)}, u32[]{:S(2)}, u32[]{:S(2)}) collective-permute-start(f32[128,512]{1,0:T(8,128)S(1)} %slice_add_fusion.11), channel_id=1, source_target_pairs={{0,1},{1,0},{2,3},{3,2},{4,5},{5,4},{6,7},{7,6},{8,9},{9,8},{10,11... | collective-permute-start | bytes 786440 | tf_op jit(solution)/shard_map/ppermute | solution.py:777
  98.1 8.0 %collective-permute-start.38 = (f32[32,3200]{1,0:T(8,128)S(1)}, f32[32,3200]{1,0:T(8,128)S(1)}, u32[]{:S(2)}, u32[]{:S(2)}) collective-permute-start(f32[32,3200]{1,0:T(8,128)S(1)} %slice_add_fusion.6), channel_id=1, source_target_pairs={{0,8},{1,9},{2,10},{3,11},{4,20},{5,21},{6,22},{7,23},{8,0},{9,1},... | collective-permute-start | bytes 1228808 | tf_op jit(solution)/shard_map/ppermute | solution.py:777
  100.2 14.8 %collective-permute-start.43 = (f32[128,512]{1,0:T(8,128)S(1)}, f32[128,512]{1,0:T(8,128)S(1)}, u32[]{:S(2)}, u32[]{:S(2)}) collective-permute-start(f32[128,512]{1,0:T(8,128)S(1)} %add.168), channel_id=1, source_target_pairs={{0,1},{1,0},{2,3},{3,2},{4,5},{5,4},{6,7},{7,6},{8,9},{9,8},{10,11... | collective-permute-start | bytes 786440 | tf_op jit(solution)/shard_map/ppermute | solution.py:777
  103.7 19.1 %collective-permute-start.46 = (f32[128,512]{1,0:T(8,128)S(1)}, f32[128,512]{1,0:T(8,128)S(1)}, u32[]{:S(2)}, u32[]{:S(2)}) collective-permute-start(f32[128,512]{1,0:T(8,128)S(1)} %fusion), channel_id=1, source_target_pairs={{0,2},{1,3},{2,0},{3,1},{4,6},{5,7},{6,4},{7,5},{8,10},{9,11},{10,... | collective-permute-start | bytes 786440 | tf_op jit(solution)/shard_map/ppermute | solution.py:777
  106.1 16.7 %collective-permute-start.42 = (f32[16,3200]{1,0:T(8,128)S(1)}, f32[16,3200]{1,0:T(8,128)S(1)}, u32[]{:S(2)}, u32[]{:S(2)}) collective-permute-start(f32[16,3200]{1,0:T(8,128)S(1)} %slice_add_fusion.20), channel_id=1, source_target_pairs={{0,16},{1,17},{2,18},{3,19},{4,12},{5,13},{6,14},{7,15},{8,24},{9,... | collective-permute-start | bytes 614408 | tf_op jit(solution)/shard_map/ppermute | solution.py:777
  106.7 16.1 %collective-permute-start.47 = (f32[32,768]{1,0:T(8,128)S(1)}, f32[32,768]{1,0:T(8,128)S(1)}, u32[]{:S(2)}, u32[]{:S(2)}) collective-permute-start(f32[32,768]{1,0:T(8,128)S(1)} %fusion.3), channel_id=1, source_target_pairs={{0,2},{1,3},{2,0},{3,1},{4,6},{5,7},{6,4},{7,5},{8,10},{9,11},{10,... | collective-permute-start | bytes 294920 | tf_op jit(solution)/shard_map/ppermute | solution.py:777
  115.0 9.2 %collective-permute-start.48 = (f32[256,512]{1,0:T(8,128)S(1)}, f32[256,512]{1,0:T(8,128)S(1)}, u32[]{:S(2)}, u32[]{:S(2)}) collective-permute-start(f32[256,512]{1,0:T(8,128)S(1)} %pad_maximum_fusion.2), channel_id=1, source_target_pairs={{0,16},{1,17},{2,18},{3,19},{4,12},{5,13},{6,14},{7,15},{8,24},{9,... | collective-permute-start | bytes 1572872 | tf_op jit(solution)/shard_map/ppermute | solution.py:777
  124.3 17.9 %collective-permute-start.52 = (f32[512,512]{1,0:T(8,128)S(1)}, f32[512,512]{1,0:T(8,128)S(1)}, u32[]{:S(2)}, u32[]{:S(2)}) collective-permute-start(f32[512,512]{1,0:T(8,128)S(1)} %pad_maximum_fusion.refs_0_), channel_id=1, source_target_pairs={{0,8},{1,9},{2,10},{3,11},{4,20},{5,21},{6,22},{7,23},{8,0},{9,1},... | collective-permute-start | bytes 3145736 | tf_op jit(solution)/shard_map/ppermute | solution.py:777
  125.4 11.1 %collective-permute-start.50 = (f32[128,512]{1,0:T(8,128)S(1)}, f32[128,512]{1,0:T(8,128)S(1)}, u32[]{:S(2)}, u32[]{:S(2)}) collective-permute-start(f32[128,512]{1,0:T(8,128)S(1)} %add.181), channel_id=1, source_target_pairs={{0,1},{1,0},{2,3},{3,2},{4,5},{5,4},{6,7},{7,6},{8,9},{9,8},{10,11... | collective-permute-start | bytes 786440 | tf_op jit(solution)/shard_map/ppermute | solution.py:777
  130.0 9.4 %collective-permute-start.53 = (f32[32,768]{1,0:T(8,128)S(1)}, f32[32,768]{1,0:T(8,128)S(1)}, u32[]{:S(2)}, u32[]{:S(2)}) collective-permute-start(f32[32,768]{1,0:T(8,128)S(1)} %add.182), channel_id=1, source_target_pairs={{0,1},{1,0},{2,3},{3,2},{4,5},{5,4},{6,7},{7,6},{8,9},{9,8},{10,11... | collective-permute-start | bytes 294920 | tf_op jit(solution)/shard_map/ppermute | solution.py:777
  132.5 22.5 %collective-permute-start.57 = (f32[512,512]{1,0:T(8,128)S(1)}, f32[512,512]{1,0:T(8,128)S(1)}, u32[]{:S(2)}, u32[]{:S(2)}) collective-permute-start(f32[512,512]{1,0:T(8,128)S(1)} %pad_maximum_fusion.refs_0_), channel_id=1, source_target_pairs={{0,4},{1,5},{2,6},{3,7},{4,0},{5,1},{6,2},{7,3},{8,12},{9,13},{10,... | collective-permute-start | bytes 3145736 | tf_op jit(solution)/shard_map/ppermute | solution.py:777
  136.5 9.2 %collective-permute-start.55 = (f32[256,512]{1,0:T(8,128)S(1)}, f32[256,512]{1,0:T(8,128)S(1)}, u32[]{:S(2)}, u32[]{:S(2)}) collective-permute-start(f32[256,512]{1,0:T(8,128)S(1)} %pad_maximum_fusion.3), channel_id=1, source_target_pairs={{0,16},{1,17},{2,18},{3,19},{4,12},{5,13},{6,14},{7,15},{8,24},{9,... | collective-permute-start | bytes 1572872 | tf_op jit(solution)/shard_map/ppermute | solution.py:777
  139.5 8.6 %collective-permute-start.59 = (f32[64,768]{1,0:T(8,128)S(1)}, f32[64,768]{1,0:T(8,128)S(1)}, u32[]{:S(2)}, u32[]{:S(2)}) collective-permute-start(f32[64,768]{1,0:T(8,128)S(1)} %pad_maximum_fusion.7), channel_id=1, source_target_pairs={{0,16},{1,17},{2,18},{3,19},{4,12},{5,13},{6,14},{7,15},{8,24},{9,... | collective-permute-start | bytes 589832 | tf_op jit(solution)/shard_map/ppermute | solution.py:777
  142.1 12.9 %collective-permute-start.58 = (f32[512,512]{1,0:T(8,128)S(1)}, f32[512,512]{1,0:T(8,128)S(1)}, u32[]{:S(2)}, u32[]{:S(2)}) collective-permute-start(f32[512,512]{1,0:T(8,128)S(1)} %collective-permute-done.52.refs_1_), channel_id=1, source_target_pairs={{0,4},{1,5},{2,6},{3,7},{4,0},{5,1},{6,2},{7,3},{8,12},{9,13},{10,... | collective-permute-start | bytes 3145736 | tf_op jit(solution)/shard_map/ppermute | solution.py:777
  145.9 16.0 %collective-permute-start.56 = (f32[512,512]{1,0:T(8,128)S(1)}, f32[512,512]{1,0:T(8,128)S(1)}, u32[]{:S(2)}, u32[]{:S(2)}) collective-permute-start(f32[512,512]{1,0:T(8,128)S(1)} %pad_maximum_fusion.1.refs_0_), channel_id=1, source_target_pairs={{0,8},{1,9},{2,10},{3,11},{4,20},{5,21},{6,22},{7,23},{8,0},{9,1},... | collective-permute-start | bytes 3145736 | tf_op jit(solution)/shard_map/ppermute | solution.py:777
  148.2 21.5 %collective-permute-start.61 = (f32[512,512]{1,0:T(8,128)S(1)}, f32[512,512]{1,0:T(8,128)S(1)}, u32[]{:S(2)}, u32[]{:S(2)}) collective-permute-start(f32[512,512]{1,0:T(8,128)S(1)} %pad_maximum_fusion.1.refs_0_), channel_id=1, source_target_pairs={{0,4},{1,5},{2,6},{3,7},{4,0},{5,1},{6,2},{7,3},{8,12},{9,13},{10,... | collective-permute-start | bytes 3145736 | tf_op jit(solution)/shard_map/ppermute | solution.py:777
  161.9 8.3 %collective-permute-start.62 = (f32[512,512]{1,0:T(8,128)S(1)}, f32[512,512]{1,0:T(8,128)S(1)}, u32[]{:S(2)}, u32[]{:S(2)}) collective-permute-start(f32[512,512]{1,0:T(8,128)S(1)} %collective-permute-done.56.refs_1_), channel_id=1, source_target_pairs={{0,4},{1,5},{2,6},{3,7},{4,0},{5,1},{6,2},{7,3},{8,12},{9,13},{10,... | collective-permute-start | bytes 3145736 | tf_op jit(solution)/shard_map/ppermute | solution.py:777
  163.3 10.8 %collective-permute-start.60 = (f32[32,3200]{1,0:T(8,128)S(1)}, f32[32,3200]{1,0:T(8,128)S(1)}, u32[]{:S(2)}, u32[]{:S(2)}) collective-permute-start(f32[32,3200]{1,0:T(8,128)S(1)} %pad_maximum_fusion.4.refs_0_), channel_id=1, source_target_pairs={{0,8},{1,9},{2,10},{3,11},{4,20},{5,21},{6,22},{7,23},{8,0},{9,1},... | collective-permute-start | bytes 1228808 | tf_op jit(solution)/shard_map/ppermute | solution.py:777
  164.1 10.2 %collective-permute-start.66 = (f32[128,768]{1,0:T(8,128)S(1)}, f32[128,768]{1,0:T(8,128)S(1)}, u32[]{:S(2)}, u32[]{:S(2)}) collective-permute-start(f32[128,768]{1,0:T(8,128)S(1)} %pad_maximum_fusion.5.refs_0_), channel_id=1, source_target_pairs={{0,4},{1,5},{2,6},{3,7},{4,0},{5,1},{6,2},{7,3},{8,12},{9,13},{10,... | collective-permute-start | bytes 1179656 | tf_op jit(solution)/shard_map/ppermute | solution.py:777
  (42 other events, 205.9 us)

commit v4 on v3

--- a/solution.py
+++ b/solution.py
@@ -11,7 +11,7 @@
 epsilon = 1e-05
 chunk_count = 8
 lane_count = 128
-block_rows = 32
+block_rows = 64
 vmem_bytes = 32 * 1024 * 1024
 gelu_scale = math.sqrt(2.0 / math.pi)
 gelu_cubic = 0.044715
@@ -719,7 +719,7 @@
 halvings = 3
 half_blocks = 1 << halvings
 turn_units = (("a", ("out", "glu"), "plane"),)
-middle_units = (("b", ("out", "glu"), "plane"), ("d", ("in",), "plane"))
+middle_units = (("b", ("out", "glu"), "plane"), ("d", ("in",), "inner"))
 last_units = (("c", ("in", "small"), "plane"),)
 after_turn = ("=a",)
 into_middle = ("=a",)

time: 178 us -> 178 us (level)
  transfers between devices with their start and end apart: 68 -> 68, of which waited for: 40 -> 35; matrix products, arithmetic and copies ran while one was open for 1% -> 1% of each run, Pallas kernels for 9% -> 8%
where the time goes in v4:
time: 178 us; the launch traced here: 177 us
  waiting for transfers between devices  89.4 us (50%)
  starting transfers between devices  53.8 us (30%)
  Pallas kernels  29.3 us (16%)
  other arithmetic  2.99 us (2%)
    ppermute x40, waiting for transfers between devices, swap(): return lax.ppermute(array, ('seq', 'batch'), pairs)  73.7 us
    ppermute x40, starting transfers between devices, swap(): return lax.ppermute(array, ('seq', 'batch'), pairs)  33.5 us
    pallas_call x9, Pallas kernels, call(): pl.pallas_call(kernel, name=name, in_specs=specs, out_specs=[pl.BlockSpec...  29.3 us
    ppermute x28, starting transfers between devices, from_other(): lax.ppermute(array, 'seq', [(index, index ^ bits) for index in range(devi...  20.3 us
    ppermute x28, waiting for transfers between devices, from_other(): lax.ppermute(array, 'seq', [(index, index ^ bits) for index in range(devi...  15.8 us
  transfers between devices with their start and end apart: 68, of which 35 were waited for; matrix products, arithmetic and copies ran while one was open for 1% of the time, Pallas kernels for 8%

profile of v4, /device:TPU:0, one launch (start us, length us, event | category | flops | bytes accessed | tf_op | source)
XLA Modules:
  0.0 177.0 jit_solution(3936621713648966578)
XLA Ops:
  1.6 3.1 %first.1 = (f32[3,256,128]{2,1,0:T(8,128)S(1)}, f32[2,16,128]{2,1,0:T(8,128)S(1)}, bf16[256,512]{1,0:T(8,128)(2,1)S(1)}, bf16[256,512]{1,0:T(8,128)(2,1)S(1)}, f...) custom-call(s32[1]{0:T(128)} %bitcast.refs_0_, s32[2,8]{1,0:T(2,128)} %refs_1_.1, ...), custom_call_target="tpu_custom_call" | custom-call | flops 4000000000 | bytes 14400000 | tf_op jit(solution)/shard_map/first/pallas_call | solution.py:1088
  4.7 3.0 %collective-permute-start.1 = (f32[8,384]{1,0:T(8,128)S(1)}, f32[8,384]{1,0:T(8,128)S(1)}, u32[]{:S(2)}, u32[]{:S(2)}) collective-permute-start(f32[8,384]{1,0:T(8,128)S(1)} %get-tuple-element.135.refs_1_), channel_id=1, source_target_pairs={{0,8},{4,12},{8,0},{12,4},{16,24},{20,28},{24,16},{28,20},{1,9},{5... | collective-permute-start | bytes 36872 | tf_op jit(solution)/shard_map/ppermute | solution.py:1150
  11.4 2.4 %collective-permute-done.5.refs_7_ = f32[8,384]{1,0:T(8,128)S(1)} collective-permute-done((f32[8,384]{1,0:T(8,128)S(1)}, f32[8,384]{1,0:T(8,128)S(1)}, u32[]{:S(2)}, u32[]{:S(2)}) %collective-permute-start.5) | collective-permute-done | bytes 12320 | tf_op jit(solution)/shard_map/ppermute | solution.py:1150
  15.0 3.7 %middle.1 = (f32[256,1536]{1,0:T(8,128)S(1)}, bf16[256,1536]{1,0:T(8,128)(2,1)S(1)}, f32[8,1536]{1,0:T(8,128)S(1)}, f32[256,512]{1,0:T(8,128)S(1)}, bf16[256,512...) custom-call(s32[1]{0:T(128)} %bitcast.refs_0_, ...), custom_call_target="tpu_custom_call" | custom-call | flops 4000000000 | bytes 14400000 | tf_op jit(solution)/shard_map/middle/pallas_call | solution.py:1088
  19.3 2.9 %collective-permute-start.12 = (f32[8,384]{1,0:T(8,128)S(1)}, f32[8,384]{1,0:T(8,128)S(1)}, u32[]{:S(2)}, u32[]{:S(2)}) collective-permute-start(f32[8,384]{1,0:T(8,128)S(1)} %get-tuple-element.142.refs_1_), channel_id=1, source_target_pairs={{0,24},{4,28},{8,16},{12,20},{16,8},{20,12},{24,0},{28,4},{1,25},{... | collective-permute-start | bytes 36872 | tf_op jit(solution)/shard_map/ppermute | solution.py:1150
  25.1 6.2 %turn.1 = (f32[1024,512]{1,0:T(8,128)S(1)}, f32[1024,512]{1,0:T(8,128)S(1)}, bf16[2,128,512]{2,1,0:T(8,128)(2,1)}, f32[256,512]{1,0:T(8,128)S(1)}, f32[256,1536]...) custom-call(s32[1]{0:T(128)} %bitcast.refs_0_, ...), custom_call_target="tpu_custom_call" | custom-call | flops 6000000000 | bytes 21600000 | tf_op jit(solution)/shard_map/turn/pallas_call | solution.py:1088
  31.6 1.9 %collective-permute-start.16 = (f32[8,384]{1,0:T(8,128)S(1)}, f32[8,384]{1,0:T(8,128)S(1)}, u32[]{:S(2)}, u32[]{:S(2)}) collective-permute-start(f32[8,384]{1,0:T(8,128)S(1)} %get-tuple-element.153.refs_1_), channel_id=1, source_target_pairs={{0,8},{4,12},{8,0},{12,4},{16,24},{20,28},{24,16},{28,20},{1,9},{5... | collective-permute-start | bytes 36872 | tf_op jit(solution)/shard_map/ppermute | solution.py:1150
  37.2 2.4 %collective-permute-done.20.refs_7_ = f32[8,384]{1,0:T(8,128)S(1)} collective-permute-done((f32[8,384]{1,0:T(8,128)S(1)}, f32[8,384]{1,0:T(8,128)S(1)}, u32[]{:S(2)}, u32[]{:S(2)}) %collective-permute-start.20) | collective-permute-done | bytes 12320 | tf_op jit(solution)/shard_map/ppermute | solution.py:1150
  41.3 5.8 %back_middle.1 = (f32[1024,512]{1,0:T(8,128)S(1)}, f32[1024,512]{1,0:T(8,128)S(1)}, f32[256,768]{1,0:T(8,128)S(1)}, f32[256,768]{1,0:T(8,128)S(1)}, f32[1,512]{1...) custom-call(s32[1]{0:T(128)} %bitcast.refs_0_, ...), custom_call_target="tpu_custom_call" | custom-call | flops 6000000000 | bytes 21600000 | tf_op jit(solution)/shard_map/back_middle/pallas_call | solution.py:1088
  47.7 7.9 %collective-permute-done.24 = f32[512,512]{1,0:T(8,128)S(1)} collective-permute-done((f32[512,512]{1,0:T(8,128)S(1)}, f32[512,512]{1,0:T(8,128)S(1)}, u32[]{:S(2)}, u32[]{:S(2)}) %collective-permute-start.24) | collective-permute-done | bytes 1048608 | tf_op jit(solution)/shard_map/ppermute | solution.py:777
  56.4 1.9 %collective-permute-start.29 = (f32[8,384]{1,0:T(8,128)S(1)}, f32[8,384]{1,0:T(8,128)S(1)}, u32[]{:S(2)}, u32[]{:S(2)}) collective-permute-start(f32[8,384]{1,0:T(8,128)S(1)} %get-tuple-element.182.refs_1_), channel_id=1, source_target_pairs={{0,16},{4,20},{8,24},{12,28},{16,0},{20,4},{24,8},{28,12},{1,17},{... | collective-permute-start | bytes 36872 | tf_op jit(solution)/shard_map/ppermute | solution.py:1150
  60.2 3.6 %collective-permute-start.26 = (f32[8,384]{1,0:T(8,128)S(1)}, f32[8,384]{1,0:T(8,128)S(1)}, u32[]{:S(2)}, u32[]{:S(2)}) collective-permute-start(f32[8,384]{1,0:T(8,128)S(1)} %get-tuple-element.182.refs_1_), channel_id=1, source_target_pairs={{0,4},{4,0},{8,12},{12,8},{16,20},{20,16},{24,28},{28,24},{1,5},{5... | collective-permute-start | bytes 36872 | tf_op jit(solution)/shard_map/ppermute | solution.py:1150
  70.7 3.6 %back_last.1 = (f32[64,3200]{1,0:T(8,128)S(1)}, f32[64,3200]{1,0:T(8,128)S(1)}, bf16[2,128,512]{2,1,0:T(8,128)(2,1)}) custom-call(s32[1]{0:T(128)} %bitcast.refs_0_, f32[8,384]{1,0:T(8,128)S(1)} %get-tuple-element.182.refs_1_, f32[8,384]{1,0:T(8,128)S(1)} %collective-permute-done.26.refs_2_, f32[8,384]{1,0:T(8,128)S(1)} %collective-permute-done.27.refs_3_, ...), custom_call_target="tpu_custom_call" | custom-call | flops 4000000000 | bytes 14400000 | tf_op jit(solution)/shard_map/back_last/pallas_call | solution.py:1088
  75.8 6.1 %collective-permute-done.33 = f32[512,512]{1,0:T(8,128)S(1)} collective-permute-done((f32[512,512]{1,0:T(8,128)S(1)}, f32[512,512]{1,0:T(8,128)S(1)}, u32[]{:S(2)}, u32[]{:S(2)}) %collective-permute-start.33) | collective-permute-done | bytes 1048608 | tf_op jit(solution)/shard_map/ppermute | solution.py:777
  82.7 2.6 %collective-permute-start.40 = (f32[128,512]{1,0:T(8,128)S(1)}, f32[128,512]{1,0:T(8,128)S(1)}, u32[]{:S(2)}, u32[]{:S(2)}) collective-permute-start(f32[128,512]{1,0:T(8,128)S(1)} %fusion.1), channel_id=1, source_target_pairs={{0,2},{1,3},{2,0},{3,1},{4,6},{5,7},{6,4},{7,5},{8,10},{9,11},{10,... | collective-permute-start | bytes 786440 | tf_op jit(solution)/shard_map/ppermute | solution.py:777
  88.6 2.8 %collective-permute-done.36 = f32[256,512]{1,0:T(8,128)S(1)} collective-permute-done((f32[256,512]{1,0:T(8,128)S(1)}, f32[256,512]{1,0:T(8,128)S(1)}, u32[]{:S(2)}, u32[]{:S(2)}) %collective-permute-start.36) | collective-permute-done | bytes 524320 | tf_op jit(solution)/shard_map/ppermute | solution.py:777
  93.2 4.5 %collective-permute-done.40 = f32[128,512]{1,0:T(8,128)S(1)} collective-permute-done((f32[128,512]{1,0:T(8,128)S(1)}, f32[128,512]{1,0:T(8,128)S(1)}, u32[]{:S(2)}, u32[]{:S(2)}) %collective-permute-start.40) | collective-permute-done | bytes 262176 | tf_op jit(solution)/shard_map/ppermute | solution.py:777
  100.5 2.7 %collective-permute-done.39 = f32[128,512]{1,0:T(8,128)S(1)} collective-permute-done((f32[128,512]{1,0:T(8,128)S(1)}, f32[128,512]{1,0:T(8,128)S(1)}, u32[]{:S(2)}, u32[]{:S(2)}) %collective-permute-start.39) | collective-permute-done | bytes 262176 | tf_op jit(solution)/shard_map/ppermute | solution.py:777
  103.4 2.8 %collective-permute-start.46 = (f32[128,512]{1,0:T(8,128)S(1)}, f32[128,512]{1,0:T(8,128)S(1)}, u32[]{:S(2)}, u32[]{:S(2)}) collective-permute-start(f32[128,512]{1,0:T(8,128)S(1)} %fusion), channel_id=1, source_target_pairs={{0,2},{1,3},{2,0},{3,1},{4,6},{5,7},{6,4},{7,5},{8,10},{9,11},{10,... | collective-permute-start | bytes 786440 | tf_op jit(solution)/shard_map/ppermute | solution.py:777
  107.2 4.0 %collective-permute-done.43 = f32[128,512]{1,0:T(8,128)S(1)} collective-permute-done((f32[128,512]{1,0:T(8,128)S(1)}, f32[128,512]{1,0:T(8,128)S(1)}, u32[]{:S(2)}, u32[]{:S(2)}) %collective-permute-start.43) | collective-permute-done | bytes 262176 | tf_op jit(solution)/shard_map/ppermute | solution.py:777
  112.9 9.6 %collective-permute-done.47 = f32[32,768]{1,0:T(8,128)S(1)} collective-permute-done((f32[32,768]{1,0:T(8,128)S(1)}, f32[32,768]{1,0:T(8,128)S(1)}, u32[]{:S(2)}, u32[]{:S(2)}) %collective-permute-start.47) | collective-permute-done | bytes 98336 | tf_op jit(solution)/shard_map/ppermute | solution.py:777
  125.8 2.6 %collective-permute-done.45 = f32[8,3200]{1,0:T(8,128)S(1)} collective-permute-done((f32[8,3200]{1,0:T(8,128)S(1)}, f32[8,3200]{1,0:T(8,128)S(1)}, u32[]{:S(2)}, u32[]{:S(2)}) %collective-permute-start.45) | collective-permute-done | bytes 102432 | tf_op jit(solution)/shard_map/ppermute | solution.py:777
  130.2 4.5 %collective-permute-done.49 = f32[8,3200]{1,0:T(8,128)S(1)} collective-permute-done((f32[8,3200]{1,0:T(8,128)S(1)}, f32[8,3200]{1,0:T(8,128)S(1)}, u32[]{:S(2)}, u32[]{:S(2)}) %collective-permute-start.49) | collective-permute-done | bytes 102432 | tf_op jit(solution)/shard_map/ppermute | solution.py:777
  135.4 2.8 %collective-permute-start.51 = (f32[8,3200]{1,0:T(8,128)S(1)}, f32[8,3200]{1,0:T(8,128)S(1)}, u32[]{:S(2)}, u32[]{:S(2)}) collective-permute-start(f32[8,3200]{1,0:T(8,128)S(1)} %add.183), channel_id=1, source_target_pairs={{0,1},{1,0},{2,3},{3,2},{4,5},{5,4},{6,7},{7,6},{8,9},{9,8},{10,11... | collective-permute-start | bytes 307208 | tf_op jit(solution)/shard_map/ppermute | solution.py:777
  138.4 5.6 %collective-permute-done.52.refs_1_ = f32[512,512]{1,0:T(8,128)S(1)} collective-permute-done((f32[512,512]{1,0:T(8,128)S(1)}, f32[512,512]{1,0:T(8,128)S(1)}, u32[]{:S(2)}, u32[]{:S(2)}) %collective-permute-start.52) | collective-permute-done | bytes 1048608 | tf_op jit(solution)/shard_map/ppermute | solution.py:777
  146.5 7.1 %collective-permute-done.54 = f32[16,3200]{1,0:T(8,128)S(1)} collective-permute-done((f32[16,3200]{1,0:T(8,128)S(1)}, f32[16,3200]{1,0:T(8,128)S(1)}, u32[]{:S(2)}, u32[]{:S(2)}) %collective-permute-start.54) | collective-permute-done | bytes 204832 | tf_op jit(solution)/shard_map/ppermute | solution.py:777
  153.7 2.0 %place_glu_out.2 = (f32[2,512,512]{2,1,0:T(8,128)}, f32[2,1536,512]{2,1,0:T(8,128)}) custom-call(f32[512,512]{1,0:T(8,128)S(1)} %pad_maximum_fusion.refs_0_, f32[512,512]{1,0:T(8,128)S(1)} %collective-permute-done.52.refs_1_, f32[512,512]{1,0:T(8,128)S(1)} %collective-permute-done.57.refs_2_, f32[512,512]{1,0:T(8,128)S(1)} %collective-permute-done.58.refs_3_), custom_call_target="tpu_custom_call" | custom-call | flops 4000000000 | bytes 14400000 | tf_op jit(solution)/shard_map/place_glu_out/pallas_call | solution.py:1088
  155.7 5.4 %collective-permute-done.56.refs_1_ = f32[512,512]{1,0:T(8,128)S(1)} collective-permute-done((f32[512,512]{1,0:T(8,128)S(1)}, f32[512,512]{1,0:T(8,128)S(1)}, u32[]{:S(2)}, u32[]{:S(2)}) %collective-permute-start.56) | collective-permute-done | bytes 1048608 | tf_op jit(solution)/shard_map/ppermute | solution.py:777
  163.4 5.5 %collective-permute-done.63.refs_1_ = f32[128,768]{1,0:T(8,128)S(1)} collective-permute-done((f32[128,768]{1,0:T(8,128)S(1)}, f32[128,768]{1,0:T(8,128)S(1)}, u32[]{:S(2)}, u32[]{:S(2)}) %collective-permute-start.63) | collective-permute-done | bytes 393248 | tf_op jit(solution)/shard_map/ppermute | solution.py:777
  169.4 2.0 %place_glu_out.3 = (f32[2,512,512]{2,1,0:T(8,128)}, f32[2,1536,512]{2,1,0:T(8,128)}) custom-call(f32[512,512]{1,0:T(8,128)S(1)} %pad_maximum_fusion.1.refs_0_, f32[512,512]{1,0:T(8,128)S(1)} %collective-permute-done.56.refs_1_, f32[512,512]{1,0:T(8,128)S(1)} %collective-permute-done.61.refs_2_, ...), custom_call_target="tpu_custom_call", output_to_operand_aliasing={{0}: (4, {}), {1}: (5, {})} | custom-call | flops 4000000000 | bytes 14400000 | tf_op jit(solution)/shard_map/place_glu_out/pallas_call | solution.py:1088
  171.5 1.9 %collective-permute-done.60.refs_1_ = f32[32,3200]{1,0:T(8,128)S(1)} collective-permute-done((f32[32,3200]{1,0:T(8,128)S(1)}, f32[32,3200]{1,0:T(8,128)S(1)}, u32[]{:S(2)}, u32[]{:S(2)}) %collective-permute-start.60) | collective-permute-done | bytes 409632 | tf_op jit(solution)/shard_map/ppermute | solution.py:777
  175.1 1.7 place_last.1
  (160 shorter events, 50.8 us)
Async XLA Ops:
  31.3 8.3 %collective-permute-start.14 = (f32[1024,512]{1,0:T(8,128)S(1)}, f32[1024,512]{1,0:T(8,128)S(1)}, u32[]{:S(2)}, u32[]{:S(2)}) collective-permute-start(f32[1024,512]{1,0:T(8,128)S(1)} %get-tuple-element.151), channel_id=1, source_target_pairs={{0,4},{1,5},{2,6},{3,7},{4,0},{5,1},{6,2},{7,3},{8,12},{9,13},{10,... | collective-permute-start | bytes 6291464 | tf_op jit(solution)/shard_map/ppermute | solution.py:777
  40.8 14.8 %collective-permute-start.24 = (f32[512,512]{1,0:T(8,128)S(1)}, f32[512,512]{1,0:T(8,128)S(1)}, u32[]{:S(2)}, u32[]{:S(2)}) collective-permute-start(f32[512,512]{1,0:T(8,128)S(1)} %slice_add_fusion.1), channel_id=1, source_target_pairs={{0,8},{1,9},{2,10},{3,11},{4,20},{5,21},{6,22},{7,23},{8,0},{9,1},... | collective-permute-start | bytes 3145736 | tf_op jit(solution)/shard_map/ppermute | solution.py:777
  47.1 19.0 %collective-permute-start.22 = (f32[1024,512]{1,0:T(8,128)S(1)}, f32[1024,512]{1,0:T(8,128)S(1)}, u32[]{:S(2)}, u32[]{:S(2)}) collective-permute-start(f32[1024,512]{1,0:T(8,128)S(1)} %get-tuple-element.176), channel_id=1, source_target_pairs={{0,4},{1,5},{2,6},{3,7},{4,0},{5,1},{6,2},{7,3},{8,12},{9,13},{10,... | collective-permute-start | bytes 6291464 | tf_op jit(solution)/shard_map/ppermute | solution.py:777
  47.2 11.2 %collective-permute-start.23 = (f32[256,768]{1,0:T(8,128)S(1)}, f32[256,768]{1,0:T(8,128)S(1)}, u32[]{:S(2)}, u32[]{:S(2)}) collective-permute-start(f32[256,768]{1,0:T(8,128)S(1)} %get-tuple-element.178), channel_id=1, source_target_pairs={{0,4},{1,5},{2,6},{3,7},{4,0},{5,1},{6,2},{7,3},{8,12},{9,13},{10,... | collective-permute-start | bytes 2359304 | tf_op jit(solution)/shard_map/ppermute | solution.py:777
  55.8 10.2 %collective-permute-start.25 = (f32[256,512]{1,0:T(8,128)S(1)}, f32[256,512]{1,0:T(8,128)S(1)}, u32[]{:S(2)}, u32[]{:S(2)}) collective-permute-start(f32[256,512]{1,0:T(8,128)S(1)} %slice_add_fusion.4), channel_id=1, source_target_pairs={{0,16},{1,17},{2,18},{3,19},{4,12},{5,13},{6,14},{7,15},{8,24},{9,... | collective-permute-start | bytes 1572872 | tf_op jit(solution)/shard_map/ppermute | solution.py:777
  56.4 9.0 %collective-permute-start.29 = (f32[8,384]{1,0:T(8,128)S(1)}, f32[8,384]{1,0:T(8,128)S(1)}, u32[]{:S(2)}, u32[]{:S(2)}) collective-permute-start(f32[8,384]{1,0:T(8,128)S(1)} %get-tuple-element.182.refs_1_), channel_id=1, source_target_pairs={{0,16},{4,20},{8,24},{12,28},{16,0},{20,4},{24,8},{28,12},{1,17},{... | collective-permute-start | bytes 36872 | tf_op jit(solution)/shard_map/ppermute | solution.py:1150
  67.1 14.8 %collective-permute-start.33 = (f32[512,512]{1,0:T(8,128)S(1)}, f32[512,512]{1,0:T(8,128)S(1)}, u32[]{:S(2)}, u32[]{:S(2)}) collective-permute-start(f32[512,512]{1,0:T(8,128)S(1)} %slice_add_fusion), channel_id=1, source_target_pairs={{0,8},{1,9},{2,10},{3,11},{4,20},{5,21},{6,22},{7,23},{8,0},{9,1},... | collective-permute-start | bytes 3145736 | tf_op jit(solution)/shard_map/ppermute | solution.py:777
  69.2 17.7 %collective-permute-start.37 = (f32[128,768]{1,0:T(8,128)S(1)}, f32[128,768]{1,0:T(8,128)S(1)}, u32[]{:S(2)}, u32[]{:S(2)}) collective-permute-start(f32[128,768]{1,0:T(8,128)S(1)} %slice_add_fusion.7), channel_id=1, source_target_pairs={{0,8},{1,9},{2,10},{3,11},{4,20},{5,21},{6,22},{7,23},{8,0},{9,1},... | collective-permute-start | bytes 1179656 | tf_op jit(solution)/shard_map/ppermute | solution.py:777
  82.1 9.4 %collective-permute-start.35 = (f32[64,3200]{1,0:T(8,128)S(1)}, f32[64,3200]{1,0:T(8,128)S(1)}, u32[]{:S(2)}, u32[]{:S(2)}) collective-permute-start(f32[64,3200]{1,0:T(8,128)S(1)} %get-tuple-element.207), channel_id=1, source_target_pairs={{0,4},{1,5},{2,6},{3,7},{4,0},{5,1},{6,2},{7,3},{8,12},{9,13},{10,... | collective-permute-start | bytes 2457608 | tf_op jit(solution)/shard_map/ppermute | solution.py:777
  82.1 9.2 %collective-permute-start.36 = (f32[256,512]{1,0:T(8,128)S(1)}, f32[256,512]{1,0:T(8,128)S(1)}, u32[]{:S(2)}, u32[]{:S(2)}) collective-permute-start(f32[256,512]{1,0:T(8,128)S(1)} %slice_add_fusion.2), channel_id=1, source_target_pairs={{0,16},{1,17},{2,18},{3,19},{4,12},{5,13},{6,14},{7,15},{8,24},{9,... | collective-permute-start | bytes 1572872 | tf_op jit(solution)/shard_map/ppermute | solution.py:777
  82.7 15.0 %collective-permute-start.40 = (f32[128,512]{1,0:T(8,128)S(1)}, f32[128,512]{1,0:T(8,128)S(1)}, u32[]{:S(2)}, u32[]{:S(2)}) collective-permute-start(f32[128,512]{1,0:T(8,128)S(1)} %fusion.1), channel_id=1, source_target_pairs={{0,2},{1,3},{2,0},{3,1},{4,6},{5,7},{6,4},{7,5},{8,10},{9,11},{10,... | collective-permute-start | bytes 786440 | tf_op jit(solution)/shard_map/ppermute | solution.py:777
  87.0 11.4 %collective-permute-start.41 = (f32[64,768]{1,0:T(8,128)S(1)}, f32[64,768]{1,0:T(8,128)S(1)}, u32[]{:S(2)}, u32[]{:S(2)}) collective-permute-start(f32[64,768]{1,0:T(8,128)S(1)} %slice_add_fusion.22), channel_id=1, source_target_pairs={{0,1},{1,0},{2,3},{3,2},{4,5},{5,4},{6,7},{7,6},{8,9},{9,8},{10,11... | collective-permute-start | bytes 589832 | tf_op jit(solution)/shard_map/ppermute | solution.py:777
  91.6 11.7 %collective-permute-start.39 = (f32[128,512]{1,0:T(8,128)S(1)}, f32[128,512]{1,0:T(8,128)S(1)}, u32[]{:S(2)}, u32[]{:S(2)}) collective-permute-start(f32[128,512]{1,0:T(8,128)S(1)} %slice_add_fusion.11), channel_id=1, source_target_pairs={{0,1},{1,0},{2,3},{3,2},{4,5},{5,4},{6,7},{7,6},{8,9},{9,8},{10,11... | collective-permute-start | bytes 786440 | tf_op jit(solution)/shard_map/ppermute | solution.py:777
  97.8 8.5 %collective-permute-start.38 = (f32[32,3200]{1,0:T(8,128)S(1)}, f32[32,3200]{1,0:T(8,128)S(1)}, u32[]{:S(2)}, u32[]{:S(2)}) collective-permute-start(f32[32,3200]{1,0:T(8,128)S(1)} %slice_add_fusion.6), channel_id=1, source_target_pairs={{0,8},{1,9},{2,10},{3,11},{4,20},{5,21},{6,22},{7,23},{8,0},{9,1},... | collective-permute-start | bytes 1228808 | tf_op jit(solution)/shard_map/ppermute | solution.py:777
  98.4 8.7 %collective-permute-start.44 = (f32[32,768]{1,0:T(8,128)S(1)}, f32[32,768]{1,0:T(8,128)S(1)}, u32[]{:S(2)}, u32[]{:S(2)}) collective-permute-start(f32[32,768]{1,0:T(8,128)S(1)} %slice_add_fusion.33), channel_id=1, source_target_pairs={{0,16},{1,17},{2,18},{3,19},{4,12},{5,13},{6,14},{7,15},{8,24},{9,... | collective-permute-start | bytes 294920 | tf_op jit(solution)/shard_map/ppermute | solution.py:777
  99.9 11.3 %collective-permute-start.43 = (f32[128,512]{1,0:T(8,128)S(1)}, f32[128,512]{1,0:T(8,128)S(1)}, u32[]{:S(2)}, u32[]{:S(2)}) collective-permute-start(f32[128,512]{1,0:T(8,128)S(1)} %add.168), channel_id=1, source_target_pairs={{0,1},{1,0},{2,3},{3,2},{4,5},{5,4},{6,7},{7,6},{8,9},{9,8},{10,11... | collective-permute-start | bytes 786440 | tf_op jit(solution)/shard_map/ppermute | solution.py:777
  103.4 19.1 %collective-permute-start.46 = (f32[128,512]{1,0:T(8,128)S(1)}, f32[128,512]{1,0:T(8,128)S(1)}, u32[]{:S(2)}, u32[]{:S(2)}) collective-permute-start(f32[128,512]{1,0:T(8,128)S(1)} %fusion), channel_id=1, source_target_pairs={{0,2},{1,3},{2,0},{3,1},{4,6},{5,7},{6,4},{7,5},{8,10},{9,11},{10,... | collective-permute-start | bytes 786440 | tf_op jit(solution)/shard_map/ppermute | solution.py:777
  106.3 16.3 %collective-permute-start.42 = (f32[16,3200]{1,0:T(8,128)S(1)}, f32[16,3200]{1,0:T(8,128)S(1)}, u32[]{:S(2)}, u32[]{:S(2)}) collective-permute-start(f32[16,3200]{1,0:T(8,128)S(1)} %slice_add_fusion.20), channel_id=1, source_target_pairs={{0,16},{1,17},{2,18},{3,19},{4,12},{5,13},{6,14},{7,15},{8,24},{9,... | collective-permute-start | bytes 614408 | tf_op jit(solution)/shard_map/ppermute | solution.py:777
  107.1 15.3 %collective-permute-start.47 = (f32[32,768]{1,0:T(8,128)S(1)}, f32[32,768]{1,0:T(8,128)S(1)}, u32[]{:S(2)}, u32[]{:S(2)}) collective-permute-start(f32[32,768]{1,0:T(8,128)S(1)} %fusion.3), channel_id=1, source_target_pairs={{0,2},{1,3},{2,0},{3,1},{4,6},{5,7},{6,4},{7,5},{8,10},{9,11},{10,... | collective-permute-start | bytes 294920 | tf_op jit(solution)/shard_map/ppermute | solution.py:777
  111.2 12.0 %collective-permute-start.48 = (f32[256,512]{1,0:T(8,128)S(1)}, f32[256,512]{1,0:T(8,128)S(1)}, u32[]{:S(2)}, u32[]{:S(2)}) collective-permute-start(f32[256,512]{1,0:T(8,128)S(1)} %pad_maximum_fusion.2), channel_id=1, source_target_pairs={{0,16},{1,17},{2,18},{3,19},{4,12},{5,13},{6,14},{7,15},{8,24},{9,... | collective-permute-start | bytes 1572872 | tf_op jit(solution)/shard_map/ppermute | solution.py:777
  123.3 20.7 %collective-permute-start.52 = (f32[512,512]{1,0:T(8,128)S(1)}, f32[512,512]{1,0:T(8,128)S(1)}, u32[]{:S(2)}, u32[]{:S(2)}) collective-permute-start(f32[512,512]{1,0:T(8,128)S(1)} %pad_maximum_fusion.refs_0_), channel_id=1, source_target_pairs={{0,8},{1,9},{2,10},{3,11},{4,20},{5,21},{6,22},{7,23},{8,0},{9,1},... | collective-permute-start | bytes 3145736 | tf_op jit(solution)/shard_map/ppermute | solution.py:777
  124.8 9.9 %collective-permute-start.50 = (f32[128,512]{1,0:T(8,128)S(1)}, f32[128,512]{1,0:T(8,128)S(1)}, u32[]{:S(2)}, u32[]{:S(2)}) collective-permute-start(f32[128,512]{1,0:T(8,128)S(1)} %add.181), channel_id=1, source_target_pairs={{0,1},{1,0},{2,3},{3,2},{4,5},{5,4},{6,7},{7,6},{8,9},{9,8},{10,11... | collective-permute-start | bytes 786440 | tf_op jit(solution)/shard_map/ppermute | solution.py:777
  130.2 8.1 %collective-permute-start.53 = (f32[32,768]{1,0:T(8,128)S(1)}, f32[32,768]{1,0:T(8,128)S(1)}, u32[]{:S(2)}, u32[]{:S(2)}) collective-permute-start(f32[32,768]{1,0:T(8,128)S(1)} %add.182), channel_id=1, source_target_pairs={{0,16},{1,17},{2,18},{3,19},{4,12},{5,13},{6,14},{7,15},{8,24},{9,... | collective-permute-start | bytes 294920 | tf_op jit(solution)/shard_map/ppermute | solution.py:777
  130.2 23.5 %collective-permute-start.57 = (f32[512,512]{1,0:T(8,128)S(1)}, f32[512,512]{1,0:T(8,128)S(1)}, u32[]{:S(2)}, u32[]{:S(2)}) collective-permute-start(f32[512,512]{1,0:T(8,128)S(1)} %pad_maximum_fusion.refs_0_), channel_id=1, source_target_pairs={{0,4},{1,5},{2,6},{3,7},{4,0},{5,1},{6,2},{7,3},{8,12},{9,13},{10,... | collective-permute-start | bytes 3145736 | tf_op jit(solution)/shard_map/ppermute | solution.py:777
  134.7 9.3 %collective-permute-start.55 = (f32[256,512]{1,0:T(8,128)S(1)}, f32[256,512]{1,0:T(8,128)S(1)}, u32[]{:S(2)}, u32[]{:S(2)}) collective-permute-start(f32[256,512]{1,0:T(8,128)S(1)} %pad_maximum_fusion.3), channel_id=1, source_target_pairs={{0,16},{1,17},{2,18},{3,19},{4,12},{5,13},{6,14},{7,15},{8,24},{9,... | collective-permute-start | bytes 1572872 | tf_op jit(solution)/shard_map/ppermute | solution.py:777
  135.4 8.6 %collective-permute-start.51 = (f32[8,3200]{1,0:T(8,128)S(1)}, f32[8,3200]{1,0:T(8,128)S(1)}, u32[]{:S(2)}, u32[]{:S(2)}) collective-permute-start(f32[8,3200]{1,0:T(8,128)S(1)} %add.183), channel_id=1, source_target_pairs={{0,1},{1,0},{2,3},{3,2},{4,5},{5,4},{6,7},{7,6},{8,9},{9,8},{10,11... | collective-permute-start | bytes 307208 | tf_op jit(solution)/shard_map/ppermute | solution.py:777
  144.0 9.7 %collective-permute-start.58 = (f32[512,512]{1,0:T(8,128)S(1)}, f32[512,512]{1,0:T(8,128)S(1)}, u32[]{:S(2)}, u32[]{:S(2)}) collective-permute-start(f32[512,512]{1,0:T(8,128)S(1)} %collective-permute-done.52.refs_1_), channel_id=1, source_target_pairs={{0,4},{1,5},{2,6},{3,7},{4,0},{5,1},{6,2},{7,3},{8,12},{9,13},{10,... | collective-permute-start | bytes 3145736 | tf_op jit(solution)/shard_map/ppermute | solution.py:777
  144.1 17.0 %collective-permute-start.56 = (f32[512,512]{1,0:T(8,128)S(1)}, f32[512,512]{1,0:T(8,128)S(1)}, u32[]{:S(2)}, u32[]{:S(2)}) collective-permute-start(f32[512,512]{1,0:T(8,128)S(1)} %pad_maximum_fusion.1.refs_0_), channel_id=1, source_target_pairs={{0,8},{1,9},{2,10},{3,11},{4,20},{5,21},{6,22},{7,23},{8,0},{9,1},... | collective-permute-start | bytes 3145736 | tf_op jit(solution)/shard_map/ppermute | solution.py:777
  146.3 22.6 %collective-permute-start.61 = (f32[512,512]{1,0:T(8,128)S(1)}, f32[512,512]{1,0:T(8,128)S(1)}, u32[]{:S(2)}, u32[]{:S(2)}) collective-permute-start(f32[512,512]{1,0:T(8,128)S(1)} %pad_maximum_fusion.1.refs_0_), channel_id=1, source_target_pairs={{0,4},{1,5},{2,6},{3,7},{4,0},{5,1},{6,2},{7,3},{8,12},{9,13},{10,... | collective-permute-start | bytes 3145736 | tf_op jit(solution)/shard_map/ppermute | solution.py:777
  161.1 8.3 %collective-permute-start.62 = (f32[512,512]{1,0:T(8,128)S(1)}, f32[512,512]{1,0:T(8,128)S(1)}, u32[]{:S(2)}, u32[]{:S(2)}) collective-permute-start(f32[512,512]{1,0:T(8,128)S(1)} %collective-permute-done.56.refs_1_), channel_id=1, source_target_pairs={{0,4},{1,5},{2,6},{3,7},{4,0},{5,1},{6,2},{7,3},{8,12},{9,13},{10,... | collective-permute-start | bytes 3145736 | tf_op jit(solution)/shard_map/ppermute | solution.py:777
  162.6 10.7 %collective-permute-start.60 = (f32[32,3200]{1,0:T(8,128)S(1)}, f32[32,3200]{1,0:T(8,128)S(1)}, u32[]{:S(2)}, u32[]{:S(2)}) collective-permute-start(f32[32,3200]{1,0:T(8,128)S(1)} %pad_maximum_fusion.4.refs_0_), channel_id=1, source_target_pairs={{0,8},{1,9},{2,10},{3,11},{4,20},{5,21},{6,22},{7,23},{8,0},{9,1},... | collective-permute-start | bytes 1228808 | tf_op jit(solution)/shard_map/ppermute | solution.py:777
  163.3 10.2 %collective-permute-start.66 = (f32[128,768]{1,0:T(8,128)S(1)}, f32[128,768]{1,0:T(8,128)S(1)}, u32[]{:S(2)}, u32[]{:S(2)}) collective-permute-start(f32[128,768]{1,0:T(8,128)S(1)} %pad_maximum_fusion.5.refs_0_), channel_id=1, source_target_pairs={{0,4},{1,5},{2,6},{3,7},{4,0},{5,1},{6,2},{7,3},{8,12},{9,13},{10,... | collective-permute-start | bytes 1179656 | tf_op jit(solution)/shard_map/ppermute | solution.py:777
  (42 other events, 210.6 us)
